TPU v7x, 32 devices: a whole 2x2x4 slice. The times are simulated.
32 devices in a mesh: dp: 4 (over z), ctx: 4 (over x, core), fsdp: 2 (over y).
Axes of the slice: x: 2, y: 2, z: 4, core: 2. Of those that a mesh axis runs over, the one named last changes fastest.
Arguments:
- hidden: bfloat16 [8, 1024, 2048], P(('dp', 'fsdp'), 'ctx'), may hold values from -6 to 6
- segment_ids: int32 [8, 1024], P(('dp', 'fsdp')), may hold values from 0 to 4, as said below
- positions: int32 [8, 1024], P(('dp', 'fsdp')), may hold values from 0 to 799, as said below
- attn_gain: bfloat16 [2048], P(('dp', 'ctx', 'fsdp')), may hold values from 0.099609375 to 1.8984375
- w_query: bfloat16 [2048, 2048], P(('dp', 'fsdp'), 'ctx'), may hold values from -0.015625 to 0.015625
- w_key: bfloat16 [2048, 2048], P(('dp', 'fsdp'), 'ctx'), may hold values from -0.125 to 0.125
- w_value: bfloat16 [2048, 2048], P(('dp', 'fsdp'), 'ctx'), may hold values from -0.125 to 0.125
- w_attn_out: bfloat16 [2048, 2048], P('ctx', ('dp', 'fsdp')), may hold values from -1.5 to 1.5
- rel_table: bfloat16 [1024], P(('dp', 'ctx', 'fsdp')), may hold values from -4 to 4
- ffn_gain: bfloat16 [2048], P(('dp', 'ctx', 'fsdp')), may hold values from 0.099609375 to 1.8984375
- w_gate: bfloat16 [2048, 5120], P(('dp', 'fsdp'), 'ctx'), may hold values from -0.125 to 0.125
- w_up: bfloat16 [2048, 5120], P(('dp', 'fsdp'), 'ctx'), may hold values from -0.125 to 0.125
- w_down: bfloat16 [5120, 2048], P('ctx', ('dp', 'fsdp')), may hold values from -0.078125 to 0.078125
- cotangent: bfloat16 [8, 1024, 2048], P(('dp', 'fsdp'), 'ctx'), may hold values from -6 to 6
Outputs:
- output: bfloat16 [8, 1024, 2048], P(('dp', 'fsdp'), 'ctx')
- grad_hidden: float32 [8, 1024, 2048], P(('dp', 'fsdp'), 'ctx')
- grad_attn_gain: float32 [2048], P(('dp', 'ctx', 'fsdp'))
- grad_query: float32 [2048, 2048], P(('dp', 'fsdp'), 'ctx')
- grad_key: float32 [2048, 2048], P(('dp', 'fsdp'), 'ctx')
- grad_value: float32 [2048, 2048], P(('dp', 'fsdp'), 'ctx')
- grad_attn_out: float32 [2048, 2048], P('ctx', ('dp', 'fsdp'))
- bias_table_gradient: float32 [1024], P(('dp', 'ctx', 'fsdp'))
- grad_ffn_gain: float32 [2048], P(('dp', 'ctx', 'fsdp'))
- grad_gate: float32 [2048, 5120], P(('dp', 'fsdp'), 'ctx')
- grad_up: float32 [2048, 5120], P(('dp', 'fsdp'), 'ctx')
- grad_down: float32 [5120, 2048], P('ctx', ('dp', 'fsdp'))
Inputs may be any that keep to these rules, and one draw needn't show every extreme that they name: `segment_ids`: within each sequence the ids number its documents from 0 and never fall. One document of each sequence, its first or its second, holds exactly 800 tokens; every other document holds 60 to 800 tokens, except the last one, which the end of the sequence may cut short. `positions`: 0 at a document's first token and rising by one along it, consistent with segment_ids.
All inputs are finite; a program needn't handle non-finite values.
Results may differ from a plain program's by a relative error of at most 0.018.
Values may be sent and summed in bfloat16 or wider, within the bound.
A program may use at most 256 MiB of HBM per device.

v0:
```python
import jax
import jax.numpy as jnp
from jax import lax
from jax.sharding import PartitionSpec as P

H = 32
DH = 64
NB = 32
QB = 512


EPSILON = 1e-06
THRESHOLDS = (12, 16, 23, 32, 46, 64, 91)
MASKED = -1e30


def rms_norm(values, gain):
    return values * lax.rsqrt(jnp.mean(values * values, axis=-1, keepdims=True) + EPSILON) * gain


def gelu_tanh(values):
    return (
        0.5
        * values
        * (1.0 + jnp.tanh(0.7978845608028654 * (values + 0.044715 * values * values * values)))
    )


def bucket_table(query_pos, key_pos):
    relative = key_pos[None, :] - query_pos[:, None]
    distance = jnp.abs(relative)
    log_bucket = 8 + sum(((distance >= threshold).astype(jnp.int32) for threshold in THRESHOLDS))
    bucket = jnp.where(distance < 8, distance, log_bucket)
    return bucket + 16 * (relative > 0).astype(jnp.int32)


def gather_attention(w_query, w_key, w_value, w_attn_out):
    return (
        lax.all_gather(w_query, ("dp", "fsdp"), axis=0, tiled=True),
        lax.all_gather(w_key, ("dp", "fsdp"), axis=0, tiled=True),
        lax.all_gather(w_value, ("dp", "fsdp"), axis=0, tiled=True),
        lax.all_gather(w_attn_out, ("dp", "fsdp"), axis=1, tiled=True),
    )


def gather_feedforward(w_gate, w_up, w_down):
    return (
        lax.all_gather(w_gate, ("dp", "fsdp"), axis=0, tiled=True),
        lax.all_gather(w_up, ("dp", "fsdp"), axis=0, tiled=True),
        lax.all_gather(w_down, ("dp", "fsdp"), axis=1, tiled=True),
    )


def block_masks(segment_row, position_row, start):
    query_pos = lax.dynamic_slice_in_dim(position_row, start, QB)
    query_seg = lax.dynamic_slice_in_dim(segment_row, start, QB)
    buckets = bucket_table(query_pos, position_row)
    one_hot = (buckets[None] == jnp.arange(NB, dtype=jnp.int32)[:, None, None]).astype(jnp.bfloat16)
    same_doc = query_seg[:, None] == segment_row[None, :]
    return (one_hot, same_doc)


def block_scores(query_block, key_rows, table_local, one_hot, same_doc):
    attention_scores = jnp.einsum(
        "ihd,jhd->hij", query_block, key_rows, preferred_element_type=jnp.float32
    )
    attention_scores = attention_scores + jnp.einsum(
        "bij,bh->hij", one_hot, table_local, preferred_element_type=jnp.float32
    )
    return jnp.where(same_doc[None], attention_scores, MASKED)


def layer_forward(tokens, small_set, attn_set, ffn_set, segment_row, position_row):
    attn_gain, ffn_gain, table_flat = small_set
    w_query, w_key, w_value, w_attn_out = attn_set
    w_gate, w_up, w_down = ffn_set
    heads_here = w_query.shape[1] // DH
    head_start = lax.axis_index("ctx") * heads_here
    table_local = lax.dynamic_slice_in_dim(table_flat.reshape(NB, H), head_start, heads_here, 1)
    normalized_rows, attn_back = jax.vjp(rms_norm, tokens, attn_gain.astype(jnp.float32))
    normed_rows = lax.all_gather(normalized_rows.astype(jnp.bfloat16), "ctx", axis=0, tiled=True)
    seq_len = normed_rows.shape[0]
    queries = (
        jnp.dot(normed_rows, w_query, preferred_element_type=jnp.float32)
        .astype(jnp.bfloat16)
        .reshape(seq_len, heads_here, DH)
    )
    key_rows = (
        jnp.dot(normed_rows, w_key, preferred_element_type=jnp.float32)
        .astype(jnp.bfloat16)
        .reshape(seq_len, heads_here, DH)
    )
    value_rows = (
        jnp.dot(normed_rows, w_value, preferred_element_type=jnp.float32)
        .astype(jnp.bfloat16)
        .reshape(seq_len, heads_here, DH)
    )
    starts = jnp.arange(seq_len // QB, dtype=jnp.int32) * QB

    def forward_block(start):
        one_hot, same_doc = block_masks(segment_row, position_row, start)
        query_block = lax.dynamic_slice_in_dim(queries, start, QB, 0)
        attention_scores = block_scores(query_block, key_rows, table_local, one_hot, same_doc)
        row_peak = jnp.max(attention_scores, axis=-1, keepdims=True)
        lifted = jnp.exp(attention_scores - row_peak)
        row_total = jnp.sum(lifted, axis=-1, keepdims=True)
        prob_low = (lifted / row_total).astype(jnp.bfloat16)
        attended_part = jnp.einsum(
            "hij,jhd->ihd", prob_low, value_rows, preferred_element_type=jnp.float32
        )
        return (attended_part, row_peak + jnp.log(row_total))

    attended, log_total = lax.map(forward_block, starts)
    attended_low = attended.reshape(seq_len, heads_here * DH).astype(jnp.bfloat16)
    attn_term = jnp.dot(attended_low, w_attn_out, preferred_element_type=jnp.float32)
    residual = tokens + lax.psum_scatter(attn_term, "ctx", scatter_dimension=0, tiled=True)
    normed_ffn, ffn_back = jax.vjp(rms_norm, residual, ffn_gain.astype(jnp.float32))
    ffn_rows = lax.all_gather(normed_ffn.astype(jnp.bfloat16), "ctx", axis=0, tiled=True)
    gate_value = jnp.dot(ffn_rows, w_gate, preferred_element_type=jnp.float32)
    up_value = jnp.dot(ffn_rows, w_up, preferred_element_type=jnp.float32)
    gelu_gate, gelu_back = jax.vjp(gelu_tanh, gate_value)
    ffn_hidden = (gelu_gate * up_value).astype(jnp.bfloat16)
    down_term = jnp.dot(ffn_hidden, w_down, preferred_element_type=jnp.float32)
    result = residual + lax.psum_scatter(
        down_term.astype(jnp.bfloat16), "ctx", scatter_dimension=0, tiled=True
    ).astype(jnp.float32)
    stored = (
        attn_back,
        normed_rows,
        queries,
        key_rows,
        value_rows,
        table_local,
        head_start,
        starts,
        log_total,
        attended_low,
        ffn_back,
        ffn_rows,
        up_value,
        gelu_gate,
        gelu_back,
        ffn_hidden,
    )
    return (result, stored)


def on_device(
    hidden,
    segment_ids,
    positions,
    attn_gain,
    w_query,
    w_key,
    w_value,
    w_attn_out,
    rel_table,
    ffn_gain,
    w_gate,
    w_up,
    w_down,
    cotangent,
):
    tokens = hidden[0].astype(jnp.float32)
    segment_row = segment_ids[0]
    position_row = positions[0]
    small_set = (
        lax.all_gather(attn_gain, ("dp", "ctx", "fsdp"), axis=0, tiled=True),
        lax.all_gather(ffn_gain, ("dp", "ctx", "fsdp"), axis=0, tiled=True),
        lax.all_gather(rel_table, ("dp", "ctx", "fsdp"), axis=0, tiled=True),
    )
    attn_set = gather_attention(w_query, w_key, w_value, w_attn_out)
    ffn_set = gather_feedforward(w_gate, w_up, w_down)
    result, unused_stored = layer_forward(
        tokens, small_set, attn_set, ffn_set, segment_row, position_row
    )
    back_attn = gather_attention(w_query, w_key, w_value, w_attn_out)
    back_ffn = gather_feedforward(w_gate, w_up, w_down)
    recomputed, stored = layer_forward(
        tokens, small_set, back_attn, back_ffn, segment_row, position_row
    )
    (
        attn_back,
        normed_rows,
        queries,
        key_rows,
        value_rows,
        table_local,
        head_start,
        starts,
        log_total,
        attended_low,
        ffn_back,
        ffn_rows,
        up_value,
        gelu_gate,
        gelu_back,
        ffn_hidden,
    ) = stored
    full_query, full_key, full_value, full_attn_out = back_attn
    full_gate, full_up, full_down = back_ffn
    seq_len = normed_rows.shape[0]
    heads_here = queries.shape[1]
    grad_rows = lax.all_gather(cotangent[0], "ctx", axis=0, tiled=True)
    grad_w_down = jnp.einsum("tf,td->fd", ffn_hidden, grad_rows, preferred_element_type=jnp.float32)
    grad_hidden_ffn = jnp.einsum(
        "td,fd->tf", grad_rows, full_down, preferred_element_type=jnp.float32
    )
    up_value_gradient = (grad_hidden_ffn * gelu_gate).astype(jnp.bfloat16)
    grad_gate_value = gelu_back(grad_hidden_ffn * up_value)[0].astype(jnp.bfloat16)
    grad_w_gate = jnp.einsum(
        "td,tf->df", ffn_rows, grad_gate_value, preferred_element_type=jnp.float32
    )
    grad_w_up = jnp.einsum(
        "td,tf->df", ffn_rows, up_value_gradient, preferred_element_type=jnp.float32
    )
    ffn_normed_term = jnp.einsum(
        "tf,df->td", grad_gate_value, full_gate, preferred_element_type=jnp.float32
    )
    ffn_normed_term = ffn_normed_term + jnp.einsum(
        "tf,df->td", up_value_gradient, full_up, preferred_element_type=jnp.float32
    )
    grad_normed_ffn = lax.psum_scatter(ffn_normed_term, "ctx", scatter_dimension=0, tiled=True)
    grad_residual_norm, grad_ffn_gain = ffn_back(grad_normed_ffn)
    grad_residual = cotangent[0].astype(jnp.float32) + grad_residual_norm
    ffn_sums = (
        lax.psum_scatter(
            grad_w_gate.astype(jnp.bfloat16), ("dp", "fsdp"), scatter_dimension=0, tiled=True
        ).astype(jnp.float32),
        lax.psum_scatter(
            grad_w_up.astype(jnp.bfloat16), ("dp", "fsdp"), scatter_dimension=0, tiled=True
        ).astype(jnp.float32),
        lax.psum_scatter(
            grad_w_down.astype(jnp.bfloat16), ("dp", "fsdp"), scatter_dimension=1, tiled=True
        ).astype(jnp.float32),
    )
    branch_rows = lax.all_gather(grad_residual.astype(jnp.bfloat16), "ctx", axis=0, tiled=True)
    grad_w_attn_out = jnp.einsum(
        "ti,td->id", attended_low, branch_rows, preferred_element_type=jnp.float32
    )
    grad_attended = jnp.einsum(
        "td,id->ti", branch_rows, full_attn_out, preferred_element_type=jnp.float32
    )
    grad_attended = grad_attended.astype(jnp.bfloat16).reshape(seq_len, heads_here, DH)

    def backward_block(operands):
        start, block_total = operands
        one_hot, same_doc = block_masks(segment_row, position_row, start)
        query_block = lax.dynamic_slice_in_dim(queries, start, QB, 0)
        grad_part = lax.dynamic_slice_in_dim(grad_attended, start, QB, 0)
        attention_scores = block_scores(query_block, key_rows, table_local, one_hot, same_doc)
        weights = jnp.exp(attention_scores - block_total)
        prob_low = weights.astype(jnp.bfloat16)
        grad_probs = jnp.einsum(
            "ihd,jhd->hij", grad_part, value_rows, preferred_element_type=jnp.float32
        )
        centred = grad_probs - jnp.sum(weights * grad_probs, axis=-1, keepdims=True)
        grad_scores = (weights * centred).astype(jnp.bfloat16)
        grad_query_part = jnp.einsum(
            "hij,jhd->ihd", grad_scores, key_rows, preferred_element_type=jnp.float32
        )
        grad_key_part = jnp.einsum(
            "hij,ihd->jhd", grad_scores, query_block, preferred_element_type=jnp.float32
        )
        grad_value_part = jnp.einsum(
            "hij,ihd->jhd", prob_low, grad_part, preferred_element_type=jnp.float32
        )
        grad_bias_part = jnp.einsum(
            "hij,bij->bh", grad_scores, one_hot, preferred_element_type=jnp.float32
        )
        return (grad_query_part, grad_key_part, grad_value_part, grad_bias_part)

    query_blocks, key_blocks, value_blocks, bias_blocks = lax.map(
        backward_block, (starts, log_total)
    )
    grad_queries_low = query_blocks.reshape(seq_len, heads_here * DH).astype(jnp.bfloat16)
    grad_keys_low = (
        jnp.sum(key_blocks, axis=0).reshape(seq_len, heads_here * DH).astype(jnp.bfloat16)
    )
    grad_values_low = (
        jnp.sum(value_blocks, axis=0).reshape(seq_len, heads_here * DH).astype(jnp.bfloat16)
    )
    grad_w_query = jnp.einsum(
        "td,te->de", normed_rows, grad_queries_low, preferred_element_type=jnp.float32
    )
    grad_w_key = jnp.einsum(
        "td,te->de", normed_rows, grad_keys_low, preferred_element_type=jnp.float32
    )
    grad_w_value = jnp.einsum(
        "td,te->de", normed_rows, grad_values_low, preferred_element_type=jnp.float32
    )
    normed_term = jnp.einsum(
        "te,de->td", grad_queries_low, full_query, preferred_element_type=jnp.float32
    )
    normed_term = normed_term + jnp.einsum(
        "te,de->td", grad_keys_low, full_key, preferred_element_type=jnp.float32
    )
    normed_term = normed_term + jnp.einsum(
        "te,de->td", grad_values_low, full_value, preferred_element_type=jnp.float32
    )
    grad_normed = lax.psum_scatter(
        normed_term.astype(jnp.bfloat16), "ctx", scatter_dimension=0, tiled=True
    ).astype(jnp.float32)
    token_norm_gradient, grad_attn_gain = attn_back(grad_normed)
    grad_tokens = grad_residual + token_norm_gradient
    attn_sums = (
        lax.psum_scatter(
            grad_w_query.astype(jnp.bfloat16), ("dp", "fsdp"), scatter_dimension=0, tiled=True
        ).astype(jnp.float32),
        lax.psum_scatter(
            grad_w_key.astype(jnp.bfloat16), ("dp", "fsdp"), scatter_dimension=0, tiled=True
        ).astype(jnp.float32),
        lax.psum_scatter(
            grad_w_value.astype(jnp.bfloat16), ("dp", "fsdp"), scatter_dimension=0, tiled=True
        ).astype(jnp.float32),
        lax.psum_scatter(
            grad_w_attn_out.astype(jnp.bfloat16), ("dp", "fsdp"), scatter_dimension=1, tiled=True
        ).astype(jnp.float32),
    )
    bias_sum = jnp.sum(bias_blocks, axis=0)
    table_term = lax.dynamic_update_slice(
        jnp.zeros((NB, H), jnp.float32), bias_sum, (jnp.int32(0), head_start)
    )
    small_sums = (
        lax.psum_scatter(grad_attn_gain, ("dp", "ctx", "fsdp"), scatter_dimension=0, tiled=True),
        lax.psum_scatter(grad_ffn_gain, ("dp", "ctx", "fsdp"), scatter_dimension=0, tiled=True),
        lax.psum_scatter(
            table_term.reshape(NB * H), ("dp", "ctx", "fsdp"), scatter_dimension=0, tiled=True
        ),
    )
    return (
        result[None].astype(jnp.bfloat16),
        grad_tokens[None],
        small_sums[0],
        attn_sums[0],
        attn_sums[1],
        attn_sums[2],
        attn_sums[3],
        small_sums[2],
        small_sums[1],
        ffn_sums[0],
        ffn_sums[1],
        ffn_sums[2],
    )


def solution(mesh):
    in_specs = (
        P(("dp", "fsdp"), "ctx", None),
        P(("dp", "fsdp"), None),
        P(("dp", "fsdp"), None),
        P(("dp", "ctx", "fsdp")),
        P(("dp", "fsdp"), "ctx"),
        P(("dp", "fsdp"), "ctx"),
        P(("dp", "fsdp"), "ctx"),
        P("ctx", ("dp", "fsdp")),
        P(("dp", "ctx", "fsdp")),
        P(("dp", "ctx", "fsdp")),
        P(("dp", "fsdp"), "ctx"),
        P(("dp", "fsdp"), "ctx"),
        P("ctx", ("dp", "fsdp")),
        P(("dp", "fsdp"), "ctx", None),
    )
    out_specs = (
        P(("dp", "fsdp"), "ctx", None),
        P(("dp", "fsdp"), "ctx", None),
        P(("dp", "ctx", "fsdp")),
        P(("dp", "fsdp"), "ctx"),
        P(("dp", "fsdp"), "ctx"),
        P(("dp", "fsdp"), "ctx"),
        P("ctx", ("dp", "fsdp")),
        P(("dp", "ctx", "fsdp")),
        P(("dp", "ctx", "fsdp")),
        P(("dp", "fsdp"), "ctx"),
        P(("dp", "fsdp"), "ctx"),
        P("ctx", ("dp", "fsdp")),
    )
    return jax.shard_map(
        on_device, mesh=mesh, in_specs=in_specs, out_specs=out_specs, check_vma=False
    )
```

profile of v0, /device:TPU:8, one launch (start us, length us, event | category | flops | bytes accessed | tf_op | source)
XLA Modules:
  0.0 1925.1 jit_solution(9889861834597921747)
XLA Ops:
  10.6 41.1 %all-reduce.8 = (bf16[2048]{0:T(1024)(128)(2,1)}, bf16[2048]{0:T(1024)(128)(2,1)S(1)}, bf16[32,32]{1,0:T(8,128)(2,1)S(1)}) all-reduce(bf16[2048]{0:T(1024)(128)(2,1)S(1)} %dynamic-update-slice.2, bf16[2048]{0:T(1024)(128)(2,1)S(1)} %dynamic-update-slice, ...), channel_id=1, replica_groups=mesh['dp'=4,'ctx'=4,'fsdp'=2] {'dp','ctx','fsdp'}, use_global_device_ids=true, to_apply=%add.2 | all-reduce | flops 5120 | bytes 20480
  61.8 35.1 %all-gather.14.cloned.1.call-done = bf16[1024,2048]{1,0:T(8,128)(2,1)} async-done(((bf16[256,2048]{1,0:T(8,128)(2,1)}), bf16[1024,2048]{1,0:T(8,128)(2,1)}) %all-gather.14.cloned.1.call-update) | async-done | bytes 4194320 | tf_op jit(solution)/shard_map/all_gather | solution.py:81
  103.1 45.2 %all-gather.18.cloned.1.call-done = bf16[2048,512]{1,0:T(8,128)(2,1)} async-done(((bf16[256,512]{1,0:T(8,128)(2,1)}), bf16[2048,512]{1,0:T(8,128)(2,1)}) %all-gather.18.cloned.1.call-update) | async-done | bytes 2097168 | tf_op jit(solution)/shard_map/all_gather | solution.py:40
  154.6 43.6 %all-gather.16.cloned.1.call-done = bf16[2048,512]{1,0:T(8,128)(2,1)} async-done(((bf16[256,512]{1,0:T(8,128)(2,1)}), bf16[2048,512]{1,0:T(8,128)(2,1)}) %all-gather.16.cloned.1.call-update) | async-done | bytes 2097168 | tf_op jit(solution)/shard_map/all_gather | solution.py:39
  204.5 128.6 %while.39 = (s32[]{:T(128)}, bf16[2,512,8,64]{1,3,2,0:T(8,128)(2,1)S(1)}, f32[2,8,512,1]{2,1,3,0:T(8,128)S(1)}, s32[2]{0:T(128)S(1)}, s32[1024]{0:T(1024)S(1)}, ...) while((s32[]{:T(128)}, ...), condition=%wide.region_11.12_spmd, body=%wide.region_8.11_spmd.sunk | while | flops 1407709184 | bytes 160060144 | solution.py:113
  236.6 24.2 %fusion.226 = (f32[8,512]{1,0:T(8,128)S(1)}, f32[8,512,1024]{2,1,0:T(8,128)}) fusion(f32[512,1024,8]{1,2,0:T(8,128)} %fusion.225, bf16[1024,8,64]{0,2,1:T(8,128)(2,1)} %get-tuple-element.720, bf16[1024,8,64]{0,2,1:T(8,128)(2,1)} %get-tuple-element.719, s32[]{:T(128)S(6)} %select_n.81, pred[512,1024]{1,0:T(8,128)(4,1)S(1)} %broadcast_compare_fusion.7), kind=kOutput, calls=%fused_computation.180.clone.1 | convolution fusion | flops 549449728 | bytes 35667972 | tf_op jit(solution)/shard_map/while/body/eval_jaxpr/ihd,jhd->hij/dot_general | solution.py:64
  293.6 24.1 %fusion.226 = (f32[8,512]{1,0:T(8,128)S(1)}, f32[8,512,1024]{2,1,0:T(8,128)}) fusion(f32[512,1024,8]{1,2,0:T(8,128)} %fusion.225, bf16[1024,8,64]{0,2,1:T(8,128)(2,1)} %get-tuple-element.720, bf16[1024,8,64]{0,2,1:T(8,128)(2,1)} %get-tuple-element.719, s32[]{:T(128)S(6)} %select_n.81, pred[512,1024]{1,0:T(8,128)(4,1)S(1)} %broadcast_compare_fusion.7), kind=kOutput, calls=%fused_computation.180.clone.1 | convolution fusion | flops 549449728 | bytes 35667972 | tf_op jit(solution)/shard_map/while/body/eval_jaxpr/ihd,jhd->hij/dot_general | solution.py:64
  343.0 69.5 %reduce-scatter.17.cloned.1.call-done = f32[256,2048]{1,0:T(8,128)} async-done(((f32[1024,2048]{1,0:T(8,128)}), f32[256,2048]{1,0:T(8,128)}) %reduce-scatter.17.cloned.1.call-update) | async-done | bytes 2097168 | tf_op jit(solution)/shard_map/reduce_scatter | solution.py:116
  418.4 142.7 %while.38 = (s32[]{:T(128)}, bf16[2,512,8,64]{1,3,2,0:T(8,128)(2,1)S(1)}, s32[2]{0:T(128)S(1)}, s32[1024]{0:T(1024)S(1)}, s32[1,1024]{1,0:T(1,128)S(1)}, /*index...) while((s32[]{:T(128)}, ...), condition=%wide.region_4.5_spmd, body=%wide.region_1.4_spmd.sunk | while | flops 1403525120 | bytes 109630152 | solution.py:113
  436.3 23.7 %fusion.218 = f32[8,512,1024]{2,1,0:T(8,128)} fusion(f32[512,1024,8]{1,2,0:T(8,128)} %fusion.217, bf16[1024,8,64]{0,2,1:T(8,128)(2,1)} %get-tuple-element.762, pred[512,1024]{1,0:T(8,128)(4,1)S(1)} %broadcast_compare_fusion.6, bf16[1024,8,64]{0,2,1:T(8,128)(2,1)} %get-tuple-element.761, s32[]{:T(128)S(6)} %select_n.79), kind=kOutput, calls=%fused_computation.5.clone.1 | convolution fusion | flops 545259520 | bytes 35651588 | tf_op jit(solution)/shard_map/while/body/eval_jaxpr/ihd,jhd->hij/dot_general | solution.py:64
  506.4 25.0 %fusion.218 = f32[8,512,1024]{2,1,0:T(8,128)} fusion(f32[512,1024,8]{1,2,0:T(8,128)} %fusion.217, bf16[1024,8,64]{0,2,1:T(8,128)(2,1)} %get-tuple-element.762, pred[512,1024]{1,0:T(8,128)(4,1)S(1)} %broadcast_compare_fusion.6, bf16[1024,8,64]{0,2,1:T(8,128)(2,1)} %get-tuple-element.761, s32[]{:T(128)S(6)} %select_n.79), kind=kOutput, calls=%fused_computation.5.clone.1 | convolution fusion | flops 545259520 | bytes 35651588 | tf_op jit(solution)/shard_map/while/body/eval_jaxpr/ihd,jhd->hij/dot_general | solution.py:64
  545.3 15.4 fusion.220
  578.9 44.9 %all-gather.26.cloned.1.call-done = bf16[2048,1280]{1,0:T(8,128)(2,1)} async-done(((bf16[256,1280]{1,0:T(8,128)(2,1)}), bf16[2048,1280]{1,0:T(8,128)(2,1)}) %all-gather.26.cloned.1.call-update) | async-done | bytes 5242896 | tf_op jit(solution)/shard_map/all_gather | solution.py:48
  634.2 24.9 %all-gather.36.cloned.1.call-done = bf16[1,1024,2048]{2,1,0:T(8,128)(2,1)} async-done(((bf16[1,256,2048]{2,1,0:T(8,128)(2,1)}), bf16[1,1024,2048]{2,1,0:T(8,128)(2,1)}) %all-gather.36.cloned.1.call-update) | async-done | bytes 4194320 | tf_op jit(solution)/shard_map/all_gather | solution.py:204
  659.1 87.7 %all-gather.30.cloned.1.call-done = bf16[1280,2048]{1,0:T(8,128)(2,1)} async-done(((bf16[1280,256]{1,0:T(8,128)(2,1)}), bf16[1280,2048]{1,0:T(8,128)(2,1)}) %all-gather.30.cloned.1.call-update) | async-done | bytes 5242896 | tf_op jit(solution)/shard_map/all_gather | solution.py:50
  746.7 16.3 multiply_convert_fusion.2
  779.1 42.0 %reduce-scatter.13.cloned.1.call-done = f32[256,2048]{1,0:T(8,128)} async-done(((f32[1024,2048]{1,0:T(8,128)}), f32[256,2048]{1,0:T(8,128)}) %reduce-scatter.13.cloned.1.call-update) | async-done | bytes 2097168 | tf_op jit(solution)/shard_map/reduce_scatter | solution.py:116
  821.1 74.3 %reduce-scatter.19.cloned.1.call-done = f32[256,2048]{1,0:T(8,128)} async-done(((f32[1024,2048]{1,0:T(8,128)}), f32[256,2048]{1,0:T(8,128)}) %reduce-scatter.19.cloned.1.call-update) | async-done | bytes 2097168 | tf_op jit(solution)/shard_map/reduce_scatter | solution.py:223
  901.4 34.5 %all-gather.34.cloned.1.call-done = bf16[1024,2048]{1,0:T(8,128)(2,1)} async-done(((bf16[256,2048]{1,0:T(8,128)(2,1)}), bf16[1024,2048]{1,0:T(8,128)(2,1)}) %all-gather.34.cloned.1.call-update) | async-done | bytes 4194320 | tf_op jit(solution)/shard_map/all_gather | solution.py:237
  943.2 214.3 %while.40 = (s32[]{:T(128)}, bf16[2,512,8,64]{1,3,2,0:T(8,128)(2,1)}, f32[2,1024,8,64]{1,3,2,0:T(8,128)}, f32[2,1024,8,64]{1,3,2,0:T(8,128)}, f32[2,32,8]{1,2,0:...) while((s32[]{:T(128)}, ...), condition=%wide.region_18.19_spmd, body=%wide.region_16.18_spmd.sunk | while | flops 3307728896 | bytes 294757248 | solution.py:273
  989.2 25.9 %multiply_reduce_fusion.6 = (f32[8,512]{1,0:T(8,128)S(1)}, f32[8,512,1024]{2,1,0:T(8,128)}) fusion(f32[8,512,1024]{2,1,0:T(8,128)} %fusion.240, f32[8,512]{1,0:T(8,128)S(1)} %dynamic-slice_bitcast_fusion.2, f32[512,1024,8]{1,2,0:T(8,128)} %fusion.242, bf16[1024,8,64]{0,2,1:T(8,128)(2,1)} %get-tuple-element.817, ...), kind=kOutput, calls=%fused_computation.64.clone.1 | convolution fusion | flops 557838336 | bytes 52461572 | tf_op jit(solution)/shard_map/while/body/eval_jaxpr/ihd,jhd->hij/dot_general | solution.py:64
  1083.5 25.9 %multiply_reduce_fusion.6 = (f32[8,512]{1,0:T(8,128)S(1)}, f32[8,512,1024]{2,1,0:T(8,128)}) fusion(f32[8,512,1024]{2,1,0:T(8,128)} %fusion.240, f32[8,512]{1,0:T(8,128)S(1)} %dynamic-slice_bitcast_fusion.2, f32[512,1024,8]{1,2,0:T(8,128)} %fusion.242, bf16[1024,8,64]{0,2,1:T(8,128)(2,1)} %get-tuple-element.817, ...), kind=kOutput, calls=%fused_computation.64.clone.1 | convolution fusion | flops 557838336 | bytes 52461572 | tf_op jit(solution)/shard_map/while/body/eval_jaxpr/ihd,jhd->hij/dot_general | solution.py:64
  1180.8 44.0 %reduce-scatter.21.cloned.1.call-done = bf16[256,2048]{1,0:T(8,128)(2,1)} async-done(((bf16[1024,2048]{1,0:T(8,128)(2,1)}), bf16[256,2048]{1,0:T(8,128)(2,1)}) %reduce-scatter.21.cloned.1.call-update) | async-done | bytes 1048592 | tf_op jit(solution)/shard_map/reduce_scatter | solution.py:301
  1301.2 19.8 %convolution_convert_fusion.3 = bf16[1024,2048]{1,0:T(8,128)(2,1)} fusion(bf16[1280,2048]{1,0:T(8,128)(2,1)} %all-gather.30.cloned.1.call-done, f32[1024,1280]{1,0:T(8,128)} %fusion.113, bf16[1024,2048]{1,0:T(8,128)(2,1)} %all-gather.24.cloned.1.call-done, bf16[2048,1280]{1,0:T(8,128)(2,1)} %all-gather.28.cloned.1.call-done), kind=kOutput, calls=%fused_computation.131 | convolution fusion | flops 10752622592 | bytes 24117248 | tf_op jit(solution)/shard_map/dot_general | solution.py:123
  1321.1 53.3 %reduce-scatter.35.cloned.1.call-done = bf16[1280,256]{1,0:T(8,128)(2,1)} async-done(((bf16[1280,2048]{1,0:T(8,128)(2,1)}), bf16[1280,256]{1,0:T(8,128)(2,1)}) %reduce-scatter.35.cloned.1.call-update) | async-done | bytes 655376 | tf_op jit(solution)/shard_map/reduce_scatter | solution.py:233
  1376.6 103.7 %reduce-scatter.33.cloned.1.call-done = bf16[256,1280]{1,0:T(8,128)(2,1)} async-done(((bf16[2048,1280]{1,0:T(8,128)(2,1)}), bf16[256,1280]{1,0:T(8,128)(2,1)}) %reduce-scatter.33.cloned.1.call-update) | async-done | bytes 655376 | tf_op jit(solution)/shard_map/reduce_scatter | solution.py:230
  1482.5 103.9 %reduce-scatter.31.cloned.1.call-done = bf16[256,1280]{1,0:T(8,128)(2,1)} async-done(((bf16[2048,1280]{1,0:T(8,128)(2,1)}), bf16[256,1280]{1,0:T(8,128)(2,1)}) %reduce-scatter.31.cloned.1.call-update) | async-done | bytes 655376 | tf_op jit(solution)/shard_map/reduce_scatter | solution.py:227
  1589.0 68.2 %reduce-scatter.29.cloned.1.call-done = bf16[512,256]{1,0:T(8,128)(2,1)} async-done(((bf16[512,2048]{1,0:T(8,128)(2,1)}), bf16[512,256]{1,0:T(8,128)(2,1)}) %reduce-scatter.29.cloned.1.call-update) | async-done | bytes 262160 | tf_op jit(solution)/shard_map/reduce_scatter | solution.py:316
  1658.9 68.6 %reduce-scatter.23.cloned.1.call-done = bf16[256,512]{1,0:T(8,128)(2,1)} async-done(((bf16[2048,512]{1,0:T(8,128)(2,1)}), bf16[256,512]{1,0:T(8,128)(2,1)}) %reduce-scatter.23.cloned.1.call-update) | async-done | bytes 262160 | tf_op jit(solution)/shard_map/reduce_scatter | solution.py:307
  1729.4 68.4 %reduce-scatter.27.cloned.1.call-done = bf16[256,512]{1,0:T(8,128)(2,1)} async-done(((bf16[2048,512]{1,0:T(8,128)(2,1)}), bf16[256,512]{1,0:T(8,128)(2,1)}) %reduce-scatter.27.cloned.1.call-update) | async-done | bytes 262160 | tf_op jit(solution)/shard_map/reduce_scatter | solution.py:313
  1799.6 68.6 %reduce-scatter.25.cloned.1.call-done = bf16[256,512]{1,0:T(8,128)(2,1)} async-done(((bf16[2048,512]{1,0:T(8,128)(2,1)}), bf16[256,512]{1,0:T(8,128)(2,1)}) %reduce-scatter.25.cloned.1.call-update) | async-done | bytes 262160 | tf_op jit(solution)/shard_map/reduce_scatter | solution.py:310
  1869.9 39.6 %all-reduce.7 = (f32[2048]{0:T(1024)S(1)}, f32[1024]{0:T(1024)S(1)}, f32[2048]{0:T(1024)S(1)}) all-reduce(f32[2048]{0:T(1024)S(1)} %get-tuple-element.343, f32[1024]{0:T(1024)S(1)} %reshape.387, f32[2048]{0:T(1024)S(1)} %copy-done.31), channel_id=8, replica_groups=mesh['dp'=4,'ctx'=4,'fsdp'=2] {'dp','ctx','fsdp'}, use_global_device_ids=true, to_apply=%region_24.25.clone | all-reduce | flops 5120 | bytes 40960
  (302 shorter events, 495.3 us)
Async XLA Ops:
  7.2 54.6 %all-gather.20.cloned.1.call-start = ((), (), s32[]{:S(2)}) async-start(), calls=%async_computation.15 | async-start | bytes 2359296 | tf_op jit(solution)/shard_map/all_gather | solution.py:41
  7.9 89.0 %all-gather.14.cloned.1.call-start = ((), (), s32[]{:S(2)}) async-start(), calls=%async_computation.12 | async-start | bytes 5242880 | tf_op jit(solution)/shard_map/all_gather | solution.py:81
  56.9 91.5 %all-gather.18.cloned.1.call-start = ((), (), s32[]{:S(2)}) async-start(), calls=%async_computation.14 | async-start | bytes 2359296 | tf_op jit(solution)/shard_map/all_gather | solution.py:40
  57.6 140.5 %all-gather.16.cloned.1.call-start = ((), (), s32[]{:S(2)}) async-start(), calls=%async_computation.13 | async-start | bytes 2359296 | tf_op jit(solution)/shard_map/all_gather | solution.py:39
  58.2 276.3 %all-gather.22.cloned.1.call-start = ((), (), s32[]{:S(2)}) async-start(), calls=%async_computation.16 | async-start | bytes 2359296 | tf_op jit(solution)/shard_map/all_gather | solution.py:42
  58.8 353.7 %reduce-scatter.17.cloned.1.call-start = ((), (), s32[]{:S(2)}) async-start(), calls=%async_computation.23 | async-start | bytes 10485760 | tf_op jit(solution)/shard_map/reduce_scatter | solution.py:116
  342.2 226.3 %all-gather.28.cloned.1.call-start = ((), (), s32[]{:S(2)}) async-start(), calls=%async_computation.20 | async-start | bytes 5898240 | tf_op jit(solution)/shard_map/all_gather | solution.py:49
  342.9 225.6 %all-gather.32.cloned.1.call-start = ((), (), s32[]{:S(2)}) async-start(), calls=%async_computation.24 | async-start | bytes 5242880 | tf_op jit(solution)/shard_map/all_gather | solution.py:118
  343.0 73.1 %copy-start.26 = (f32[2048]{0:T(1024)}, f32[2048]{0:T(1024)S(1)}, u32[]{:S(2)}) copy-start(f32[2048]{0:T(1024)S(1)} %convert_element_type.321) | copy-start | bytes 24580
  416.1 207.7 %all-gather.26.cloned.1.call-start = ((), (), s32[]{:S(2)}) async-start(), calls=%async_computation.19 | async-start | bytes 5898240 | tf_op jit(solution)/shard_map/all_gather | solution.py:48
  416.9 242.2 %all-gather.36.cloned.1.call-start = ((), (), s32[]{:S(2)}) async-start(), calls=%async_computation.35 | async-start | bytes 5242880 | tf_op jit(solution)/shard_map/all_gather | solution.py:204
  417.4 329.3 %all-gather.30.cloned.1.call-start = ((), (), s32[]{:S(2)}) async-start(), calls=%async_computation.21 | async-start | bytes 5898240 | tf_op jit(solution)/shard_map/all_gather | solution.py:50
  418.2 403.0 %reduce-scatter.13.cloned.1.call-start = ((), (), s32[]{:S(2)}) async-start(), calls=%async_computation.17 | async-start | bytes 10485760 | tf_op jit(solution)/shard_map/reduce_scatter | solution.py:116
  568.4 327.1 %reduce-scatter.19.cloned.1.call-start = ((), (), s32[]{:S(2)}) async-start(), calls=%async_computation.25 | async-start | bytes 10485760 | tf_op jit(solution)/shard_map/reduce_scatter | solution.py:223
  779.0 116.5 %copy-start.3 = (bf16[1,256,2048]{2,1,0:T(8,128)(2,1)S(1)}, bf16[1,256,2048]{2,1,0:T(8,128)(2,1)}, u32[]{:S(2)}) copy-start(bf16[1,256,2048]{2,1,0:T(8,128)(2,1)} %param.20) | copy-start | bytes 3145732
  779.0 116.5 %copy-start.6 = (f32[256,2048]{1,0:T(8,128)S(1)}, f32[256,2048]{1,0:T(8,128)}, u32[]{:S(2)}) copy-start(f32[256,2048]{1,0:T(8,128)} %reduce-scatter.17.cloned.1.call-done) | copy-start | bytes 6291460
  779.0 116.5 %copy-start.27 = (f32[2048]{0:T(1024)S(1)}, f32[2048]{0:T(1024)}, u32[]{:S(2)}) copy-start(f32[2048]{0:T(1024)} %copy-done.26) | copy-start | bytes 24580
  779.0 116.5 %copy-start.33 = (f32[256]{0:T(256)S(1)}, f32[256]{0:T(256)}, u32[]{:S(2)}) copy-start(f32[256]{0:T(256)} %copy-done.32) | copy-start | bytes 3076
  779.1 120.4 %copy-start.42 = (f32[256]{0:T(256)S(1)}, f32[256]{0:T(256)}, u32[]{:S(2)}) copy-start(f32[256]{0:T(256)} %copy-done.41) | copy-start | bytes 3076
  779.1 156.9 %all-gather.34.cloned.1.call-start = ((), (), s32[]{:S(2)}) async-start(), calls=%async_computation.26 | async-start | bytes 5242880 | tf_op jit(solution)/shard_map/all_gather | solution.py:237
  901.3 323.5 %reduce-scatter.21.cloned.1.call-start = ((), (), s32[]{:S(2)}) async-start(), calls=%async_computation.27 | async-start | bytes 5242880 | tf_op jit(solution)/shard_map/reduce_scatter | solution.py:301
  1180.2 110.5 %all-gather.24.cloned.1.call-start = ((), (), s32[]{:S(2)}) async-start(), calls=%async_computation.18 | async-start | bytes 5242880 | tf_op jit(solution)/shard_map/all_gather | solution.py:118
  1233.2 141.1 %reduce-scatter.35.cloned.1.call-start = ((), (), s32[]{:S(2)}) async-start(), calls=%async_computation.34 | async-start | bytes 5898240 | tf_op jit(solution)/shard_map/reduce_scatter | solution.py:233
  1245.0 235.3 %reduce-scatter.33.cloned.1.call-start = ((), (), s32[]{:S(2)}) async-start(), calls=%async_computation.33 | async-start | bytes 5898240 | tf_op jit(solution)/shard_map/reduce_scatter | solution.py:230
  1254.9 331.5 %reduce-scatter.31.cloned.1.call-start = ((), (), s32[]{:S(2)}) async-start(), calls=%async_computation.32 | async-start | bytes 5898240 | tf_op jit(solution)/shard_map/reduce_scatter | solution.py:227
  1264.8 392.4 %reduce-scatter.29.cloned.1.call-start = ((), (), s32[]{:S(2)}) async-start(), calls=%async_computation.31 | async-start | bytes 2359296 | tf_op jit(solution)/shard_map/reduce_scatter | solution.py:316
  1271.9 455.7 %reduce-scatter.23.cloned.1.call-start = ((), (), s32[]{:S(2)}) async-start(), calls=%async_computation.28 | async-start | bytes 2359296 | tf_op jit(solution)/shard_map/reduce_scatter | solution.py:307
  1278.0 519.8 %reduce-scatter.27.cloned.1.call-start = ((), (), s32[]{:S(2)}) async-start(), calls=%async_computation.30 | async-start | bytes 2359296 | tf_op jit(solution)/shard_map/reduce_scatter | solution.py:313
  1284.5 583.6 %reduce-scatter.25.cloned.1.call-start = ((), (), s32[]{:S(2)}) async-start(), calls=%async_computation.29 | async-start | bytes 2359296 | tf_op jit(solution)/shard_map/reduce_scatter | solution.py:310
  1290.5 624.9 %reduce-scatter.15.cloned.1.call-start = ((), (), s32[]{:S(2)}) async-start(), calls=%async_computation.22 | async-start | bytes 5242880 | tf_op jit(solution)/shard_map/reduce_scatter | solution.py:124
  1321.1 548.9 %copy-start.31 = (f32[2048]{0:T(1024)S(1)}, f32[2048]{0:T(1024)}, u32[]{:S(2)}) copy-start(f32[2048]{0:T(1024)} %get-tuple-element.341) | copy-start | bytes 24580
  1321.1 594.4 %copy-start.9 = (f32[256,2048]{1,0:T(8,128)S(1)}, f32[256,2048]{1,0:T(8,128)}, u32[]{:S(2)}) copy-start(f32[256,2048]{1,0:T(8,128)} %reduce-scatter.13.cloned.1.call-done) | copy-start | bytes 6291460
  (48 other events, 791.1 us)
Sparse Core Ops, SparseCore 0:
  10.1 51.6 all-gather.19
  63.9 32.9 all-gather.13
  99.1 49.2 all-gather.17
  150.4 47.7 all-gather.15
  200.1 47.7 all-gather.21
  342.3 70.1 reduce-scatter.16
  414.9 85.1 all-gather.27
  502.4 33.7 all-gather.31
  538.6 85.1 all-gather.25
  625.3 33.7 all-gather.35
  661.3 85.3 all-gather.29
  749.3 71.7 reduce-scatter.12
  823.7 71.7 reduce-scatter.18
  901.4 34.4 all-gather.33
  1180.3 44.4 reduce-scatter.20
  1233.3 34.4 all-gather.23
  1271.3 102.9 reduce-scatter.34
  1377.8 102.4 reduce-scatter.32
  1483.9 102.4 reduce-scatter.30
  1589.8 67.3 reduce-scatter.28
  1660.7 66.8 reduce-scatter.22
  1731.1 66.6 reduce-scatter.26
  1801.3 66.7 reduce-scatter.24
  1870.5 44.8 reduce-scatter.14
where the time goes:
time: 1930 us
  waiting for transfers between devices  1090 us (56%)
  matrix products  520 us (27%)
  other arithmetic  126 us (7%)
  blocking collectives  80.8 us (4%)
  loops' own time  53 us (3%)
  local copies, waits for them, and re-layouts  36.1 us (2%)
    dot_general x6, matrix products, block_scores(): jnp.einsum('ihd,jhd->hij', query_block, key_rows, preferred_element_type=...  149 us
    reduce_scatter x2, waiting for transfers between devices, layer_forward(): lax.psum_scatter(attn_term, 'ctx', scatter_dimension=0, tiled=True)  112 us
    reduce_scatter x1, waiting for transfers between devices, on_device(): lax.psum_scatter(grad_w_gate.astype(jnp.bfloat16), ('dp', 'fsdp'), scatte...  104 us
    reduce_scatter x1, waiting for transfers between devices, on_device(): lax.psum_scatter(grad_w_up.astype(jnp.bfloat16), ('dp', 'fsdp'), scatter_...  104 us
    all_gather x1, waiting for transfers between devices, gather_feedforward(): lax.all_gather(w_down, ('dp', 'fsdp'), axis=1, tiled=True)  87.7 us
    unnamed x2, blocking collectives  80.8 us
    dot_general x6, matrix products, block_scores(): jnp.einsum('bij,bh->hij', one_hot, table_local, preferred_element_type=jn...  75.4 us
    reduce_scatter x1, waiting for transfers between devices, on_device(): lax.psum_scatter(ffn_normed_term, 'ctx', scatter_dimension=0, tiled=True)  74.3 us
  transfers between devices with their start and end apart: 24, of which 20 were waited for; matrix products, arithmetic and copies ran while one was open for 23% of the time, Pallas kernels for 0%

commit v1 on v0

--- a/solution.py
+++ b/solution.py
@@ -1,17 +1,848 @@
+import functools
+
 import jax
 import jax.numpy as jnp
 from jax import lax
+from jax.experimental import pallas as pl
+from jax.experimental.pallas import tpu as pltpu
 from jax.sharding import PartitionSpec as P
 
 H = 32
 DH = 64
 NB = 32
-QB = 512
-
-
 EPSILON = 1e-06
 THRESHOLDS = (12, 16, 23, 32, 46, 64, 91)
 MASKED = -1e30
+BF = jnp.bfloat16
+F32 = jnp.float32
+ANY = pl.BlockSpec(memory_space=pl.ANY)
+VM = pl.BlockSpec(memory_space=pltpu.VMEM)
+MESH = pl.DeviceIdType.MESH
+DMA = pltpu.SemaphoreType.DMA
+
+
+class Place:
+    def __init__(self):
+        self.z = lax.axis_index("dp")
+        self.c = lax.axis_index("ctx")
+        self.y = lax.axis_index("fsdp")
+        self.x = self.c // 2
+        self.k = self.c % 2
+
+    def device(self, z=None, x=None, k=None, y=None):
+        z = self.z if z is None else z
+        x = self.x if x is None else x
+        k = self.k if k is None else k
+        y = self.y if y is None else y
+        return {"dp": z, "ctx": x * 2 + k, "fsdp": y}
+
+    def x_peer(self):
+        return self.device(x=1 - self.x)
+
+    def y_peer(self):
+        return self.device(y=1 - self.y)
+
+    def core_peer(self):
+        return self.device(k=1 - self.k)
+
+
+def block_of(x, k, y):
+    return y * 4 + x * 2 + k
+
+
+def remote(src, dst, send_sem, recv_sem, device):
+    return pltpu.make_async_remote_copy(
+        src_ref=src,
+        dst_ref=dst,
+        send_sem=send_sem,
+        recv_sem=recv_sem,
+        device_id=device,
+        device_id_type=MESH,
+    )
+
+
+def greet(devices):
+    barrier = pltpu.get_barrier_semaphore()
+    for device in devices:
+        pl.semaphore_signal(barrier, inc=1, device_id=device, device_id_type=MESH)
+    pl.semaphore_wait(barrier, len(devices))
+
+
+class ActGather:
+    def __init__(self, me, own, out, send, recv, local):
+        self.me, self.own, self.out = me, own, out
+        self.send, self.recv, self.local = send, recv, local
+        self.rows = own.shape[0]
+        self.half = self.rows // 2
+
+    def part(self, ref, block, h):
+        return ref.at[block, pl.ds(h * self.half, self.half)]
+
+    def copy(self, i):
+        me = self.me
+        x, k, y = me.x, me.k, me.y
+        own = block_of(x, k, y)
+        if i == 0:
+            src, dst, dev = self.own.at[pl.ds(0, self.half)], self.part(self.out, own, 0), me.x_peer()
+        elif i == 1:
+            src, dst, dev = self.own.at[pl.ds(self.half, self.half)], self.part(self.out, own, 1), me.y_peer()
+        elif i == 2:
+            src, dst, dev = self.own.at[pl.ds(0, self.half)], self.part(self.out, own, 0), me.y_peer()
+        elif i == 3:
+            b = block_of(1 - x, k, y)
+            src, dst, dev = self.part(self.out, b, 0), self.part(self.out, b, 0), me.y_peer()
+        elif i == 4:
+            src, dst, dev = self.own.at[pl.ds(self.half, self.half)], self.part(self.out, own, 1), me.x_peer()
+        elif i == 5:
+            b = block_of(x, k, 1 - y)
+            src, dst, dev = self.part(self.out, b, 1), self.part(self.out, b, 1), me.x_peer()
+        elif i == 6:
+            src, dst, dev = self.own, self.out.at[own], me.core_peer()
+        else:
+            px, py, h = ((1, 0, 0), (0, 1, 1), (0, 1, 0), (1, 1, 0), (1, 0, 1), (1, 1, 1))[i - 7]
+            b = block_of(1 - x if px else x, k, 1 - y if py else y)
+            src, dst, dev = self.part(self.out, b, h), self.part(self.out, b, h), me.core_peer()
+        return remote(src, dst, self.send.at[i], self.recv.at[i], dev)
+
+    def start(self):
+        for i in (0, 1, 2, 4, 6):
+            self.copy(i).start()
+        own = block_of(self.me.x, self.me.k, self.me.y)
+        pltpu.make_async_copy(self.own, self.out.at[own], self.local).start()
+
+    def forward(self):
+        self.copy(0).wait_recv()
+        self.copy(3).start()
+        self.copy(7).start()
+        self.copy(1).wait_recv()
+        self.copy(5).start()
+        self.copy(8).start()
+
+    def forward_core(self):
+        for i in (2, 4, 3, 5):
+            self.copy(i).wait_recv()
+            self.copy(i + 7).start()
+
+    def finish(self):
+        for i in range(6, 13):
+            self.copy(i).wait_recv()
+        for i in range(13):
+            self.copy(i).wait_send()
+        own = block_of(self.me.x, self.me.k, self.me.y)
+        pltpu.make_async_copy(self.own, self.out.at[own], self.local).wait()
+
+
+def gather_sems():
+    return [DMA((13,)), DMA((13,)), DMA]
+
+
+class ActReduce:
+    def __init__(self, me, part, core_in, mine, a_y, b_x, a_x, b_y, send, recv, local):
+        self.me, self.part, self.core_in, self.mine = me, part, core_in, mine
+        self.a_y, self.b_x, self.a_x, self.b_y = a_y, b_x, a_x, b_y
+        self.send, self.recv, self.local = send, recv, local
+        self.half = part.shape[1] // 2
+
+    def order(self):
+        x, y = self.me.x, self.me.y
+        return ((1 - x, 1 - y), (x, 1 - y), (1 - x, y), (x, y))
+
+    def core_copy(self, i):
+        me = self.me
+        ox, oy = self.order()[i]
+        return remote(
+            self.part.at[block_of(ox, 1 - me.k, oy)],
+            self.core_in.at[oy * 2 + ox],
+            self.send.at[i],
+            self.recv.at[i],
+            me.core_peer(),
+        )
+
+    def local_copy(self, i):
+        ox, oy = self.order()[i]
+        return pltpu.make_async_copy(
+            self.part.at[block_of(ox, self.me.k, oy)], self.mine.at[oy * 2 + ox], self.local.at[i]
+        )
+
+    def start(self):
+        for i in range(4):
+            self.core_copy(i).start()
+            self.local_copy(i).start()
+
+    def rows(self, h):
+        return pl.ds(h * self.half, self.half)
+
+    def add(self, slot, h, extra=None):
+        steps = self.half // 16
+
+        def body(i, carry):
+            r = pl.ds(pl.multiple_of(h * self.half + i * 16, 16), 16)
+            total = self.mine[slot, r, :].astype(F32) + self.core_in[slot, r, :].astype(F32)
+            if extra is not None:
+                total = total + extra[pl.ds(pl.multiple_of(i * 16, 16), 16), :].astype(F32)
+            self.mine[slot, r, :] = total.astype(BF)
+            return carry
+
+        lax.fori_loop(0, steps, body, 0)
+
+    def copies(self):
+        me = self.me
+        x, y = me.x, me.y
+        out = {}
+        out["ay0"] = remote(self.mine.at[(1 - y) * 2 + (1 - x), self.rows(0)], self.a_y.at[0], self.send.at[4], self.recv.at[4], me.y_peer())
+        out["ay1"] = remote(self.mine.at[(1 - y) * 2 + x, self.rows(0)], self.a_y.at[1], self.send.at[5], self.recv.at[5], me.y_peer())
+        out["bx0"] = remote(self.mine.at[(1 - y) * 2 + (1 - x), self.rows(1)], self.b_x.at[0], self.send.at[6], self.recv.at[6], me.x_peer())
+        out["bx1"] = remote(self.mine.at[y * 2 + (1 - x), self.rows(1)], self.b_x.at[1], self.send.at[7], self.recv.at[7], me.x_peer())
+        out["ax"] = remote(self.mine.at[y * 2 + (1 - x), self.rows(0)], self.a_x, self.send.at[8], self.recv.at[8], me.x_peer())
+        out["by"] = remote(self.mine.at[(1 - y) * 2 + x, self.rows(1)], self.b_y, self.send.at[9], self.recv.at[9], me.y_peer())
+        return out
+
+    def run(self):
+        x, y = self.me.x, self.me.y
+        c = self.copies()
+        self.core_copy(0).wait_recv()
+        self.local_copy(0).wait()
+        self.add((1 - y) * 2 + (1 - x), 0)
+        c["ay0"].start()
+        self.add((1 - y) * 2 + (1 - x), 1)
+        c["bx0"].start()
+        self.core_copy(1).wait_recv()
+        self.local_copy(1).wait()
+        self.add((1 - y) * 2 + x, 0)
+        c["ay1"].start()
+        self.core_copy(2).wait_recv()
+        self.local_copy(2).wait()
+        self.add(y * 2 + (1 - x), 1)
+        c["bx1"].start()
+        c["ay0"].wait_recv()
+        self.add(y * 2 + (1 - x), 0, self.a_y.at[0])
+        c["ax"].start()
+        c["bx0"].wait_recv()
+        self.add((1 - y) * 2 + x, 1, self.b_x.at[0])
+        c["by"].start()
+        self.core_copy(3).wait_recv()
+        self.local_copy(3).wait()
+        for name in ("ay1", "bx1", "ax", "by"):
+            c[name].wait_recv()
+
+    def total(self, h, i):
+        slot = self.me.y * 2 + self.me.x
+        r = pl.ds(pl.multiple_of(h * self.half + i * 16, 16), 16)
+        q = pl.ds(pl.multiple_of(i * 16, 16), 16)
+        total = self.mine[slot, r, :].astype(F32) + self.core_in[slot, r, :].astype(F32)
+        if h == 0:
+            return total + self.a_y[1, q, :].astype(F32) + self.a_x[q, :].astype(F32)
+        return total + self.b_x[1, q, :].astype(F32) + self.b_y[q, :].astype(F32)
+
+    def finish(self):
+        for i in range(4):
+            self.core_copy(i).wait_send()
+        for copy in self.copies().values():
+            copy.wait_send()
+
+
+def reduce_scratch(rows, width):
+    half = rows // 2
+    return [
+        pltpu.VMEM((4, rows, width), BF),
+        pltpu.VMEM((4, rows, width), BF),
+        pltpu.VMEM((2, half, width), BF),
+        pltpu.VMEM((2, half, width), BF),
+        pltpu.VMEM((half, width), BF),
+        pltpu.VMEM((half, width), BF),
+        DMA((10,)),
+        DMA((10,)),
+        DMA((4,)),
+    ]
+
+
+def first_kernel(
+    n, wq, wk, wv, wo, wg, wu, wd, xin, small, seg,
+    wqkv, wof, wgu_y, wd_y, xall, smalls, segs,
+    y_send, y_recv, y_local, r_send, l_send, z_recv,
+    ag_send, ag_recv, ag_local, s_send, s_recv, s2_send, s2_recv, s_local,
+):
+    me = Place()
+    z, y = me.z, me.y
+    rows = wq.shape[0]
+    heads = wq.shape[1] // 2
+    hid = wg.shape[1] // 2
+    group = [me.device(x=ox, k=ok, y=oy) for ox in (me.x, 1 - me.x) for ok in (me.k, 1 - me.k) for oy in (me.y, 1 - me.y)][1:]
+    others = [me.device(z=lax.rem(z + s, n)) for s in range(1, n)]
+    greet(group + others)
+
+    piece = z * 2 + y
+    row = pl.ds(pl.multiple_of(piece * rows, rows), rows)
+
+    def y_copies(yh):
+        col = pl.ds(pl.multiple_of(yh * heads, heads), heads)
+        fcol = pl.ds(pl.multiple_of(yh * hid, hid), hid)
+        sub = pl.ds(pl.multiple_of(y * rows, rows), rows)
+        return [
+            (wq.at[:, col], wqkv.at[row, pl.ds(0, heads)]),
+            (wk.at[:, col], wqkv.at[row, pl.ds(heads, heads)]),
+            (wv.at[:, col], wqkv.at[row, pl.ds(2 * heads, heads)]),
+            (wo.at[col, :], wof.at[:, row]),
+            (wg.at[:, fcol], wgu_y.at[sub, pl.ds(0, hid)]),
+            (wu.at[:, fcol], wgu_y.at[sub, pl.ds(hid, hid)]),
+            (wd.at[fcol, :], wd_y.at[:, sub]),
+        ]
+
+    sends = [
+        remote(src, dst, y_send.at[i], y_recv.at[i], me.y_peer())
+        for i, (src, dst) in enumerate(y_copies(1 - y))
+    ]
+    keeps = [
+        pltpu.make_async_copy(src, dst, y_local.at[i]) for i, (src, dst) in enumerate(y_copies(y))
+    ]
+    me_small = z * 8 + me.c * 2 + y
+    small_local = pltpu.make_async_copy(small, smalls.at[me_small], s_local.at[0])
+    seg_local = pltpu.make_async_copy(seg, segs.at[y], s_local.at[1])
+    small_sends = [
+        remote(small, smalls.at[me_small], s_send.at[i], s_recv.at[i], dev) for i, dev in enumerate(group)
+    ]
+    seg_send = remote(seg, segs.at[y], s_send.at[7], s_recv.at[7], me.y_peer())
+    for i in range(4):
+        sends[i].start()
+        keeps[i].start()
+    small_local.start()
+    seg_local.start()
+    for copy in small_sends:
+        copy.start()
+    seg_send.start()
+    act = ActGather(me, xin, xall, ag_send, ag_recv, ag_local)
+    act.start()
+    for i in range(4, 7):
+        sends[i].start()
+        keeps[i].start()
+
+    def slot_copies(t, yy, sem, right):
+        r = pl.ds(pl.multiple_of((t * 2 + yy) * rows, rows), rows)
+        dev = me.device(z=z + 1 if right else z - 1)
+        recv = z_recv.at[t, yy, 0], z_recv.at[t, yy, 1]
+        return (
+            remote(wqkv.at[r, :], wqkv.at[r, :], sem.at[t, yy, 0], recv[0], dev),
+            remote(wof.at[:, r], wof.at[:, r], sem.at[t, yy, 1], recv[1], dev),
+        )
+
+    def send_both(t, yy, do):
+        @pl.when(z + 1 <= n - 1)
+        def _():
+            for copy in slot_copies(t, yy, r_send, True):
+                do(copy)
+
+        @pl.when(z >= 1)
+        def _():
+            for copy in slot_copies(t, yy, l_send, False):
+                do(copy)
+
+    for i in range(4):
+        keeps[i].wait()
+    send_both(z, y, lambda copy: copy.start())
+    for i in range(4):
+        sends[i].wait_recv()
+    send_both(z, 1 - y, lambda copy: copy.start())
+
+    small_local.wait()
+    for copy in small_sends:
+        copy.wait_recv()
+    block8 = smalls.at[pl.ds(pl.multiple_of(z * 8, 8), 8)]
+    small_z = [remote(block8, block8, s2_send.at[i], s2_recv.at[i], dev) for i, dev in enumerate(others)]
+    for copy in small_z:
+        copy.start()
+    act.forward()
+    act.forward_core()
+
+    for s in range(1, n):
+        for first in range(2):
+            yy = y if first == 0 else 1 - y
+
+            @pl.when(z - s >= 0)
+            def _():
+                for copy in slot_copies(z - s, yy, r_send, True):
+                    copy.wait_recv()
+
+                @pl.when(z + 1 <= n - 1)
+                def _():
+                    for copy in slot_copies(z - s, yy, r_send, True):
+                        copy.start()
+
+            @pl.when(z + s <= n - 1)
+            def _():
+                for copy in slot_copies(z + s, yy, l_send, False):
+                    copy.wait_recv()
+
+                @pl.when(z >= 1)
+                def _():
+                    for copy in slot_copies(z + s, yy, l_send, False):
+                        copy.start()
+
+    act.finish()
+    for copy in small_z:
+        copy.wait()
+    for copy in small_sends:
+        copy.wait_send()
+    seg_send.wait()
+    seg_local.wait()
+    for i in range(7):
+        sends[i].wait_send()
+    for i in range(4, 7):
+        sends[i].wait_recv()
+        keeps[i].wait()
+    for yy in range(2):
+        send_both(z, yy, lambda copy: copy.wait_send())
+        for s in range(1, n):
+
+            @pl.when((z - s >= 0) & (z + 1 <= n - 1))
+            def _():
+                for copy in slot_copies(z - s, yy, r_send, True):
+                    copy.wait_send()
+
+            @pl.when((z + s <= n - 1) & (z >= 1))
+            def _():
+                for copy in slot_copies(z + s, yy, l_send, False):
+                    copy.wait_send()
+
+
+def first_gather(n, wq, wk, wv, wo, wg, wu, wd, xin, small, seg):
+    rows, width = wq.shape[0], xin.shape[1]
+    heads = wq.shape[1] // 2
+    hid = wg.shape[1] // 2
+    shapes = [
+        ((2 * n * rows, 3 * heads), BF),
+        ((heads, 2 * n * rows), BF),
+        ((2 * rows, 2 * hid), BF),
+        ((hid, 2 * rows), BF),
+        ((8,) + xin.shape, BF),
+        ((8 * n,) + small.shape, F32),
+        ((2,) + seg.shape, jnp.int32),
+    ]
+    return pl.pallas_call(
+        functools.partial(first_kernel, n),
+        out_shape=[jax.ShapeDtypeStruct(s, d) for s, d in shapes],
+        in_specs=[ANY] * 10,
+        out_specs=[ANY] * 7,
+        scratch_shapes=[DMA((7,)), DMA((7,)), DMA((7,)), DMA((n, 2, 2)), DMA((n, 2, 2)), DMA((n, 2, 2))]
+        + gather_sems()
+        + [DMA((8,)), DMA((8,)), DMA((n - 1,)), DMA((n - 1,)), DMA((2,))],
+        compiler_params=pltpu.CompilerParams(collective_id=0, has_side_effects=True),
+        name="first_gather",
+    )(wq, wk, wv, wo, wg, wu, wd, xin, small, seg)
+
+
+def neighbours(me):
+    return [me.x_peer(), me.y_peer(), me.core_peer()]
+
+
+def mid_kernel(part, xin, gain, mid, a2all, *scratch):
+    red = scratch[:9]
+    a2, = scratch[9:10]
+    gs = scratch[10:]
+    me = Place()
+    greet(neighbours(me))
+    r = ActReduce(me, part, *red)
+    r.start()
+    r.run()
+    half = xin.shape[0] // 2
+    for h in range(2):
+
+        def body(i, carry):
+            rr = pl.ds(pl.multiple_of(h * half + i * 16, 16), 16)
+            m = xin[rr, :].astype(F32) + r.total(h, i)
+            mid[rr, :] = m
+            inv = lax.rsqrt(jnp.mean(m * m, axis=-1, keepdims=True) + EPSILON)
+            a2[rr, :] = (m * inv * gain[...]).astype(BF)
+            return carry
+
+        lax.fori_loop(0, half // 16, body, 0)
+    g = ActGather(me, a2, a2all, *gs)
+    g.start()
+    g.forward()
+    g.forward_core()
+    g.finish()
+    r.finish()
+
+
+def mid_step(part, xin, gain):
+    rows, width = xin.shape
+    return pl.pallas_call(
+        mid_kernel,
+        out_shape=[jax.ShapeDtypeStruct((rows, width), F32), jax.ShapeDtypeStruct((8, rows, width), BF)],
+        in_specs=[ANY, VM, VM],
+        out_specs=[VM, ANY],
+        scratch_shapes=reduce_scratch(rows, width) + [pltpu.VMEM((rows, width), BF)] + gather_sems(),
+        compiler_params=pltpu.CompilerParams(collective_id=1, has_side_effects=True, vmem_limit_bytes=40 << 20),
+        name="mid_step",
+    )(part, xin, gain)
+
+
+def dz_kernel(part, mid, cot, gain, gmid, dzall, ggain, *scratch):
+    red = scratch[:9]
+    dz, = scratch[9:10]
+    gs = scratch[10:]
+    me = Place()
+    greet(neighbours(me))
+    r = ActReduce(me, part, *red)
+    r.start()
+    r.run()
+    half = mid.shape[0] // 2
+    ggain[...] = jnp.zeros_like(ggain)
+    for h in range(2):
+
+        def body(i, carry):
+            rr = pl.ds(pl.multiple_of(h * half + i * 16, 16), 16)
+            ga = r.total(h, i)
+            m = mid[rr, :]
+            inv = lax.rsqrt(jnp.mean(m * m, axis=-1, keepdims=True) + EPSILON)
+            prod = ga * (m * inv)
+            ggain[...] += prod[:8] + prod[8:]
+            u = ga * gain[...]
+            corr = jnp.mean(u * m, axis=-1, keepdims=True) * inv * inv * inv
+            gm = cot[rr, :].astype(F32) + inv * u - m * corr
+            gmid[rr, :] = gm
+            dz[rr, :] = gm.astype(BF)
+            return carry
+
+        lax.fori_loop(0, half // 16, body, 0)
+    g = ActGather(me, dz, dzall, *gs)
+    g.start()
+    g.forward()
+    g.forward_core()
+    g.finish()
+    r.finish()
+
+
+def dz_step(part, mid, cot, gain):
+    rows, width = mid.shape
+    return pl.pallas_call(
+        dz_kernel,
+        out_shape=[
+            jax.ShapeDtypeStruct((rows, width), F32),
+            jax.ShapeDtypeStruct((8, rows, width), BF),
+            jax.ShapeDtypeStruct((8, width), F32),
+        ],
+        in_specs=[ANY, VM, VM, VM],
+        out_specs=[VM, ANY, VM],
+        scratch_shapes=reduce_scratch(rows, width) + [pltpu.VMEM((rows, width), BF)] + gather_sems(),
+        compiler_params=pltpu.CompilerParams(collective_id=2, has_side_effects=True, vmem_limit_bytes=40 << 20),
+        name="dz_step",
+    )(part, mid, cot, gain)
+
+
+def last_kernel(ga_part, out_part, xin, gmid, mid, gain, gx, out, ggain, *scratch):
+    me = Place()
+    greet(neighbours(me))
+    r = ActReduce(me, ga_part, *scratch[:9])
+    q = ActReduce(me, out_part, *scratch[9:18])
+    r.start()
+    q.start()
+    r.run()
+    q.run()
+    half = xin.shape[0] // 2
+    ggain[...] = jnp.zeros_like(ggain)
+    for h in range(2):
+
+        def body(i, carry):
+            rr = pl.ds(pl.multiple_of(h * half + i * 16, 16), 16)
+            ga = r.total(h, i)
+            m = xin[rr, :].astype(F32)
+            inv = lax.rsqrt(jnp.mean(m * m, axis=-1, keepdims=True) + EPSILON)
+            prod = ga * (m * inv)
+            ggain[...] += prod[:8] + prod[8:]
+            u = ga * gain[...]
+            corr = jnp.mean(u * m, axis=-1, keepdims=True) * inv * inv * inv
+            gx[rr, :] = gmid[rr, :] + inv * u - m * corr
+            out[rr, :] = (mid[rr, :] + q.total(h, i)).astype(BF)
+            return carry
+
+        lax.fori_loop(0, half // 16, body, 0)
+    r.finish()
+    q.finish()
+
+
+def last_step(ga_part, out_part, xin, gmid, mid, gain):
+    rows, width = xin.shape
+    return pl.pallas_call(
+        last_kernel,
+        out_shape=[
+            jax.ShapeDtypeStruct((rows, width), F32),
+            jax.ShapeDtypeStruct((rows, width), BF),
+            jax.ShapeDtypeStruct((8, width), F32),
+        ],
+        in_specs=[ANY, ANY, VM, VM, VM, VM],
+        out_specs=[VM, VM, VM],
+        scratch_shapes=reduce_scratch(rows, width) * 2,
+        compiler_params=pltpu.CompilerParams(collective_id=3, has_side_effects=True, vmem_limit_bytes=50 << 20),
+        name="last_step",
+    )(ga_part, out_part, xin, gmid, mid, gain)
+
+
+TQ = 256
+
+
+def attention_forward(fvec, q, k, v, segr, segc, o, p, toep):
+    length = q.shape[0]
+    for h in range(2):
+        cols = slice(h * DH, (h + 1) * DH)
+        toep[...] = pltpu.roll(
+            jnp.broadcast_to(fvec[h], toep.shape), 0, 1, stride=1, stride_axis=0
+        )
+        kh = k[:, cols]
+        vh = v[:, cols]
+        for t in range(length // TQ):
+            rows = slice(t * TQ, (t + 1) * TQ)
+            s = lax.dot_general(q[rows, cols], kh, (((1,), (1,)), ((), ())), preferred_element_type=F32)
+            s = s + toep[:, length - t * TQ : 2 * length - t * TQ]
+            s = jnp.where(segc[0, rows, :] == segr[0], s, MASKED)
+            e = jnp.exp(s - jnp.max(s, axis=-1, keepdims=True))
+            pb = (e * (1.0 / jnp.sum(e, axis=-1, keepdims=True))).astype(BF)
+            p[h, rows, :] = pb
+            o[rows, cols] = jnp.dot(pb, vh, preferred_element_type=F32).astype(BF)
+
+
+def run_attention_forward(fvec, qkv, segr, segc):
+    total, width = qkv.shape
+    heads = width // 3 // DH
+    length = segr.shape[-1]
+    seqs = total // length
+    pairs = heads // 2
+    qspec = lambda off: pl.BlockSpec((length, 2 * DH), lambda s, h: (s, off * pairs + h))
+    return pl.pallas_call(
+        attention_forward,
+        grid=(seqs, pairs),
+        out_shape=[
+            jax.ShapeDtypeStruct((total, heads * DH), BF),
+            jax.ShapeDtypeStruct((seqs * heads, length, length), BF),
+        ],
+        in_specs=[
+            pl.BlockSpec((2, 1, 2 * length), lambda s, h: (h, 0, 0)),
+            qspec(0),
+            qspec(1),
+            qspec(2),
+            pl.BlockSpec((1, 1, length), lambda s, h: (s, 0, 0)),
+            pl.BlockSpec((1, length, 1), lambda s, h: (s, 0, 0)),
+        ],
+        out_specs=[
+            pl.BlockSpec((length, 2 * DH), lambda s, h: (s, h)),
+            pl.BlockSpec((2, length, length), lambda s, h: (s * pairs + h, 0, 0)),
+        ],
+        scratch_shapes=[pltpu.VMEM((TQ, 2 * length), F32)],
+        compiler_params=pltpu.CompilerParams(vmem_limit_bytes=48 << 20),
+        name="attention_forward",
+    )(fvec, qkv, qkv, qkv, segr, segc)
+
+
+def attention_backward(q, k, v, do, p, dq, dk, dv, diag, acc, dkt, dvt):
+    length = q.shape[0]
+    for h in range(2):
+        cols = slice(h * DH, (h + 1) * DH)
+        kh = k[:, cols]
+        vh = v[:, cols]
+        acc[...] = jnp.zeros_like(acc)
+        for t in range(length // TQ):
+            rows = slice(t * TQ, (t + 1) * TQ)
+            pb = p[h, rows, :]
+            doh = do[rows, cols]
+            qh = q[rows, cols]
+            dp = lax.dot_general(doh, vh, (((1,), (1,)), ((), ())), preferred_element_type=F32)
+            pf = pb.astype(F32)
+            ds = (pf * (dp - jnp.sum(pf * dp, axis=-1, keepdims=True))).astype(BF)
+            dq[rows, cols] = jnp.dot(ds, kh, preferred_element_type=F32).astype(BF)
+            ck = lax.dot_general(qh, ds, (((0,), (0,)), ((), ())), preferred_element_type=F32)
+            cv = lax.dot_general(doh, pb, (((0,), (0,)), ((), ())), preferred_element_type=F32)
+            if t == 0:
+                dkt[...] = ck
+                dvt[...] = cv
+            else:
+                dkt[...] += ck
+                dvt[...] += cv
+            acc[:, length - t * TQ : 2 * length - t * TQ] += ds.astype(F32)
+        dk[:, cols] = dkt[...].T.astype(BF)
+        dv[:, cols] = dvt[...].T.astype(BF)
+        n = TQ // 2
+        while n >= 8:
+            acc[0:n, :] += pltpu.roll(acc[n : 2 * n, :], 2 * length - n, 1)
+            n //= 2
+        diag[h] = acc[0:8, :]
+
+
+def run_attention_backward(qkv, do, p):
+    total, width = qkv.shape
+    heads = width // 3 // DH
+    length = p.shape[1]
+    seqs = total // length
+    pairs = heads // 2
+    qspec = lambda off: pl.BlockSpec((length, 2 * DH), lambda s, h: (s, off * pairs + h))
+    flat = pl.BlockSpec((length, 2 * DH), lambda s, h: (s, h))
+    return pl.pallas_call(
+        attention_backward,
+        grid=(seqs, pairs),
+        out_shape=[jax.ShapeDtypeStruct((total, heads * DH), BF)] * 3
+        + [jax.ShapeDtypeStruct((seqs * heads, 8, 2 * length), F32)],
+        in_specs=[
+            qspec(0),
+            qspec(1),
+            qspec(2),
+            flat,
+            pl.BlockSpec((2, length, length), lambda s, h: (s * pairs + h, 0, 0)),
+        ],
+        out_specs=[flat, flat, flat, pl.BlockSpec((2, 8, 2 * length), lambda s, h: (s * pairs + h, 0, 0))],
+        scratch_shapes=[
+            pltpu.VMEM((TQ, 2 * length), F32),
+            pltpu.VMEM((DH, length), F32),
+            pltpu.VMEM((DH, length), F32),
+        ],
+        compiler_params=pltpu.CompilerParams(vmem_limit_bytes=48 << 20),
+        name="attention_backward",
+    )(qkv, qkv, qkv, do, p)
+
+
+def offset_buckets(length):
+    relative = jnp.arange(2 * length, dtype=jnp.int32) - length
+    distance = jnp.abs(relative)
+    log_bucket = 8 + sum((distance >= t).astype(jnp.int32) for t in THRESHOLDS)
+    bucket = jnp.where(distance < 8, distance, log_bucket) + 16 * (relative > 0).astype(jnp.int32)
+    return (bucket[:, None] == jnp.arange(NB, dtype=jnp.int32)[None, :]).astype(F32)
+
+
+def swap_rows(part, y, swap):
+    rows = part.shape[0] // 2
+    mine = lax.dynamic_slice_in_dim(part, y * rows, rows, 0)
+    theirs = lax.ppermute(lax.dynamic_slice_in_dim(part, (1 - y) * rows, rows, 0), "fsdp", swap)
+    return jnp.where(y == 0, mine, theirs), jnp.where(y == 0, theirs, mine)
+
+
+def on_device(
+    n, hidden, segment_ids, positions, attn_gain, w_query, w_key, w_value, w_attn_out,
+    rel_table, ffn_gain, w_gate, w_up, w_down, cotangent,
+):
+    xin = hidden[0]
+    cot = cotangent[0]
+    rows, width = xin.shape
+    length = segment_ids.shape[1]
+    heads = w_query.shape[1] // 2
+    hid = w_gate.shape[1] // 2
+    y = lax.axis_index("fsdp")
+    c = lax.axis_index("ctx")
+    swap = [(0, 1), (1, 0)]
+    share = attn_gain.shape[0]
+    packed = jnp.concatenate([attn_gain.astype(F32), ffn_gain.astype(F32), rel_table.astype(F32)])
+    packed = jnp.pad(packed, (0, 256 - packed.shape[0]))
+    small = jnp.broadcast_to(packed[None, :], (8, 256))
+    seg = jnp.broadcast_to(segment_ids, (8, length))
+    wqkv, wo, wgu_y, wd_y, xall, smalls, segs = first_gather(
+        n, w_query, w_key, w_value, w_attn_out, w_gate, w_up, w_down, xin, small, seg
+    )
+    wgu = lax.all_gather(wgu_y, "dp", axis=0, tiled=True)
+    wd = lax.all_gather(wd_y, "dp", axis=1, tiled=True)
+    gain1 = smalls[:, 0, 0:share].reshape(1, width)
+    gain2 = smalls[:, 0, share : 2 * share].reshape(1, width)
+    table = smalls[:, 0, 2 * share : 2 * share + NB * H // (8 * n)].reshape(NB, H)
+    local_heads = heads // DH
+    table_local = lax.dynamic_slice_in_dim(table, (c * 2 + y) * local_heads, local_heads, 1)
+    one_hot = offset_buckets(length)
+    fvec = lax.dot_general(
+        table_local, one_hot, (((0,), (1,)), ((), ())), precision=lax.Precision.HIGHEST
+    ).reshape(local_heads, 1, 2 * length)
+    segr = segs[:, 0:1, :]
+    segc = segs[:, 0, :, None]
+    xf = xall.reshape(8 * rows, width).astype(F32)
+    a1 = (xf * lax.rsqrt(jnp.mean(xf * xf, axis=-1, keepdims=True) + EPSILON) * gain1).astype(BF)
+    qkv = jnp.dot(a1, wqkv, preferred_element_type=F32).astype(BF)
+    o, p = run_attention_forward(fvec, qkv, segr, segc)
+    attn_part = jnp.dot(o, wo, preferred_element_type=F32).astype(BF)
+    mid, a2all = mid_step(attn_part.reshape(8, rows, width), xin, gain2)
+    a2 = a2all.reshape(8 * rows, width)
+    gall = gather_cot(cot, mid).reshape(8 * rows, width)
+    gate_up = jnp.dot(a2, wgu, preferred_element_type=F32)
+    gate, up = gate_up[:, :hid], gate_up[:, hid:]
+    inner = 0.7978845608028654 * (gate + 0.044715 * gate * gate * gate)
+    th = jnp.tanh(inner)
+    gelu = 0.5 * gate * (1.0 + th)
+    slope = 0.5 * (1.0 + th) + 0.5 * gate * (1.0 - th * th) * 0.7978845608028654 * (
+        1.0 + 3 * 0.044715 * gate * gate
+    )
+    m = (gelu * up).astype(BF)
+    gm = lax.dot_general(gall, wd, (((1,), (1,)), ((), ())), preferred_element_type=F32)
+    dgu = jnp.concatenate([(gm * up * slope).astype(BF), (gm * gelu).astype(BF)], axis=1)
+    gw_gu = lax.dot_general(a2, dgu, (((0,), (0,)), ((), ())), preferred_element_type=F32).astype(BF)
+    gw_d = lax.dot_general(m, gall, (((0,), (0,)), ((), ())), preferred_element_type=F32).astype(BF)
+    ga2 = lax.dot_general(dgu, wgu, (((1,), (1,)), ((), ())), preferred_element_type=F32).astype(BF)
+    out_part = jnp.dot(m, wd, preferred_element_type=F32).astype(BF)
+    rs_gu = lax.psum_scatter(gw_gu, "dp", scatter_dimension=0, tiled=True)
+    rs_d = lax.psum_scatter(gw_d, "dp", scatter_dimension=1, tiled=True)
+    gmid, dzall, ggain2 = dz_step(ga2.reshape(8, rows, width), mid, cot, gain2)
+    dz = dzall.reshape(8 * rows, width)
+    do = lax.dot_general(dz, wo, (((1,), (1,)), ((), ())), preferred_element_type=F32).astype(BF)
+    gw_o = lax.dot_general(o, dz, (((0,), (0,)), ((), ())), preferred_element_type=F32).astype(BF)
+    rs_o = lax.psum_scatter(gw_o, "dp", scatter_dimension=1, tiled=True)
+    dq, dk, dv, diag = run_attention_backward(qkv, do, p)
+    dqkv = jnp.concatenate([dq, dk, dv], axis=1)
+    gw_qkv = lax.dot_general(a1, dqkv, (((0,), (0,)), ((), ())), preferred_element_type=F32).astype(BF)
+    rs_qkv = lax.psum_scatter(gw_qkv, "dp", scatter_dimension=0, tiled=True)
+    ga1 = lax.dot_general(dqkv, wqkv, (((1,), (1,)), ((), ())), preferred_element_type=F32).astype(BF)
+    gx, out, ggain1 = last_step(
+        ga1.reshape(8, rows, width), out_part.reshape(8, rows, width), xin, gmid, mid, gain1
+    )
+
+    d8 = jnp.sum(diag.reshape(-1, local_heads, 8, 2 * length), axis=0)
+    lanes = sum(jnp.roll(d8[:, r, :], -r, axis=-1) for r in range(8))
+    bias = lax.dot_general(
+        one_hot, lanes, (((0,), (1,)), ((), ())), precision=lax.Precision.HIGHEST
+    )
+    table_term = lax.dynamic_update_slice(
+        jnp.zeros((NB, H), F32), bias, (jnp.int32(0), (c * 2 + y) * local_heads)
+    )
+    axes = ("dp", "ctx", "fsdp")
+    g_attn_gain = lax.psum_scatter(jnp.sum(ggain1, axis=0), axes, scatter_dimension=0, tiled=True)
+    g_ffn_gain = lax.psum_scatter(jnp.sum(ggain2, axis=0), axes, scatter_dimension=0, tiled=True)
+    g_table = lax.psum_scatter(table_term.reshape(NB * H), axes, scatter_dimension=0, tiled=True)
+
+    lo, hi = swap_rows(rs_gu, y, swap)
+    g_gate = jnp.concatenate([lo[:, :hid], hi[:, :hid]], axis=1).astype(F32)
+    g_up = jnp.concatenate([lo[:, hid:], hi[:, hid:]], axis=1).astype(F32)
+    lo, hi = swap_rows(rs_qkv, y, swap)
+    g_q, g_k, g_v = (
+        jnp.concatenate([lo[:, i * heads : (i + 1) * heads], hi[:, i * heads : (i + 1) * heads]], axis=1).astype(F32)
+        for i in range(3)
+    )
+
+    def swap_cols(part):
+        mine = lax.dynamic_slice_in_dim(part, y * rows, rows, 1)
+        theirs = lax.ppermute(lax.dynamic_slice_in_dim(part, (1 - y) * rows, rows, 1), "fsdp", swap)
+        return jnp.concatenate(
+            [jnp.where(y == 0, mine, theirs), jnp.where(y == 0, theirs, mine)], axis=0
+        ).astype(F32)
+
+    return (
+        out[None], gx[None], g_attn_gain, g_q, g_k, g_v, swap_cols(rs_o), g_table, g_ffn_gain,
+        g_gate, g_up, swap_cols(rs_d),
+    )
+
+
+def gather_cot_kernel(cot, after, gall, send, recv, local):
+    me = Place()
+    greet(neighbours(me))
+    g = ActGather(me, cot, gall, send, recv, local)
+    g.start()
+    g.forward()
+    g.forward_core()
+    g.finish()
+
+
+def gather_cot(cot, after):
+    return pl.pallas_call(
+        gather_cot_kernel,
+        out_shape=jax.ShapeDtypeStruct((8,) + cot.shape, BF),
+        in_specs=[ANY, ANY],
+        out_specs=ANY,
+        scratch_shapes=gather_sems(),
+        compiler_params=pltpu.CompilerParams(collective_id=4, has_side_effects=True),
+        name="gather_cot",
+    )(cot, after)
+
+
+QB = 512
 
 
 def rms_norm(values, gain):
@@ -145,7 +976,7 @@
     return (result, stored)
 
 
-def on_device(
+def plain_on_device(
     hidden,
     segment_ids,
     positions,
@@ -344,7 +1175,7 @@
     )
 
 
-def solution(mesh):
+def plain_solution(mesh):
     in_specs = (
         P(("dp", "fsdp"), "ctx", None),
         P(("dp", "fsdp"), None),
@@ -376,5 +1207,22 @@
         P("ctx", ("dp", "fsdp")),
     )
     return jax.shard_map(
-        on_device, mesh=mesh, in_specs=in_specs, out_specs=out_specs, check_vma=False
-    )
+        plain_on_device, mesh=mesh, in_specs=in_specs, out_specs=out_specs, check_vma=False
+    )
+
+
+def solution(mesh):
+    if 2048 // (mesh.shape["dp"] * mesh.shape["fsdp"]) % 128 or mesh.shape["fsdp"] != 2 or mesh.shape["ctx"] != 4:
+        return plain_solution(mesh)
+    tokens = P(("dp", "fsdp"), "ctx", None)
+    line = P(("dp", "fsdp"), None)
+    every = P(("dp", "ctx", "fsdp"))
+    into = P(("dp", "fsdp"), "ctx")
+    back = P("ctx", ("dp", "fsdp"))
+    return jax.shard_map(
+        functools.partial(on_device, mesh.shape["dp"]),
+        mesh=mesh,
+        in_specs=(tokens, line, line, every, into, into, into, back, every, every, into, into, back, tokens),
+        out_specs=(tokens, tokens, every, into, into, into, back, every, every, into, into, back),
+        check_vma=False,
+    )

time: 1930 us -> 742 us (0.38)
  waiting for transfers between devices: 1090 us -> 22.8 us
  Pallas kernels: 0 us -> 459 us
  matrix products: 520 us -> 135 us
  other arithmetic: 126 us -> 24.4 us
  loops' own time: 53 us -> 0 us
  blocking collectives: 80.8 us -> 45.1 us
    reduce_scatter x12 -> x4, waiting for transfers between devices: 769 us -> 0.03 us  [the longest x1 0.02 us: on_device(): rs_qkv = lax.psum_scatter(gw_qkv, 'dp', scatter_dimension=0, tiled=True)]
    pallas_call x0 -> x7, Pallas kernels: none -> 459 us  [the longest x1 118 us: first_gather(): pl.pallas_call(functools.partial(first_kernel, n), out_shape=[jax.ShapeDt...]
    dot_general x49 -> x14, matrix products: 520 us -> 135 us  [the longest x1 18 us: on_device(): gate_up = jnp.dot(a2, wgu, preferred_element_type=F32)]
    all_gather x12 -> x2, waiting for transfers between devices: 319 us -> 0.02 us  [the longest x1 0.02 us: on_device(): wgu = lax.all_gather(wgu_y, 'dp', axis=0, tiled=True)]
    another operation x3 -> x0, loops' own time: 53 us -> none  [the longest x1 29.7 us: on_device(): lax.map(backward_block, (starts, log_total))]
    unnamed x2 -> x1, blocking collectives: 80.8 us -> 45.1 us
    convert_element_type x15 -> x8, other arithmetic: 45.1 us -> 15.9 us  [the longest x1 9.09 us: on_device(): (xf * lax.rsqrt(jnp.mean(xf * xf, axis=-1, keepdims=True) + EPSILON) * ga...]
    sub x2 -> x0, other arithmetic: 27.8 us -> none  [forward_block(): lifted = jnp.exp(attention_scores - row_peak)]
  transfers between devices with their start and end apart: 24 -> 10, of which waited for: 20 -> 3; matrix products, arithmetic and copies ran while one was open for 23% -> 18% of each run, Pallas kernels for 0% -> 35%
where the time goes in v1:
time: 742 us; the launch traced here: 734 us
  Pallas kernels  459 us (62%)
  matrix products  135 us (18%)
  blocking collectives  45.1 us (6%)
  local copies, waits for them, and re-layouts  27.4 us (4%)
  other arithmetic  24.4 us (3%)
  waiting for transfers between devices  22.8 us (3%)
  between operations  14.8 us (2%)
    pallas_call x1, Pallas kernels, first_gather(): pl.pallas_call(functools.partial(first_kernel, n), out_shape=[jax.ShapeDt...  118 us
    pallas_call x1, Pallas kernels, last_step(): pl.pallas_call(last_kernel, out_shape=[jax.ShapeDtypeStruct((rows, width)...  83.4 us
    pallas_call x1, Pallas kernels, dz_step(): pl.pallas_call(dz_kernel, out_shape=[jax.ShapeDtypeStruct((rows, width),...  81 us
    pallas_call x1, Pallas kernels, mid_step(): pl.pallas_call(mid_kernel, out_shape=[jax.ShapeDtypeStruct((rows, width),...  80.3 us
    unnamed x1, blocking collectives  45.1 us
    pallas_call x1, Pallas kernels, gather_cot(): pl.pallas_call(gather_cot_kernel, out_shape=jax.ShapeDtypeStruct((8,) + c...  39.9 us
    pallas_call x1, Pallas kernels, run_attention_backward(): pl.pallas_call(attention_backward, grid=(seqs, pairs), out_shape=[jax.Sha...  30.1 us
    pallas_call x1, Pallas kernels, run_attention_forward(): pl.pallas_call(attention_forward, grid=(seqs, pairs), out_shape=[jax.Shap...  26.6 us
  transfers between devices with their start and end apart: 10, of which 3 were waited for; matrix products, arithmetic and copies ran while one was open for 18% of the time, Pallas kernels for 35%

profile of v1, /device:TPU:8, one launch (start us, length us, event | category | flops | bytes accessed | tf_op | source)
XLA Modules:
  0.0 733.8 jit_solution(842586265980291191)
XLA Ops:
  9.9 117.9 %first_gather.1 = (bf16[2048,768]{1,0:T(8,128)(2,1)}, bf16[256,2048]{1,0:T(8,128)(2,1)}, bf16[512,1280]{1,0:T(8,128)(2,1)}, bf16[640,512]{1,0:T(8,128)(2,1)}, bf...) custom-call(bf16[256,512]{1,0:T(8,128)(2,1)} %wq.1, bf16[256,512]{1,0:T(8,128)(2,1)} %wk.1, ...), custom_call_target="tpu_custom_call" | custom-call | tf_op jit(solution)/shard_map/first_gather/pallas_call | solution.py:420
  128.7 1.6 slice_reduce_fusion
  131.3 5.1 multiply_reduce_fusion
  138.7 9.1 %fusion.1 = bf16[2048,2048]{1,0:T(8,128)(2,1)} fusion(f32[2048]{0:T(1024)S(1)} %mul.108, f32[2048]{0:T(1024)S(1)} %bitcast.91, bf16[8,256,2048]{2,1,0:T(8,128)(2,1)} %get-tuple-element.33), kind=kLoop, calls=%fused_computation.2 | loop fusion | flops 16777216 | bytes 16793600 | tf_op jit(solution)/shard_map/convert_element_type | solution.py:750
  147.7 10.3 %convolution_convert_fusion.5.q.k.v = bf16[2048,768]{1,0:T(8,128)(2,1)S(1)} fusion(bf16[2048,2048]{1,0:T(8,128)(2,1)} %fusion.1, bf16[2048,768]{1,0:T(8,128)(2,1)} %get-tuple-element.35), kind=kOutput, calls=%fused_computation.22 | convolution fusion | flops 6444023808 | bytes 14680064 | tf_op jit(solution)/shard_map/dot_general | solution.py:751
  158.1 26.6 %attention_forward.1 = (bf16[2048,256]{1,0:T(8,128)(2,1)S(1)}, bf16[8,1024,1024]{2,1,0:T(8,128)(2,1)}) custom-call(f32[4,1,2048]{2,1,0:T(1,128)S(1)} %reshape.108.fvec, bf16[2048,768]{1,0:T(8,128)(2,1)S(1)} %convolution_convert_fusion.5.q.k.v, bf16[2048,768]{1,0:T(8,128)(2,1)S(1)} %convolution_convert_fusion.5.q.k.v, ...), custom_call_target="tpu_custom_call" | custom-call | tf_op jit(solution)/shard_map/attention_forward/pallas_call | solution.py:610
  184.7 5.6 convolution_convert_fusion.3
  190.3 80.3 %mid_step.1 = (f32[256,2048]{1,0:T(8,128)S(1)}, bf16[8,256,2048]{2,1,0:T(8,128)(2,1)S(1)}) custom-call(bf16[8,256,2048]{2,1,0:T(8,128)(2,1)} %bitcast.79, bf16[256,2048]{1,0:T(8,128)(2,1)S(1)} %bitcast.71, f32[1,2048]{1,0:T(1,128)S(1)} %reshape_squeeze.6.gain), custom_call_target="tpu_custom_call" | custom-call | tf_op jit(solution)/shard_map/mid_step/pallas_call | solution.py:468
  272.0 3.3 copy-done.8
  275.3 39.9 %gather_cot.1 = bf16[8,256,2048]{2,1,0:T(8,128)(2,1)} custom-call(bf16[256,2048]{1,0:T(8,128)(2,1)} %bitcast.73, f32[256,2048]{1,0:T(8,128)} %copy-done.2), custom_call_target="tpu_custom_call" | custom-call | tf_op jit(solution)/shard_map/gather_cot/pallas_call | solution.py:834
  315.2 18.0 %fusion.46 = f32[2048,1280]{0,1:T(8,128)} fusion(bf16[2048,2048]{1,0:T(8,128)(2,1)} %bitcast.77, bf16[2048,1280]{1,0:T(8,128)(2,1)} %all-gather.5.cloned.1.call-done), kind=kOutput, calls=%fused_computation.102 | convolution fusion | flops 10737418240 | bytes 24117248 | tf_op jit(solution)/shard_map/dot_general | solution.py:757
  333.2 17.7 %fusion.8 = (bf16[2048,640]{0,1:T(8,128)(2,1)}, bf16[2048,640]{0,1:T(8,128)(2,1)}, bf16[2048,640]{0,1:T(8,128)(2,1)}) fusion(f32[2048,1280]{0,1:T(8,128)} %fusion.46, bf16[2048,2048]{1,0:T(8,128)(2,1)} %bitcast.85, bf16[640,2048]{1,0:T(8,128)(2,1)} %all-gather.3.cloned.1.call-done), kind=kOutput, calls=%fused_computation.17 | convolution fusion | flops 5401477120 | bytes 29360128 | tf_op jit(solution)/shard_map/dot_general | solution.py:766
  350.9 16.1 %convolution_convert_fusion.2 = bf16[2048,2048]{1,0:T(8,128)(2,1)} fusion(bf16[2048,1280]{1,0:T(8,128)(2,1)S(1)} %copy-done.18, bf16[2048,640]{0,1:T(8,128)(2,1)} %get-tuple-element.60, bf16[2048,640]{0,1:T(8,128)(2,1)} %get-tuple-element.59), kind=kOutput, calls=%fused_computation.8 | convolution fusion | flops 10752098304 | bytes 18874368 | tf_op jit(solution)/shard_map/dot_general | solution.py:770
  367.0 81.0 %dz_step.1 = (f32[256,2048]{1,0:T(8,128)S(1)}, bf16[8,256,2048]{2,1,0:T(8,128)(2,1)S(1)}, f32[8,2048]{1,0:T(8,128)S(1)}) custom-call(bf16[8,256,2048]{2,1,0:T(8,128)(2,1)} %bitcast.84, f32[256,2048]{1,0:T(8,128)S(1)} %copy-done.3, bf16[256,2048]{1,0:T(8,128)(2,1)S(1)} %bitcast.74, f32[1,2048]{1,0:T(1,128)S(1)} %reshape_squeeze.6.gain), custom_call_target="tpu_custom_call" | custom-call | tf_op jit(solution)/shard_map/dz_step/pallas_call | solution.py:517
  448.0 1.4 copy-done.7
  449.4 3.3 copy-done.1
  452.6 3.3 convolution_convert_fusion.8
  456.1 10.6 %convolution_convert_fusion.7 = bf16[640,2048]{1,0:T(8,128)(2,1)} fusion(bf16[2048,640]{0,1:T(8,128)(2,1)} %get-tuple-element.61, bf16[2048,2048]{1,0:T(8,128)(2,1)} %bitcast.86), kind=kOutput, calls=%fused_computation.24 | convolution fusion | flops 5370019840 | bytes 13631488 | tf_op jit(solution)/shard_map/dot_general | solution.py:769
  466.8 6.0 convolution_convert_fusion.9.do
  472.7 30.1 %attention_backward.1 = (bf16[2048,256]{1,0:T(8,128)(2,1)S(1)}, bf16[2048,256]{1,0:T(8,128)(2,1)S(1)}, bf16[2048,256]{1,0:T(8,128)(2,1)S(1)}, f32[8,8,2048]{2,1,0:T(8,128)S(1)}) custom-call(bf16[2048,768]{1,0:T(8,128)(2,1)} %copy-done, bf16[2048,768]{1,0:T(8,128)(2,1)} %copy-done, bf16[2048,768]{1,0:T(8,128)(2,1)} %copy-done, ...), custom_call_target="tpu_custom_call" | custom-call | tf_op jit(solution)/shard_map/attention_backward/pallas_call | solution.py:677
  503.1 1.7 copy-done.12
  504.7 8.4 %convolution_convert_fusion.6 = bf16[2048,768]{1,0:T(8,128)(2,1)} fusion(bf16[2048,2048]{1,0:T(8,128)(2,1)S(1)} %bitcast.83, bf16[2048,768]{1,0:T(8,128)(2,1)S(1)} %constant_dynamic-update-slice_fusion), kind=kOutput, calls=%fused_computation.23 | convolution fusion | flops 6444023808 | bytes 14680064 | tf_op jit(solution)/shard_map/dot_general | solution.py:781
  513.2 16.4 %convolution_convert_fusion.4 = bf16[2048,1280]{1,0:T(8,128)(2,1)} fusion(bf16[2048,2048]{1,0:T(8,128)(2,1)} %bitcast.78, bf16[2048,640]{0,1:T(8,128)(2,1)} %get-tuple-element.60, bf16[2048,640]{0,1:T(8,128)(2,1)S(1)} %copy-done.20), kind=kOutput, calls=%fused_computation.10 | convolution fusion | flops 10750525440 | bytes 18874368 | tf_op jit(solution)/shard_map/dot_general | solution.py:768
  531.4 11.4 %convolution_convert_fusion = bf16[2048,2048]{1,0:T(8,128)(2,1)} fusion(bf16[2048,640]{0,1:T(8,128)(2,1)} %get-tuple-element.61, bf16[640,2048]{1,0:T(8,128)(2,1)} %all-gather.3.cloned.1.call-done), kind=kOutput, calls=%fused_computation.6 | convolution fusion | flops 5372903424 | bytes 13631488 | tf_op jit(solution)/shard_map/dot_general | solution.py:771
  542.8 9.2 %convolution_convert_fusion.1 = bf16[2048,2048]{1,0:T(8,128)(2,1)} fusion(bf16[2048,768]{1,0:T(8,128)(2,1)S(1)} %copy-done.13, bf16[2048,768]{1,0:T(8,128)(2,1)S(1)} %copy-done.19), kind=kOutput, calls=%fused_computation.7 | convolution fusion | flops 6446645248 | bytes 14680064 | tf_op jit(solution)/shard_map/dot_general | solution.py:783
  554.7 83.4 %last_step.1 = (f32[256,2048]{1,0:T(8,128)}, bf16[256,2048]{1,0:T(8,128)(2,1)S(1)}, f32[8,2048]{1,0:T(8,128)S(1)}) custom-call(bf16[8,256,2048]{2,1,0:T(8,128)(2,1)} %bitcast.81, bf16[8,256,2048]{2,1,0:T(8,128)(2,1)} %bitcast.80, bf16[256,2048]{1,0:T(8,128)(2,1)S(1)} %bitcast.72, f32[256,2048]{1,0:T(8,128)} %copy-done.7, f32[256,2048]{1,0:T(8,128)} %copy-done.2, ...), custom_call_target="tpu_custom_call" | custom-call | tf_op jit(solution)/shard_map/last_step/pallas_call | solution.py:565
  638.2 45.1 %all-reduce.4 = (f32[2048]{0:T(1024)S(1)}, f32[1024]{0:T(1024)S(1)}, f32[2048]{0:T(1024)S(1)}) all-reduce(f32[2048]{0:T(1024)S(1)} %reduce_sum.37, f32[1024]{0:T(1024)S(1)} %reshape.117, f32[2048]{0:T(1024)S(1)} %reduce_sum.39), channel_id=2, replica_groups=mesh['dp'=4,'ctx'=4,'fsdp'=2] {'dp','ctx','fsdp'}, use_global_device_ids=true, to_apply=%region_2.3.clone | all-reduce | flops 5120 | bytes 40960
  686.0 2.4 collective-permute-start.3
  689.3 6.3 collective-permute-done.3
  700.9 1.5 collective-permute-start.2
  702.4 7.6 %collective-permute-done = bf16[256,768]{1,0:T(8,128)(2,1)S(1)} collective-permute-done((bf16[256,768]{1,0:T(8,128)(2,1)S(1)}, bf16[256,768]{1,0:T(8,128)(2,1)S(1)}, u32[]{:S(2)}, u32[]{:S(2)}) %collective-permute-start) | collective-permute-done | bytes 393248 | tf_op jit(solution)/shard_map/ppermute | solution.py:711
  713.7 8.1 %collective-permute-done.2 = bf16[256,1280]{1,0:T(8,128)(2,1)S(1)} collective-permute-done((bf16[256,1280]{1,0:T(8,128)(2,1)S(1)}, bf16[256,1280]{1,0:T(8,128)(2,1)S(1)}, u32[]{:S(2)}, u32[]{:S(2)}) %collective-permute-start.2) | collective-permute-done | bytes 655392 | tf_op jit(solution)/shard_map/ppermute | solution.py:711
  (130 shorter events, 30.4 us)
Async XLA Ops:
  7.2 308.1 %all-gather.5.cloned.1.call-start = ((), (), s32[]{:S(2)}) async-start(), calls=%async_computation.5 | async-start | bytes 6553600 | tf_op jit(solution)/shard_map/all_gather | solution.py:736
  127.9 205.3 %all-gather.3.cloned.1.call-start = ((), (), s32[]{:S(2)}) async-start(), calls=%async_computation.4 | async-start | bytes 3276800 | tf_op jit(solution)/shard_map/all_gather | solution.py:737
  128.6 423.4 %reduce-scatter.7.cloned.1.call-start = ((), (), s32[]{:S(2)}) async-start(), calls=%async_computation.7 | async-start | bytes 1310720 | tf_op jit(solution)/shard_map/reduce_scatter | solution.py:778
  131.2 16.5 %copy-start.16 = (s32[2048]{0:T(1024)}, s32[2048]{0:T(1024)S(1)}, u32[]{:S(2)}) copy-start(s32[2048]{0:T(1024)S(1)} %fusion.22) | copy-start | bytes 24580
  158.1 26.7 %copy-start = (bf16[2048,768]{1,0:T(8,128)(2,1)}, bf16[2048,768]{1,0:T(8,128)(2,1)S(1)}, u32[]{:S(2)}) copy-start(bf16[2048,768]{1,0:T(8,128)(2,1)S(1)} %convolution_convert_fusion.5.q.k.v) | copy-start | bytes 9437188
  158.1 26.6 %copy-start.11 = (bf16[256,2048]{1,0:T(8,128)(2,1)S(1)}, bf16[256,2048]{1,0:T(8,128)(2,1)}, u32[]{:S(2)}) copy-start(bf16[256,2048]{1,0:T(8,128)(2,1)} %get-tuple-element.38) | copy-start | bytes 3145732
  184.7 5.6 copy-start.4
  270.7 1.3 copy-start.2
  272.0 3.3 copy-start.8
  333.2 17.7 %copy-start.18 = (bf16[2048,1280]{1,0:T(8,128)(2,1)S(1)}, bf16[2048,1280]{1,0:T(8,128)(2,1)}, u32[]{:S(2)}) copy-start(bf16[2048,1280]{1,0:T(8,128)(2,1)} %all-gather.5.cloned.1.call-done) | copy-start | bytes 15728644
  350.9 16.2 %copy-start.3 = (f32[256,2048]{1,0:T(8,128)S(1)}, f32[256,2048]{1,0:T(8,128)}, u32[]{:S(2)}) copy-start(f32[256,2048]{1,0:T(8,128)} %copy-done.2) | copy-start | bytes 6291460
  350.9 16.2 %copy-start.6 = (bf16[1,256,2048]{2,1,0:T(8,128)(2,1)S(1)}, bf16[1,256,2048]{2,1,0:T(8,128)(2,1)}, u32[]{:S(2)}) copy-start(bf16[1,256,2048]{2,1,0:T(8,128)(2,1)} %param.26) | copy-start | bytes 3145732
  448.0 1.4 copy-start.7
  449.4 3.3 copy-start.1
  456.0 229.0 %reduce-scatter.11.cloned.1.call-start = ((), (), s32[]{:S(2)}) async-start(), calls=%async_computation.9 | async-start | bytes 3276800 | tf_op jit(solution)/shard_map/reduce_scatter | solution.py:773
  466.7 230.1 %reduce-scatter.5.cloned.1.call-start = ((), (), s32[]{:S(2)}) async-start(), calls=%async_computation.6 | async-start | bytes 3932160 | tf_op jit(solution)/shard_map/reduce_scatter | solution.py:782
  466.8 38.0 %slice-start = ((s8[8388608]{0:T(1024)(128)(4,1)}), s8[4194304]{0:T(1024)(128)(4,1)S(1)}, s32[]{:S(2)}) async-start(s8[8388608]{0:T(1024)(128)(4,1)} %bitcast.82), calls=%async_computation.10 | async-start | bytes 8388608
  472.7 32.0 %slice-start.1 = ((s8[8388608]{0:T(1024)(128)(4,1)}), s8[4194304]{0:T(1024)(128)(4,1)S(1)}, s32[]{:S(2)}) async-start(s8[8388608]{0:T(1024)(128)(4,1)} %bitcast.82), calls=%async_computation.11 | async-start | bytes 8388608
  503.1 1.7 copy-start.12
  504.7 8.5 %copy-start.20 = (bf16[2048,640]{0,1:T(8,128)(2,1)S(1)}, bf16[2048,640]{0,1:T(8,128)(2,1)}, u32[]{:S(2)}) copy-start(bf16[2048,640]{0,1:T(8,128)(2,1)} %get-tuple-element.59) | copy-start | bytes 7864324
  513.2 186.4 %reduce-scatter.9.cloned.1.call-start = ((), (), s32[]{:S(2)}) async-start(), calls=%async_computation.8 | async-start | bytes 6553600 | tf_op jit(solution)/shard_map/reduce_scatter | solution.py:772
  531.4 11.4 %copy-start.13 = (bf16[2048,768]{1,0:T(8,128)(2,1)S(1)}, bf16[2048,768]{1,0:T(8,128)(2,1)}, u32[]{:S(2)}) copy-start(bf16[2048,768]{1,0:T(8,128)(2,1)} %copy-done.12) | copy-start | bytes 9437188
  531.4 11.4 %copy-start.19 = (bf16[2048,768]{1,0:T(8,128)(2,1)S(1)}, bf16[2048,768]{1,0:T(8,128)(2,1)}, u32[]{:S(2)}) copy-start(bf16[2048,768]{1,0:T(8,128)(2,1)} %get-tuple-element.35) | copy-start | bytes 9437188
  542.8 10.6 %copy-start.17 = (s32[2048]{0:T(1024)S(1)}, s32[2048]{0:T(1024)}, u32[]{:S(2)}) copy-start(s32[2048]{0:T(1024)} %copy-done.16) | copy-start | bytes 24580
  542.8 11.9 %copy-start.5 = (bf16[1,256,2048]{2,1,0:T(8,128)(2,1)S(1)}, bf16[1,256,2048]{2,1,0:T(8,128)(2,1)}, u32[]{:S(2)}) copy-start(bf16[1,256,2048]{2,1,0:T(8,128)(2,1)} %param.14) | copy-start | bytes 3145732
  553.0 135.5 %collective-permute-start.1 = (bf16[256,256]{1,0:T(8,128)(2,1)S(1)}, bf16[256,256]{1,0:T(8,128)(2,1)S(1)}, u32[]{:S(2)}, u32[]{:S(2)}) collective-permute-start(bf16[256,256]{1,0:T(8,128)(2,1)S(1)} %constant_dynamic-slice_fusion.2), channel_id=1, source_target_pairs={{0,1},{1,0},{2,3},{3,2},{4,5},{5,4},{6,7},{7,6},{8,9},{9,8},{10,11... | collective-permute-start | bytes 393224 | tf_op jit(solution)/shard_map/ppermute | solution.py:812
  554.7 133.7 %copy-start.14 = (bf16[256,512]{1,0:T(8,128)(2,1)S(1)}, bf16[256,512]{1,0:T(8,128)(2,1)}, u32[]{:S(2)}) copy-start(bf16[256,512]{1,0:T(8,128)(2,1)} %reduce-scatter.7.cloned.1.call-done) | copy-start | bytes 786436
  686.0 9.6 %collective-permute-start.3 = (bf16[640,256]{1,0:T(8,128)(2,1)S(1)}, bf16[640,256]{1,0:T(8,128)(2,1)S(1)}, u32[]{:S(2)}, u32[]{:S(2)}) collective-permute-start(bf16[640,256]{1,0:T(8,128)(2,1)S(1)} %constant_dynamic-slice_fusion), channel_id=1, source_target_pairs={{0,1},{1,0},{2,3},{3,2},{4,5},{5,4},{6,7},{7,6},{8,9},{9,8},{10,11... | collective-permute-start | bytes 983048 | tf_op jit(solution)/shard_map/ppermute | solution.py:812
  697.8 12.1 %collective-permute-start = (bf16[256,768]{1,0:T(8,128)(2,1)S(1)}, bf16[256,768]{1,0:T(8,128)(2,1)S(1)}, u32[]{:S(2)}, u32[]{:S(2)}) collective-permute-start(bf16[256,768]{1,0:T(8,128)(2,1)S(1)} %constant_dynamic-slice_fusion.3), channel_id=1, source_target_pairs={{0,1},{1,0},{2,3},{3,2},{4,5},{5,4},{6,7},{7,6},{8,9},{9,8},{10,11... | collective-permute-start | bytes 1179656 | tf_op jit(solution)/shard_map/ppermute | solution.py:711
  699.6 22.1 %copy-start.10 = (bf16[512,1280]{1,0:T(8,128)(2,1)S(1)}, bf16[512,1280]{1,0:T(8,128)(2,1)}, u32[]{:S(2)}) copy-start(bf16[512,1280]{1,0:T(8,128)(2,1)} %reduce-scatter.9.cloned.1.call-done) | copy-start | bytes 3932164
  700.9 20.9 %collective-permute-start.2 = (bf16[256,1280]{1,0:T(8,128)(2,1)S(1)}, bf16[256,1280]{1,0:T(8,128)(2,1)S(1)}, u32[]{:S(2)}, u32[]{:S(2)}) collective-permute-start(bf16[256,1280]{1,0:T(8,128)(2,1)S(1)} %constant_dynamic-slice_fusion.1), channel_id=1, source_target_pairs={{0,1},{1,0},{2,3},{3,2},{4,5},{5,4},{6,7},{7,6},{8,9},{9,8},{10,11... | collective-permute-start | bytes 1966088 | tf_op jit(solution)/shard_map/ppermute | solution.py:711
  713.7 11.7 %copy-start.9 = (f32[256,2048]{1,0:T(8,128)S(1)}, f32[256,2048]{1,0:T(8,128)}, u32[]{:S(2)}) copy-start(f32[256,2048]{1,0:T(8,128)} %get-tuple-element.50) | copy-start | bytes 6291460
  (1 other events, 0.7 us)
Sparse Core Ops, SparseCore 0:
  128.0 96.7 all-gather.4
  226.3 54.1 all-gather.2
  456.1 26.0 reduce-scatter.6
  484.5 52.0 reduce-scatter.10
  538.8 60.2 reduce-scatter.4
  601.4 95.3 reduce-scatter.8

commit v2 on v1

--- a/solution.py
+++ b/solution.py
@@ -104,11 +104,19 @@
             src, dst, dev = self.part(self.out, b, h), self.part(self.out, b, h), me.core_peer()
         return remote(src, dst, self.send.at[i], self.recv.at[i], dev)
 
-    def start(self):
-        for i in (0, 1, 2, 4, 6):
+    def start_x(self):
+        for i in (0, 4, 6):
             self.copy(i).start()
         own = block_of(self.me.x, self.me.k, self.me.y)
         pltpu.make_async_copy(self.own, self.out.at[own], self.local).start()
+
+    def start_y(self):
+        for i in (1, 2):
+            self.copy(i).start()
+
+    def start(self):
+        self.start_x()
+        self.start_y()
 
     def forward(self):
         self.copy(0).wait_recv()
@@ -137,91 +145,91 @@
 
 
 class ActReduce:
-    def __init__(self, me, part, core_in, mine, a_y, b_x, a_x, b_y, send, recv, local):
-        self.me, self.part, self.core_in, self.mine = me, part, core_in, mine
+    def __init__(self, me, peer_out, core_in, mine, a_y, b_x, a_x, b_y, send, recv):
+        self.me, self.peer_out, self.core_in, self.mine = me, peer_out, core_in, mine
         self.a_y, self.b_x, self.a_x, self.b_y = a_y, b_x, a_x, b_y
-        self.send, self.recv, self.local = send, recv, local
-        self.half = part.shape[1] // 2
+        self.send, self.recv = send, recv
+        self.half = mine.shape[1] // 2
 
     def order(self):
         x, y = self.me.x, self.me.y
         return ((1 - x, 1 - y), (x, 1 - y), (1 - x, y), (x, y))
 
     def core_copy(self, i):
-        me = self.me
         ox, oy = self.order()[i]
         return remote(
-            self.part.at[block_of(ox, 1 - me.k, oy)],
-            self.core_in.at[oy * 2 + ox],
-            self.send.at[i],
-            self.recv.at[i],
-            me.core_peer(),
+            self.peer_out.at[i], self.core_in.at[oy * 2 + ox], self.send.at[i], self.recv.at[i], self.me.core_peer()
         )
 
-    def local_copy(self, i):
+    def produce(self, i, make):
         ox, oy = self.order()[i]
-        return pltpu.make_async_copy(
-            self.part.at[block_of(ox, self.me.k, oy)], self.mine.at[oy * 2 + ox], self.local.at[i]
-        )
-
-    def start(self):
-        for i in range(4):
-            self.core_copy(i).start()
-            self.local_copy(i).start()
+        self.peer_out[i] = make(block_of(ox, 1 - self.me.k, oy))
+        self.core_copy(i).start()
+        self.mine[oy * 2 + ox] = make(block_of(ox, self.me.k, oy))
 
     def rows(self, h):
         return pl.ds(h * self.half, self.half)
 
     def add(self, slot, h, extra=None):
-        steps = self.half // 16
-
         def body(i, carry):
             r = pl.ds(pl.multiple_of(h * self.half + i * 16, 16), 16)
             total = self.mine[slot, r, :].astype(F32) + self.core_in[slot, r, :].astype(F32)
             if extra is not None:
-                total = total + extra[pl.ds(pl.multiple_of(i * 16, 16), 16), :].astype(F32)
+                total = total + self.extra(extra, i)
             self.mine[slot, r, :] = total.astype(BF)
             return carry
 
-        lax.fori_loop(0, steps, body, 0)
+        lax.fori_loop(0, self.half // 16, body, 0)
+
+    def extra(self, name, i):
+        q = pl.ds(pl.multiple_of(i * 16, 16), 16)
+        return (self.a_y if name == "a" else self.b_x)[0, q, :].astype(F32)
 
     def copies(self):
-        me = self.me
-        x, y = me.x, me.y
-        out = {}
-        out["ay0"] = remote(self.mine.at[(1 - y) * 2 + (1 - x), self.rows(0)], self.a_y.at[0], self.send.at[4], self.recv.at[4], me.y_peer())
-        out["ay1"] = remote(self.mine.at[(1 - y) * 2 + x, self.rows(0)], self.a_y.at[1], self.send.at[5], self.recv.at[5], me.y_peer())
-        out["bx0"] = remote(self.mine.at[(1 - y) * 2 + (1 - x), self.rows(1)], self.b_x.at[0], self.send.at[6], self.recv.at[6], me.x_peer())
-        out["bx1"] = remote(self.mine.at[y * 2 + (1 - x), self.rows(1)], self.b_x.at[1], self.send.at[7], self.recv.at[7], me.x_peer())
-        out["ax"] = remote(self.mine.at[y * 2 + (1 - x), self.rows(0)], self.a_x, self.send.at[8], self.recv.at[8], me.x_peer())
-        out["by"] = remote(self.mine.at[(1 - y) * 2 + x, self.rows(1)], self.b_y, self.send.at[9], self.recv.at[9], me.y_peer())
-        return out
-
-    def run(self):
         x, y = self.me.x, self.me.y
+        xp, yp = self.me.x_peer(), self.me.y_peer()
+        far, yfar, xfar = (1 - y) * 2 + (1 - x), (1 - y) * 2 + x, y * 2 + (1 - x)
+        table = {
+            "ay0": (far, 0, self.a_y.at[0], 4, yp),
+            "ay1": (yfar, 0, self.a_y.at[1], 5, yp),
+            "bx0": (far, 1, self.b_x.at[0], 6, xp),
+            "bx1": (xfar, 1, self.b_x.at[1], 7, xp),
+            "ax": (xfar, 0, self.a_x, 8, xp),
+            "by": (yfar, 1, self.b_y, 9, yp),
+        }
+        return {
+            name: remote(self.mine.at[slot, self.rows(h)], dst, self.send.at[i], self.recv.at[i], dev)
+            for name, (slot, h, dst, i, dev) in table.items()
+        }
+
+    def run(self, make, between=None):
+        x, y = self.me.x, self.me.y
+        far, yfar, xfar = (1 - y) * 2 + (1 - x), (1 - y) * 2 + x, y * 2 + (1 - x)
         c = self.copies()
+        self.produce(0, make)
+        self.produce(1, make)
         self.core_copy(0).wait_recv()
-        self.local_copy(0).wait()
-        self.add((1 - y) * 2 + (1 - x), 0)
+        self.add(far, 0)
         c["ay0"].start()
-        self.add((1 - y) * 2 + (1 - x), 1)
+        self.add(far, 1)
         c["bx0"].start()
+        self.produce(2, make)
         self.core_copy(1).wait_recv()
-        self.local_copy(1).wait()
-        self.add((1 - y) * 2 + x, 0)
+        self.add(yfar, 0)
         c["ay1"].start()
+        self.produce(3, make)
         self.core_copy(2).wait_recv()
-        self.local_copy(2).wait()
-        self.add(y * 2 + (1 - x), 1)
+        self.add(xfar, 1)
         c["bx1"].start()
         c["ay0"].wait_recv()
-        self.add(y * 2 + (1 - x), 0, self.a_y.at[0])
+        self.add(xfar, 0, "a")
         c["ax"].start()
         c["bx0"].wait_recv()
-        self.add((1 - y) * 2 + x, 1, self.b_x.at[0])
+        self.add(yfar, 1, "b")
         c["by"].start()
         self.core_copy(3).wait_recv()
-        self.local_copy(3).wait()
+        if between is not None:
+            between()
         for name in ("ay1", "bx1", "ax", "by"):
             c[name].wait_recv()
 
@@ -246,55 +254,144 @@
     return [
         pltpu.VMEM((4, rows, width), BF),
         pltpu.VMEM((4, rows, width), BF),
+        pltpu.VMEM((4, rows, width), BF),
         pltpu.VMEM((2, half, width), BF),
         pltpu.VMEM((2, half, width), BF),
         pltpu.VMEM((half, width), BF),
         pltpu.VMEM((half, width), BF),
         DMA((10,)),
         DMA((10,)),
-        DMA((4,)),
     ]
 
 
-def first_kernel(
-    n, wq, wk, wv, wo, wg, wu, wd, xin, small, seg,
-    wqkv, wof, wgu_y, wd_y, xall, smalls, segs,
-    y_send, y_recv, y_local, r_send, l_send, z_recv,
-    ag_send, ag_recv, ag_local, s_send, s_recv, s2_send, s2_recv, s_local,
+TQ = 256
+
+
+def softmax_tile(q, k, v, bias, same):
+    s = lax.dot_general(q, k, (((1,), (1,)), ((), ())), preferred_element_type=F32) + bias
+    s = jnp.where(same, s, MASKED)
+    e = jnp.exp(s - jnp.max(s, axis=-1, keepdims=True))
+    pb = (e * (1.0 / jnp.sum(e, axis=-1, keepdims=True))).astype(BF)
+    return pb, jnp.dot(pb, v, preferred_element_type=F32).astype(BF)
+
+
+class Line:
+    def __init__(self, me, n, views, send_r, send_l, recv):
+        self.me, self.n, self.views = me, n, views
+        self.send_r, self.send_l, self.recv = send_r, send_l, recv
+
+    def copies(self, t, yy, right):
+        me = self.me
+        dev = me.device(z=me.z + 1 if right else me.z - 1)
+        sem = self.send_r if right else self.send_l
+        return [
+            remote(view, view, sem.at[t, yy, i], self.recv.at[t, yy, i], dev)
+            for i, view in enumerate(self.views(t, yy))
+        ]
+
+    def send(self, t, yy, keep, start):
+        for right in (True, False):
+            go = (self.me.z + 1 <= self.n - 1) if right else (self.me.z >= 1)
+            if keep[right] is not None:
+                go = go & keep[right]
+
+            @pl.when(go)
+            def _():
+                for copy in self.copies(t, yy, right):
+                    if start:
+                        copy.start()
+                    else:
+                        copy.wait_send()
+
+    def own(self, yy):
+        self.send(self.me.z, yy, {True: None, False: None}, True)
+
+    def pump(self, s, yy):
+        z, n = self.me.z, self.n
+        for right in (True, False):
+            t = z - s if right else z + s
+            here = (z - s >= 0) if right else (z + s <= n - 1)
+            on = (z + 1 <= n - 1) if right else (z >= 1)
+
+            @pl.when(here)
+            def _():
+                for copy in self.copies(t, yy, right):
+                    copy.wait_recv()
+
+            if s < n - 1:
+
+                @pl.when(here & on)
+                def _():
+                    for copy in self.copies(t, yy, right):
+                        copy.start()
+
+    def finish(self):
+        z, n = self.me.z, self.n
+        for yy in range(2):
+            self.send(z, yy, {True: None, False: None}, False)
+            for s in range(1, n - 1):
+                for right in (True, False):
+                    t = z - s if right else z + s
+                    here = (z - s >= 0) if right else (z + s <= n - 1)
+                    on = (z + 1 <= n - 1) if right else (z >= 1)
+
+                    @pl.when(here & on)
+                    def _():
+                        for copy in self.copies(t, yy, right):
+                            copy.wait_send()
+
+
+def line_sems(n, parts):
+    return [DMA((n, 2, parts))] * 3
+
+
+def forward_kernel(
+    n, length, wq, wk, wv, wo, wg, wu, wd, cot, small, seg, xin,
+    wqkv, wof, wgu, wdf, a1, qkv, o, p, mid, a2all, gall, gain1, gain2,
+    smalls, segs, segt, xv, wqkv_v, wo_v, qkv_v, o_v, toep, pbuf, a2,
+    peer_out, mine, core_in, ra_y, rb_x, ra_x, rb_y,
+    y_send, y_recv, y_local, s_send, s_recv, s2_send, s2_recv, s_local, c_local, p_sem, red_send, red_recv,
+    *rest,
 ):
+    attn_sems, ffn_sems, x_sems, g_sems = rest[0:3], rest[3:6], rest[6:9], rest[9:12]
     me = Place()
     z, y = me.z, me.y
-    rows = wq.shape[0]
+    rows, width = xin.shape
+    piece_rows = wq.shape[0]
     heads = wq.shape[1] // 2
     hid = wg.shape[1] // 2
-    group = [me.device(x=ox, k=ok, y=oy) for ox in (me.x, 1 - me.x) for ok in (me.k, 1 - me.k) for oy in (me.y, 1 - me.y)][1:]
+    group = [
+        me.device(x=ox, k=ok, y=oy)
+        for ox in (me.x, 1 - me.x)
+        for ok in (me.k, 1 - me.k)
+        for oy in (me.y, 1 - me.y)
+    ][1:]
     others = [me.device(z=lax.rem(z + s, n)) for s in range(1, n)]
     greet(group + others)
 
-    piece = z * 2 + y
-    row = pl.ds(pl.multiple_of(piece * rows, rows), rows)
+    def piece(t, yy):
+        return pl.ds(pl.multiple_of((t * 2 + yy) * piece_rows, piece_rows), piece_rows)
+
+    row = piece(z, y)
 
     def y_copies(yh):
         col = pl.ds(pl.multiple_of(yh * heads, heads), heads)
         fcol = pl.ds(pl.multiple_of(yh * hid, hid), hid)
-        sub = pl.ds(pl.multiple_of(y * rows, rows), rows)
         return [
             (wq.at[:, col], wqkv.at[row, pl.ds(0, heads)]),
             (wk.at[:, col], wqkv.at[row, pl.ds(heads, heads)]),
             (wv.at[:, col], wqkv.at[row, pl.ds(2 * heads, heads)]),
             (wo.at[col, :], wof.at[:, row]),
-            (wg.at[:, fcol], wgu_y.at[sub, pl.ds(0, hid)]),
-            (wu.at[:, fcol], wgu_y.at[sub, pl.ds(hid, hid)]),
-            (wd.at[fcol, :], wd_y.at[:, sub]),
+            (wg.at[:, fcol], wgu.at[row, pl.ds(0, hid)]),
+            (wu.at[:, fcol], wgu.at[row, pl.ds(hid, hid)]),
+            (wd.at[fcol, :], wdf.at[:, row]),
         ]
 
     sends = [
         remote(src, dst, y_send.at[i], y_recv.at[i], me.y_peer())
         for i, (src, dst) in enumerate(y_copies(1 - y))
     ]
-    keeps = [
-        pltpu.make_async_copy(src, dst, y_local.at[i]) for i, (src, dst) in enumerate(y_copies(y))
-    ]
+    keeps = [pltpu.make_async_copy(src, dst, y_local.at[i]) for i, (src, dst) in enumerate(y_copies(y))]
     me_small = z * 8 + me.c * 2 + y
     small_local = pltpu.make_async_copy(small, smalls.at[me_small], s_local.at[0])
     seg_local = pltpu.make_async_copy(seg, segs.at[y], s_local.at[1])
@@ -302,47 +399,30 @@
         remote(small, smalls.at[me_small], s_send.at[i], s_recv.at[i], dev) for i, dev in enumerate(group)
     ]
     seg_send = remote(seg, segs.at[y], s_send.at[7], s_recv.at[7], me.y_peer())
+    attn = Line(me, n, lambda t, yy: (wqkv.at[piece(t, yy), :], wof.at[:, piece(t, yy)]), *attn_sems)
+    ffn = Line(me, n, lambda t, yy: (wgu.at[piece(t, yy), :], wdf.at[:, piece(t, yy)]), *ffn_sems)
+    xact = ActGather(me, xin, xv, *x_sems)
+    gact = ActGather(me, cot, gall, *g_sems)
+
     for i in range(4):
+        keeps[i].start()
         sends[i].start()
-        keeps[i].start()
     small_local.start()
     seg_local.start()
     for copy in small_sends:
         copy.start()
     seg_send.start()
-    act = ActGather(me, xin, xall, ag_send, ag_recv, ag_local)
-    act.start()
-    for i in range(4, 7):
-        sends[i].start()
-        keeps[i].start()
-
-    def slot_copies(t, yy, sem, right):
-        r = pl.ds(pl.multiple_of((t * 2 + yy) * rows, rows), rows)
-        dev = me.device(z=z + 1 if right else z - 1)
-        recv = z_recv.at[t, yy, 0], z_recv.at[t, yy, 1]
-        return (
-            remote(wqkv.at[r, :], wqkv.at[r, :], sem.at[t, yy, 0], recv[0], dev),
-            remote(wof.at[:, r], wof.at[:, r], sem.at[t, yy, 1], recv[1], dev),
-        )
-
-    def send_both(t, yy, do):
-        @pl.when(z + 1 <= n - 1)
-        def _():
-            for copy in slot_copies(t, yy, r_send, True):
-                do(copy)
-
-        @pl.when(z >= 1)
-        def _():
-            for copy in slot_copies(t, yy, l_send, False):
-                do(copy)
-
+    xact.start_x()
     for i in range(4):
         keeps[i].wait()
-    send_both(z, y, lambda copy: copy.start())
+    attn.own(y)
     for i in range(4):
         sends[i].wait_recv()
-    send_both(z, 1 - y, lambda copy: copy.start())
-
+    attn.own(1 - y)
+    xact.start_y()
+    for i in range(4, 7):
+        keeps[i].start()
+        sends[i].start()
     small_local.wait()
     for copy in small_sends:
         copy.wait_recv()
@@ -350,130 +430,230 @@
     small_z = [remote(block8, block8, s2_send.at[i], s2_recv.at[i], dev) for i, dev in enumerate(others)]
     for copy in small_z:
         copy.start()
-    act.forward()
-    act.forward_core()
-
-    for s in range(1, n):
-        for first in range(2):
-            yy = y if first == 0 else 1 - y
-
-            @pl.when(z - s >= 0)
-            def _():
-                for copy in slot_copies(z - s, yy, r_send, True):
-                    copy.wait_recv()
-
-                @pl.when(z + 1 <= n - 1)
-                def _():
-                    for copy in slot_copies(z - s, yy, r_send, True):
-                        copy.start()
-
-            @pl.when(z + s <= n - 1)
-            def _():
-                for copy in slot_copies(z + s, yy, l_send, False):
-                    copy.wait_recv()
-
-                @pl.when(z >= 1)
-                def _():
-                    for copy in slot_copies(z + s, yy, l_send, False):
-                        copy.start()
-
-    act.finish()
+    xact.forward()
+    attn.pump(1, y)
+    attn.pump(1, 1 - y)
+    xact.forward_core()
+
     for copy in small_z:
-        copy.wait()
+        copy.wait_recv()
+    for j in range(4 * n):
+        gain1[:, 128 * j : 128 * j + 128] = (smalls[2 * j, :, 0:128] + smalls[2 * j + 1, :, 0:128])[0:1]
+        gain2[:, 128 * j : 128 * j + 128] = (smalls[2 * j, :, 128:256] + smalls[2 * j + 1, :, 128:256])[0:1]
+    seg_local.wait()
+    seg_send.wait_recv()
+    for s in range(2):
+        wide = jnp.concatenate([segs[s]] * 16, axis=0).astype(F32)
+        segt[s] = wide.T
+    attn.pump(2, y)
+    xact.finish()
+    gact.start_x()
+    gact.start_y()
+
+    def norm_rows(i, carry):
+        r = pl.ds(pl.multiple_of(lax.rem(i, rows // 16) * 16, 16), 16)
+        b = i // (rows // 16)
+        xf = xv[b, r, :].astype(F32)
+        inv = lax.rsqrt(jnp.mean(xf * xf, axis=-1, keepdims=True) + EPSILON)
+        xv[b, r, :] = (xf * inv * gain1[...]).astype(BF)
+        return carry
+
+    lax.fori_loop(0, 8 * rows // 16, norm_rows, 0)
+    a1_out = pltpu.make_async_copy(xv, a1, c_local.at[0])
+    a1_out.start()
+    attn.pump(2, 1 - y)
+    for i in range(4, 7):
+        keeps[i].wait()
+    ffn.own(y)
+    for i in range(4, 7):
+        sends[i].wait_recv()
+    ffn.own(1 - y)
+    gact.forward()
+    for yy in (y, 1 - y):
+        for s in range(3, n):
+            attn.pump(s, yy)
+    w_in = pltpu.make_async_copy(wqkv, wqkv_v, c_local.at[1])
+    wo_in = pltpu.make_async_copy(wof, wo_v, c_local.at[2])
+    w_in.start()
+    wo_in.start()
+    w_in.wait()
+
+    def project(b, carry):
+        r = pl.ds(pl.multiple_of(b * rows, rows), rows)
+        qkv_v[r, :] = jnp.dot(xv[b], wqkv_v[...], preferred_element_type=F32).astype(BF)
+        return carry
+
+    lax.fori_loop(0, 8, project, 0)
+    qkv_out = pltpu.make_async_copy(qkv_v, qkv, c_local.at[3])
+    qkv_out.start()
+    gact.forward_core()
+
+    offset = lax.broadcasted_iota(jnp.int32, (NB, 2 * length), 1) - length
+    far = jnp.abs(offset)
+    bucket = jnp.where(far < 8, far, 8 + sum((far >= t).astype(jnp.int32) for t in THRESHOLDS))
+    bucket = bucket + 16 * (offset > 0).astype(jnp.int32)
+    own_bucket = bucket == lax.broadcasted_iota(jnp.int32, (NB, 2 * length), 0)
+    table = smalls[:, 0, 256:384]
+    lane = lax.broadcasted_iota(jnp.int32, (NB, 128), 1)
+    local_heads = heads // DH
+    tiles = length // TQ
+
+    def p_copy(slot, head, t):
+        return pltpu.make_async_copy(
+            pbuf.at[slot], p.at[head, pl.ds(t * TQ, TQ)], p_sem.at[slot]
+        )
+
+    def head_pair(hp):
+        for h in range(2):
+            head = (me.c * 2 + y) * local_heads + hp * 2 + h
+            value = jnp.sum(jnp.where(lane == head, table, 0.0), axis=1, keepdims=True)
+            fvec = jnp.sum(jnp.where(own_bucket, value, 0.0), axis=0, keepdims=True)
+            toep[h] = pltpu.roll(jnp.broadcast_to(fvec, (TQ, 2 * length)), 0, 1, stride=1, stride_axis=0)
+
+        def sequence(s, carry):
+            for h in range(2):
+                first = hp * 128
+                base = pl.multiple_of(s * length, length)
+                kh = qkv_v[pl.ds(base, length), heads + first + h * DH : heads + first + (h + 1) * DH]
+                vh = qkv_v[pl.ds(base, length), 2 * heads + first + h * DH : 2 * heads + first + (h + 1) * DH]
+                head = s * local_heads + hp * 2 + h
+                for t in range(tiles):
+                    r = pl.ds(pl.multiple_of(base + t * TQ, TQ), TQ)
+                    qt = qkv_v[r, first + h * DH : first + (h + 1) * DH]
+                    same = segt[s, t * TQ : (t + 1) * TQ, 0:1] == segs[s, 0:1, :].astype(F32)
+                    pb, ot = softmax_tile(
+                        qt, kh, vh, toep[h, :, length - t * TQ : 2 * length - t * TQ], same
+                    )
+                    slot = t % 2
+                    if hp or h or t >= 2:
+                        p_copy(slot, head, t).wait()
+                    else:
+
+                        @pl.when(s > 0)
+                        def _():
+                            p_copy(slot, head, t).wait()
+
+                    pbuf[slot] = pb
+                    p_copy(slot, head, t).start()
+                    o_v[r, first + h * DH : first + (h + 1) * DH] = ot
+            return carry
+
+        lax.fori_loop(0, 2, sequence, 0)
+
+    head_pair(0)
+    ffn.pump(1, y)
+    head_pair(1)
+    for slot in range(2):
+        p_copy(slot, 0, slot).wait()
+    o_out = pltpu.make_async_copy(o_v, o, c_local.at[4])
+    o_out.start()
+    ffn.pump(1, 1 - y)
+    wo_in.wait()
+
+    def attn_term(block):
+        r = pl.ds(pl.multiple_of(block * rows, rows), rows)
+        return jnp.dot(o_v[r, :], wo_v[...], preferred_element_type=F32).astype(BF)
+
+    red = ActReduce(me, peer_out, core_in, mine, ra_y, rb_x, ra_x, rb_y, red_send, red_recv)
+    red.run(attn_term, lambda: ffn.pump(2, y))
+
+    half = rows // 2
+    for h in range(2):
+
+        def body(i, carry):
+            rr = pl.ds(pl.multiple_of(h * half + i * 16, 16), 16)
+            m = xin[rr, :].astype(F32) + red.total(h, i)
+            mid[rr, :] = m
+            inv = lax.rsqrt(jnp.mean(m * m, axis=-1, keepdims=True) + EPSILON)
+            a2[rr, :] = (m * inv * gain2[...]).astype(BF)
+            return carry
+
+        lax.fori_loop(0, half // 16, body, 0)
+    gact.finish()
+    aact = ActGather(me, a2, a2all, *rest[12:15])
+    aact.start_x()
+    aact.start_y()
+    aact.forward()
+    ffn.pump(2, 1 - y)
+    aact.forward_core()
+    aact.finish()
+    red.finish()
+    for yy in (y, 1 - y):
+        for s in range(3, n):
+            ffn.pump(s, yy)
+    attn.finish()
+    ffn.finish()
     for copy in small_sends:
         copy.wait_send()
-    seg_send.wait()
-    seg_local.wait()
-    for i in range(7):
-        sends[i].wait_send()
-    for i in range(4, 7):
-        sends[i].wait_recv()
-        keeps[i].wait()
-    for yy in range(2):
-        send_both(z, yy, lambda copy: copy.wait_send())
-        for s in range(1, n):
-
-            @pl.when((z - s >= 0) & (z + 1 <= n - 1))
-            def _():
-                for copy in slot_copies(z - s, yy, r_send, True):
-                    copy.wait_send()
-
-            @pl.when((z + s <= n - 1) & (z >= 1))
-            def _():
-                for copy in slot_copies(z + s, yy, l_send, False):
-                    copy.wait_send()
-
-
-def first_gather(n, wq, wk, wv, wo, wg, wu, wd, xin, small, seg):
-    rows, width = wq.shape[0], xin.shape[1]
+    for copy in small_z:
+        copy.wait_send()
+    seg_send.wait_send()
+    for copy in sends:
+        copy.wait_send()
+    a1_out.wait()
+    qkv_out.wait()
+    o_out.wait()
+
+
+def forward(n, wq, wk, wv, wo, wg, wu, wd, cot, small, seg, xin):
+    rows, width = xin.shape
     heads = wq.shape[1] // 2
     hid = wg.shape[1] // 2
+    length = seg.shape[1]
+    local_heads = heads // DH
     shapes = [
-        ((2 * n * rows, 3 * heads), BF),
-        ((heads, 2 * n * rows), BF),
-        ((2 * rows, 2 * hid), BF),
-        ((hid, 2 * rows), BF),
-        ((8,) + xin.shape, BF),
-        ((8 * n,) + small.shape, F32),
-        ((2,) + seg.shape, jnp.int32),
+        ((width, 3 * heads), BF),
+        ((heads, width), BF),
+        ((width, 2 * hid), BF),
+        ((hid, width), BF),
+        ((8, rows, width), BF),
+        ((8 * rows, 3 * heads), BF),
+        ((8 * rows, heads), BF),
+        ((2 * local_heads, length, length), BF),
+        ((rows, width), F32),
+        ((8, rows, width), BF),
+        ((8, rows, width), BF),
+        ((1, width), F32),
+        ((1, width), F32),
     ]
+    half = rows // 2
+    scratch = [
+        pltpu.VMEM((8 * n,) + small.shape, F32),
+        pltpu.VMEM((2,) + seg.shape, jnp.int32),
+        pltpu.VMEM((2, length, 128), F32),
+        pltpu.VMEM((8, rows, width), BF),
+        pltpu.VMEM((width, 3 * heads), BF),
+        pltpu.VMEM((heads, width), BF),
+        pltpu.VMEM((8 * rows, 3 * heads), BF),
+        pltpu.VMEM((8 * rows, heads), BF),
+        pltpu.VMEM((2, TQ, 2 * length), F32),
+        pltpu.VMEM((2, TQ, length), BF),
+        pltpu.VMEM((rows, width), BF),
+        pltpu.VMEM((4, rows, width), BF),
+        pltpu.VMEM((4, rows, width), BF),
+        pltpu.VMEM((4, rows, width), BF),
+        pltpu.VMEM((2, half, width), BF),
+        pltpu.VMEM((2, half, width), BF),
+        pltpu.VMEM((half, width), BF),
+        pltpu.VMEM((half, width), BF),
+        DMA((7,)), DMA((7,)), DMA((7,)), DMA((8,)), DMA((8,)), DMA((n - 1,)), DMA((n - 1,)), DMA((2,)),
+        DMA((5,)), DMA((2,)), DMA((10,)), DMA((10,)),
+    ] + line_sems(n, 2) * 2 + gather_sems() * 3
     return pl.pallas_call(
-        functools.partial(first_kernel, n),
+        functools.partial(forward_kernel, n, length),
         out_shape=[jax.ShapeDtypeStruct(s, d) for s, d in shapes],
-        in_specs=[ANY] * 10,
-        out_specs=[ANY] * 7,
-        scratch_shapes=[DMA((7,)), DMA((7,)), DMA((7,)), DMA((n, 2, 2)), DMA((n, 2, 2)), DMA((n, 2, 2))]
-        + gather_sems()
-        + [DMA((8,)), DMA((8,)), DMA((n - 1,)), DMA((n - 1,)), DMA((2,))],
-        compiler_params=pltpu.CompilerParams(collective_id=0, has_side_effects=True),
-        name="first_gather",
-    )(wq, wk, wv, wo, wg, wu, wd, xin, small, seg)
+        in_specs=[ANY] * 10 + [VM],
+        out_specs=[ANY] * 8 + [VM] + [ANY] * 2 + [VM] * 2,
+        scratch_shapes=scratch,
+        compiler_params=pltpu.CompilerParams(
+            collective_id=0, has_side_effects=True, vmem_limit_bytes=60 << 20
+        ),
+        name="forward",
+    )(wq, wk, wv, wo, wg, wu, wd, cot, small, seg, xin)
 
 
 def neighbours(me):
     return [me.x_peer(), me.y_peer(), me.core_peer()]
-
-
-def mid_kernel(part, xin, gain, mid, a2all, *scratch):
-    red = scratch[:9]
-    a2, = scratch[9:10]
-    gs = scratch[10:]
-    me = Place()
-    greet(neighbours(me))
-    r = ActReduce(me, part, *red)
-    r.start()
-    r.run()
-    half = xin.shape[0] // 2
-    for h in range(2):
-
-        def body(i, carry):
-            rr = pl.ds(pl.multiple_of(h * half + i * 16, 16), 16)
-            m = xin[rr, :].astype(F32) + r.total(h, i)
-            mid[rr, :] = m
-            inv = lax.rsqrt(jnp.mean(m * m, axis=-1, keepdims=True) + EPSILON)
-            a2[rr, :] = (m * inv * gain[...]).astype(BF)
-            return carry
-
-        lax.fori_loop(0, half // 16, body, 0)
-    g = ActGather(me, a2, a2all, *gs)
-    g.start()
-    g.forward()
-    g.forward_core()
-    g.finish()
-    r.finish()
-
-
-def mid_step(part, xin, gain):
-    rows, width = xin.shape
-    return pl.pallas_call(
-        mid_kernel,
-        out_shape=[jax.ShapeDtypeStruct((rows, width), F32), jax.ShapeDtypeStruct((8, rows, width), BF)],
-        in_specs=[ANY, VM, VM],
-        out_specs=[VM, ANY],
-        scratch_shapes=reduce_scratch(rows, width) + [pltpu.VMEM((rows, width), BF)] + gather_sems(),
-        compiler_params=pltpu.CompilerParams(collective_id=1, has_side_effects=True, vmem_limit_bytes=40 << 20),
-        name="mid_step",
-    )(part, xin, gain)
 
 
 def dz_kernel(part, mid, cot, gain, gmid, dzall, ggain, *scratch):
@@ -482,9 +662,8 @@
     gs = scratch[10:]
     me = Place()
     greet(neighbours(me))
-    r = ActReduce(me, part, *red)
-    r.start()
-    r.run()
+    r = ActReduce(me, *red)
+    r.run(lambda b: part[b])
     half = mid.shape[0] // 2
     ggain[...] = jnp.zeros_like(ggain)
     for h in range(2):
@@ -521,10 +700,10 @@
             jax.ShapeDtypeStruct((8, rows, width), BF),
             jax.ShapeDtypeStruct((8, width), F32),
         ],
-        in_specs=[ANY, VM, VM, VM],
+        in_specs=[VM, VM, VM, VM],
         out_specs=[VM, ANY, VM],
         scratch_shapes=reduce_scratch(rows, width) + [pltpu.VMEM((rows, width), BF)] + gather_sems(),
-        compiler_params=pltpu.CompilerParams(collective_id=2, has_side_effects=True, vmem_limit_bytes=40 << 20),
+        compiler_params=pltpu.CompilerParams(collective_id=2, has_side_effects=True, vmem_limit_bytes=60 << 20),
         name="dz_step",
     )(part, mid, cot, gain)
 
@@ -532,12 +711,10 @@
 def last_kernel(ga_part, out_part, xin, gmid, mid, gain, gx, out, ggain, *scratch):
     me = Place()
     greet(neighbours(me))
-    r = ActReduce(me, ga_part, *scratch[:9])
-    q = ActReduce(me, out_part, *scratch[9:18])
-    r.start()
-    q.start()
-    r.run()
-    q.run()
+    r = ActReduce(me, *scratch[:9])
+    q = ActReduce(me, *scratch[9:18])
+    r.run(lambda b: ga_part[b])
+    q.run(lambda b: out_part[b])
     half = xin.shape[0] // 2
     ggain[...] = jnp.zeros_like(ggain)
     for h in range(2):
@@ -569,67 +746,12 @@
             jax.ShapeDtypeStruct((rows, width), BF),
             jax.ShapeDtypeStruct((8, width), F32),
         ],
-        in_specs=[ANY, ANY, VM, VM, VM, VM],
+        in_specs=[VM, VM, VM, VM, VM, VM],
         out_specs=[VM, VM, VM],
         scratch_shapes=reduce_scratch(rows, width) * 2,
-        compiler_params=pltpu.CompilerParams(collective_id=3, has_side_effects=True, vmem_limit_bytes=50 << 20),
+        compiler_params=pltpu.CompilerParams(collective_id=3, has_side_effects=True, vmem_limit_bytes=62 << 20),
         name="last_step",
     )(ga_part, out_part, xin, gmid, mid, gain)
-
-
-TQ = 256
-
-
-def attention_forward(fvec, q, k, v, segr, segc, o, p, toep):
-    length = q.shape[0]
-    for h in range(2):
-        cols = slice(h * DH, (h + 1) * DH)
-        toep[...] = pltpu.roll(
-            jnp.broadcast_to(fvec[h], toep.shape), 0, 1, stride=1, stride_axis=0
-        )
-        kh = k[:, cols]
-        vh = v[:, cols]
-        for t in range(length // TQ):
-            rows = slice(t * TQ, (t + 1) * TQ)
-            s = lax.dot_general(q[rows, cols], kh, (((1,), (1,)), ((), ())), preferred_element_type=F32)
-            s = s + toep[:, length - t * TQ : 2 * length - t * TQ]
-            s = jnp.where(segc[0, rows, :] == segr[0], s, MASKED)
-            e = jnp.exp(s - jnp.max(s, axis=-1, keepdims=True))
-            pb = (e * (1.0 / jnp.sum(e, axis=-1, keepdims=True))).astype(BF)
-            p[h, rows, :] = pb
-            o[rows, cols] = jnp.dot(pb, vh, preferred_element_type=F32).astype(BF)
-
-
-def run_attention_forward(fvec, qkv, segr, segc):
-    total, width = qkv.shape
-    heads = width // 3 // DH
-    length = segr.shape[-1]
-    seqs = total // length
-    pairs = heads // 2
-    qspec = lambda off: pl.BlockSpec((length, 2 * DH), lambda s, h: (s, off * pairs + h))
-    return pl.pallas_call(
-        attention_forward,
-        grid=(seqs, pairs),
-        out_shape=[
-            jax.ShapeDtypeStruct((total, heads * DH), BF),
-            jax.ShapeDtypeStruct((seqs * heads, length, length), BF),
-        ],
-        in_specs=[
-            pl.BlockSpec((2, 1, 2 * length), lambda s, h: (h, 0, 0)),
-            qspec(0),
-            qspec(1),
-            qspec(2),
-            pl.BlockSpec((1, 1, length), lambda s, h: (s, 0, 0)),
-            pl.BlockSpec((1, length, 1), lambda s, h: (s, 0, 0)),
-        ],
-        out_specs=[
-            pl.BlockSpec((length, 2 * DH), lambda s, h: (s, h)),
-            pl.BlockSpec((2, length, length), lambda s, h: (s * pairs + h, 0, 0)),
-        ],
-        scratch_shapes=[pltpu.VMEM((TQ, 2 * length), F32)],
-        compiler_params=pltpu.CompilerParams(vmem_limit_bytes=48 << 20),
-        name="attention_forward",
-    )(fvec, qkv, qkv, qkv, segr, segc)
 
 
 def attention_backward(q, k, v, do, p, dq, dk, dv, diag, acc, dkt, dvt):
@@ -725,35 +847,18 @@
     y = lax.axis_index("fsdp")
     c = lax.axis_index("ctx")
     swap = [(0, 1), (1, 0)]
-    share = attn_gain.shape[0]
-    packed = jnp.concatenate([attn_gain.astype(F32), ffn_gain.astype(F32), rel_table.astype(F32)])
-    packed = jnp.pad(packed, (0, 256 - packed.shape[0]))
-    small = jnp.broadcast_to(packed[None, :], (8, 256))
+    lanes = lambda v: jnp.where(y == 0, jnp.pad(v, (0, 64)), jnp.pad(v, (64, 0))).astype(F32)
+    packed = jnp.concatenate([lanes(attn_gain), lanes(ffn_gain), jnp.pad(rel_table.astype(F32), (0, 96))])
+    small = jnp.broadcast_to(packed[None, :], (8, packed.shape[0]))
     seg = jnp.broadcast_to(segment_ids, (8, length))
-    wqkv, wo, wgu_y, wd_y, xall, smalls, segs = first_gather(
-        n, w_query, w_key, w_value, w_attn_out, w_gate, w_up, w_down, xin, small, seg
-    )
-    wgu = lax.all_gather(wgu_y, "dp", axis=0, tiled=True)
-    wd = lax.all_gather(wd_y, "dp", axis=1, tiled=True)
-    gain1 = smalls[:, 0, 0:share].reshape(1, width)
-    gain2 = smalls[:, 0, share : 2 * share].reshape(1, width)
-    table = smalls[:, 0, 2 * share : 2 * share + NB * H // (8 * n)].reshape(NB, H)
+    wqkv, wo, wgu, wd, a1, qkv, o, p, mid, a2all, gall, gain1, gain2 = forward(
+        n, w_query, w_key, w_value, w_attn_out, w_gate, w_up, w_down, cot, small, seg, xin
+    )
     local_heads = heads // DH
-    table_local = lax.dynamic_slice_in_dim(table, (c * 2 + y) * local_heads, local_heads, 1)
     one_hot = offset_buckets(length)
-    fvec = lax.dot_general(
-        table_local, one_hot, (((0,), (1,)), ((), ())), precision=lax.Precision.HIGHEST
-    ).reshape(local_heads, 1, 2 * length)
-    segr = segs[:, 0:1, :]
-    segc = segs[:, 0, :, None]
-    xf = xall.reshape(8 * rows, width).astype(F32)
-    a1 = (xf * lax.rsqrt(jnp.mean(xf * xf, axis=-1, keepdims=True) + EPSILON) * gain1).astype(BF)
-    qkv = jnp.dot(a1, wqkv, preferred_element_type=F32).astype(BF)
-    o, p = run_attention_forward(fvec, qkv, segr, segc)
-    attn_part = jnp.dot(o, wo, preferred_element_type=F32).astype(BF)
-    mid, a2all = mid_step(attn_part.reshape(8, rows, width), xin, gain2)
+    a1 = a1.reshape(8 * rows, width)
     a2 = a2all.reshape(8 * rows, width)
-    gall = gather_cot(cot, mid).reshape(8 * rows, width)
+    gall = gall.reshape(8 * rows, width)
     gate_up = jnp.dot(a2, wgu, preferred_element_type=F32)
     gate, up = gate_up[:, :hid], gate_up[:, hid:]
     inner = 0.7978845608028654 * (gate + 0.044715 * gate * gate * gate)
@@ -786,9 +891,9 @@
     )
 
     d8 = jnp.sum(diag.reshape(-1, local_heads, 8, 2 * length), axis=0)
-    lanes = sum(jnp.roll(d8[:, r, :], -r, axis=-1) for r in range(8))
+    shifted = sum(jnp.roll(d8[:, r, :], -r, axis=-1) for r in range(8))
     bias = lax.dot_general(
-        one_hot, lanes, (((0,), (1,)), ((), ())), precision=lax.Precision.HIGHEST
+        one_hot, shifted, (((0,), (1,)), ((), ())), precision=lax.Precision.HIGHEST
     )
     table_term = lax.dynamic_update_slice(
         jnp.zeros((NB, H), F32), bias, (jnp.int32(0), (c * 2 + y) * local_heads)
@@ -818,28 +923,6 @@
         out[None], gx[None], g_attn_gain, g_q, g_k, g_v, swap_cols(rs_o), g_table, g_ffn_gain,
         g_gate, g_up, swap_cols(rs_d),
     )
-
-
-def gather_cot_kernel(cot, after, gall, send, recv, local):
-    me = Place()
-    greet(neighbours(me))
-    g = ActGather(me, cot, gall, send, recv, local)
-    g.start()
-    g.forward()
-    g.forward_core()
-    g.finish()
-
-
-def gather_cot(cot, after):
-    return pl.pallas_call(
-        gather_cot_kernel,
-        out_shape=jax.ShapeDtypeStruct((8,) + cot.shape, BF),
-        in_specs=[ANY, ANY],
-        out_specs=ANY,
-        scratch_shapes=gather_sems(),
-        compiler_params=pltpu.CompilerParams(collective_id=4, has_side_effects=True),
-        name="gather_cot",
-    )(cot, after)
 
 
 QB = 512

time: 742 us -> 687 us (0.926)
  matrix products: 135 us -> 120 us
  Pallas kernels: 459 us -> 444 us
  local copies, waits for them, and re-layouts: 27.4 us -> 13.3 us
  other arithmetic: 24.4 us -> 11.8 us
    pallas_call x4 -> x1, Pallas kernels: 265 us -> 238 us  [forward(): pl.pallas_call(functools.partial(forward_kernel, n, length), out_shape=[j...]
    dot_general x4 -> x1, matrix products: 17.7 us -> 1.02 us  [on_device(): lax.dot_general(one_hot, shifted, (((0,), (1,)), ((), ())), precision=lax...]
    unnamed x55 -> x36, local copies, waits for them, and re-layouts: 15.9 us -> 5.94 us
    convert_element_type x1 -> x0, other arithmetic: 9.09 us -> none  [on_device(): (xf * lax.rsqrt(jnp.mean(xf * xf, axis=-1, keepdims=True) + EPSILON) * ga...]
  transfers between devices with their start and end apart: 10 -> 8, of which waited for: 3 -> 3; matrix products, arithmetic and copies ran while one was open for 18% -> 12% of each run, Pallas kernels for 35% -> 18%
where the time goes in v2:
time: 687 us; the launch traced here: 680 us
  Pallas kernels  444 us (65%)
  matrix products  120 us (17%)
  blocking collectives  47.4 us (7%)
  waiting for transfers between devices  23.5 us (3%)
  between operations  14.6 us (2%)
  local copies, waits for them, and re-layouts  13.3 us (2%)
  other arithmetic  11.8 us (2%)
    pallas_call x1, Pallas kernels, forward(): pl.pallas_call(functools.partial(forward_kernel, n, length), out_shape=[j...  238 us
    pallas_call x1, Pallas kernels, last_step(): pl.pallas_call(last_kernel, out_shape=[jax.ShapeDtypeStruct((rows, width)...  90.6 us
    pallas_call x1, Pallas kernels, dz_step(): pl.pallas_call(dz_kernel, out_shape=[jax.ShapeDtypeStruct((rows, width),...  86.6 us
    unnamed x1, blocking collectives  47.4 us
    pallas_call x1, Pallas kernels, run_attention_backward(): pl.pallas_call(attention_backward, grid=(seqs, pairs), out_shape=[jax.Sha...  29.7 us
    dot_general x1, matrix products, on_device(): gate_up = jnp.dot(a2, wgu, preferred_element_type=F32)  17.8 us
    dot_general x1, matrix products, on_device(): lax.dot_general(dgu, wgu, (((1,), (1,)), ((), ())), preferred_element_typ...  17.1 us
    ppermute x2, waiting for transfers between devices, swap_rows(): lax.ppermute(lax.dynamic_slice_in_dim(part, (1 - y) * rows, rows, 0), 'fs...  16.9 us
  transfers between devices with their start and end apart: 8, of which 3 were waited for; matrix products, arithmetic and copies ran while one was open for 12% of the time, Pallas kernels for 18%

profile of v2, /device:TPU:8, one launch (start us, length us, event | category | flops | bytes accessed | tf_op | source)
XLA Modules:
  0.0 679.9 jit_solution(11431249951133693597)
XLA Ops:
  9.3 1.3 broadcast_in_dim.26.seg
  10.6 237.5 %forward.1 = (bf16[2048,768]{1,0:T(8,128)(2,1)}, bf16[256,2048]{1,0:T(8,128)(2,1)}, bf16[2048,1280]{1,0:T(8,128)(2,1)}, bf16[640,2048]{1,0:T(8,128)(2,1)}, bf16[...) custom-call(bf16[256,512]{1,0:T(8,128)(2,1)} %wq.1, ...), custom_call_target="tpu_custom_call" | custom-call | tf_op jit(solution)/shard_map/forward/pallas_call | solution.py:642
  248.1 17.8 %fusion.39 = f32[2048,1280]{0,1:T(8,128)} fusion(bf16[2048,2048]{1,0:T(8,128)(2,1)} %bitcast.84, bf16[2048,1280]{1,0:T(8,128)(2,1)} %get-tuple-element.39), kind=kOutput, calls=%fused_computation.88 | convolution fusion | flops 10737418240 | bytes 24117248 | tf_op jit(solution)/shard_map/dot_general | solution.py:862
  265.9 13.7 %fusion.6 = (bf16[2048,640]{0,1:T(8,128)(2,1)}, bf16[2048,640]{0,1:T(8,128)(2,1)}, bf16[2048,640]{0,1:T(8,128)(2,1)}) fusion(f32[2048,1280]{0,1:T(8,128)} %fusion.39, bf16[2048,2048]{1,0:T(8,128)(2,1)S(1)} %bitcast.88, bf16[640,2048]{1,0:T(8,128)(2,1)S(1)} %copy-done.10), kind=kOutput, calls=%fused_computation.12 | convolution fusion | flops 5401477120 | bytes 29360128 | tf_op jit(solution)/shard_map/dot_general | solution.py:871
  279.6 17.1 %convolution_convert_fusion.2 = bf16[2048,2048]{1,0:T(8,128)(2,1)} fusion(bf16[2048,1280]{1,0:T(8,128)(2,1)} %get-tuple-element.39, bf16[2048,640]{0,1:T(8,128)(2,1)} %get-tuple-element.62, bf16[2048,640]{0,1:T(8,128)(2,1)} %get-tuple-element.61), kind=kOutput, calls=%fused_computation.4 | convolution fusion | flops 10752098304 | bytes 18874368 | tf_op jit(solution)/shard_map/dot_general | solution.py:875
  296.7 86.6 %dz_step.1 = (f32[256,2048]{1,0:T(8,128)}, bf16[8,256,2048]{2,1,0:T(8,128)(2,1)}, f32[8,2048]{1,0:T(8,128)}) custom-call(bf16[8,256,2048]{2,1,0:T(8,128)(2,1)} %bitcast.62, f32[256,2048]{1,0:T(8,128)} %get-tuple-element.40.mid, bf16[256,2048]{1,0:T(8,128)(2,1)} %bitcast.64, f32[1,2048]{1,0:T(1,128)} %get-tuple-element.41.gain), custom_call_target="tpu_custom_call" | custom-call | tf_op jit(solution)/shard_map/dz_step/pallas_call | solution.py:696
  383.4 6.7 convolution_convert_fusion.6
  390.1 10.6 %convolution_convert_fusion.5 = bf16[640,2048]{1,0:T(8,128)(2,1)} fusion(bf16[2048,640]{0,1:T(8,128)(2,1)} %get-tuple-element.63, bf16[2048,2048]{1,0:T(8,128)(2,1)} %bitcast.87), kind=kOutput, calls=%fused_computation.18 | convolution fusion | flops 5370019840 | bytes 13631488 | tf_op jit(solution)/shard_map/dot_general | solution.py:874
  401.0 6.0 convolution_convert_fusion.7.do
  407.1 29.7 %attention_backward.1 = (bf16[2048,256]{1,0:T(8,128)(2,1)S(1)}, bf16[2048,256]{1,0:T(8,128)(2,1)S(1)}, bf16[2048,256]{1,0:T(8,128)(2,1)S(1)}, f32[8,8,2048]{2,1,0:T(8,128)S(1)}) custom-call(bf16[2048,768]{1,0:T(8,128)(2,1)} %get-tuple-element.35.q.k.v, bf16[2048,768]{1,0:T(8,128)(2,1)} %get-tuple-element.35.q.k.v, ...), custom_call_target="tpu_custom_call" | custom-call | tf_op jit(solution)/shard_map/attention_backward/pallas_call | solution.py:799
  437.1 1.6 copy-done.4
  438.7 10.4 %convolution_convert_fusion.4 = bf16[2048,768]{1,0:T(8,128)(2,1)} fusion(bf16[2048,2048]{1,0:T(8,128)(2,1)} %bitcast.86, bf16[2048,768]{1,0:T(8,128)(2,1)S(1)} %constant_dynamic-update-slice_fusion), kind=kOutput, calls=%fused_computation.17 | convolution fusion | flops 6444023808 | bytes 14680064 | tf_op jit(solution)/shard_map/dot_general | solution.py:886
  449.4 16.6 %convolution_convert_fusion.3 = bf16[2048,1280]{1,0:T(8,128)(2,1)} fusion(bf16[2048,2048]{1,0:T(8,128)(2,1)} %bitcast.85, bf16[2048,640]{0,1:T(8,128)(2,1)} %get-tuple-element.62, bf16[2048,640]{0,1:T(8,128)(2,1)} %get-tuple-element.61), kind=kOutput, calls=%fused_computation.5 | convolution fusion | flops 10750525440 | bytes 18874368 | tf_op jit(solution)/shard_map/dot_general | solution.py:873
  467.1 10.9 %convolution_convert_fusion = bf16[2048,2048]{1,0:T(8,128)(2,1)} fusion(bf16[2048,640]{0,1:T(8,128)(2,1)} %get-tuple-element.63, bf16[640,2048]{1,0:T(8,128)(2,1)S(1)} %copy-done.10), kind=kOutput, calls=%fused_computation.2 | convolution fusion | flops 5372903424 | bytes 13631488 | tf_op jit(solution)/shard_map/dot_general | solution.py:876
  477.9 9.3 %convolution_convert_fusion.1 = bf16[2048,2048]{1,0:T(8,128)(2,1)} fusion(bf16[2048,768]{1,0:T(8,128)(2,1)S(1)} %copy-done.5, bf16[2048,768]{1,0:T(8,128)(2,1)S(1)} %copy-done.9), kind=kOutput, calls=%fused_computation.3 | convolution fusion | flops 6446645248 | bytes 14680064 | tf_op jit(solution)/shard_map/dot_general | solution.py:888
  488.2 1.0 collective-permute-start.1
  489.2 1.0 fusion.8
  490.5 90.6 %last_step.1 = (f32[256,2048]{1,0:T(8,128)}, bf16[256,2048]{1,0:T(8,128)(2,1)}, f32[8,2048]{1,0:T(8,128)}) custom-call(bf16[8,256,2048]{2,1,0:T(8,128)(2,1)} %bitcast.61, bf16[8,256,2048]{2,1,0:T(8,128)(2,1)} %bitcast.60, bf16[256,2048]{1,0:T(8,128)(2,1)} %bitcast.66, f32[256,2048]{1,0:T(8,128)} %get-tuple-element.49.gmid, ...), custom_call_target="tpu_custom_call" | custom-call | tf_op jit(solution)/shard_map/last_step/pallas_call | solution.py:742
  582.0 47.4 %all-reduce.8 = (f32[2048]{0:T(1024)S(1)}, f32[1024]{0:T(1024)S(1)}, f32[2048]{0:T(1024)S(1)}) all-reduce(f32[2048]{0:T(1024)S(1)} %reduce_sum.27, f32[1024]{0:T(1024)S(1)} %reshape.91, f32[2048]{0:T(1024)S(1)} %reduce_sum.29), channel_id=2, replica_groups=mesh['dp'=4,'ctx'=4,'fsdp'=2] {'dp','ctx','fsdp'}, use_global_device_ids=true, to_apply=%region_1.2.clone | all-reduce | flops 5120 | bytes 40960
  631.1 1.0 constant_dynamic-slice_fusion
  632.1 2.4 collective-permute-start.3
  635.4 1.0 constant_dynamic-slice_fusion.3
  636.5 6.6 collective-permute-done.3
  643.1 1.1 broadcast_select_fusion.5
  644.2 1.2 maximum_convert_fusion.2
  645.3 4.8 collective-permute-done
  650.1 1.1 broadcast_select_fusion.3
  651.3 1.2 constant_dynamic-slice_fusion.1
  655.8 12.1 %collective-permute-done.2 = bf16[256,1280]{1,0:T(8,128)(2,1)S(1)} collective-permute-done((bf16[256,1280]{1,0:T(8,128)(2,1)S(1)}, bf16[256,1280]{1,0:T(8,128)(2,1)S(1)}, u32[]{:S(2)}, u32[]{:S(2)}) %collective-permute-start.2) | collective-permute-done | bytes 655392 | tf_op jit(solution)/shard_map/ppermute | solution.py:833
  668.3 1.1 maximum_convert_fusion.1
  669.4 1.1 maximum_convert_fusion
  671.6 1.3 copy.81
  (86 shorter events, 13.4 us)
Async XLA Ops:
  7.2 480.1 %reduce-scatter.7.cloned.1.call-start = ((), (), s32[]{:S(2)}) async-start(), calls=%async_computation.5 | async-start | bytes 1310720 | tf_op jit(solution)/shard_map/reduce_scatter | solution.py:883
  248.1 17.8 %copy-start.8 = (bf16[8,256,2048]{2,1,0:T(8,128)(2,1)S(1)}, bf16[8,256,2048]{2,1,0:T(8,128)(2,1)}, u32[]{:S(2)}) copy-start(bf16[8,256,2048]{2,1,0:T(8,128)(2,1)} %get-tuple-element.36) | copy-start | bytes 25165828
  248.1 17.8 %copy-start.10 = (bf16[640,2048]{1,0:T(8,128)(2,1)S(1)}, bf16[640,2048]{1,0:T(8,128)(2,1)}, u32[]{:S(2)}) copy-start(bf16[640,2048]{1,0:T(8,128)(2,1)} %get-tuple-element.37) | copy-start | bytes 7864324
  296.7 86.6 %copy-start = (bf16[2048,256]{1,0:T(8,128)(2,1)S(1)}, bf16[2048,256]{1,0:T(8,128)(2,1)}, u32[]{:S(2)}) copy-start(bf16[2048,256]{1,0:T(8,128)(2,1)} %get-tuple-element.55) | copy-start | bytes 3145732
  390.1 241.0 %reduce-scatter.11.cloned.1.call-start = ((), (), s32[]{:S(2)}) async-start(), calls=%async_computation.7 | async-start | bytes 3276800 | tf_op jit(solution)/shard_map/reduce_scatter | solution.py:878
  400.8 234.6 %reduce-scatter.5.cloned.1.call-start = ((), (), s32[]{:S(2)}) async-start(), calls=%async_computation.4 | async-start | bytes 3932160 | tf_op jit(solution)/shard_map/reduce_scatter | solution.py:887
  437.1 1.6 copy-start.4
  449.1 202.1 %reduce-scatter.9.cloned.1.call-start = ((), (), s32[]{:S(2)}) async-start(), calls=%async_computation.6 | async-start | bytes 6553600 | tf_op jit(solution)/shard_map/reduce_scatter | solution.py:877
  467.0 10.9 %copy-start.5 = (bf16[2048,768]{1,0:T(8,128)(2,1)S(1)}, bf16[2048,768]{1,0:T(8,128)(2,1)}, u32[]{:S(2)}) copy-start(bf16[2048,768]{1,0:T(8,128)(2,1)} %copy-done.4) | copy-start | bytes 9437188
  467.0 10.9 %copy-start.9 = (bf16[2048,768]{1,0:T(8,128)(2,1)S(1)}, bf16[2048,768]{1,0:T(8,128)(2,1)}, u32[]{:S(2)}) copy-start(bf16[2048,768]{1,0:T(8,128)(2,1)} %get-tuple-element.48) | copy-start | bytes 9437188
  488.2 146.3 %collective-permute-start.1 = (bf16[256,256]{1,0:T(8,128)(2,1)S(1)}, bf16[256,256]{1,0:T(8,128)(2,1)S(1)}, u32[]{:S(2)}, u32[]{:S(2)}) collective-permute-start(bf16[256,256]{1,0:T(8,128)(2,1)S(1)} %constant_dynamic-slice_fusion.2), channel_id=1, source_target_pairs={{0,1},{1,0},{2,3},{3,2},{4,5},{5,4},{6,7},{7,6},{8,9},{9,8},{10,11... | collective-permute-start | bytes 393224 | tf_op jit(solution)/shard_map/ppermute | solution.py:917
  490.5 91.4 %copy-start.7 = (f32[8,2048]{1,0:T(8,128)S(1)}, f32[8,2048]{1,0:T(8,128)}, u32[]{:S(2)}) copy-start(f32[8,2048]{1,0:T(8,128)} %get-tuple-element.57) | copy-start | bytes 196612
  490.5 144.0 %copy-start.6 = (bf16[256,512]{1,0:T(8,128)(2,1)S(1)}, bf16[256,512]{1,0:T(8,128)(2,1)}, u32[]{:S(2)}) copy-start(bf16[256,512]{1,0:T(8,128)(2,1)} %reduce-scatter.7.cloned.1.call-done) | copy-start | bytes 786436
  632.1 11.0 %collective-permute-start.3 = (bf16[640,256]{1,0:T(8,128)(2,1)S(1)}, bf16[640,256]{1,0:T(8,128)(2,1)S(1)}, u32[]{:S(2)}, u32[]{:S(2)}) collective-permute-start(bf16[640,256]{1,0:T(8,128)(2,1)S(1)} %constant_dynamic-slice_fusion), channel_id=1, source_target_pairs={{0,1},{1,0},{2,3},{3,2},{4,5},{5,4},{6,7},{7,6},{8,9},{9,8},{10,11... | collective-permute-start | bytes 983048 | tf_op jit(solution)/shard_map/ppermute | solution.py:917
  636.4 13.7 %collective-permute-start = (bf16[256,768]{1,0:T(8,128)(2,1)S(1)}, bf16[256,768]{1,0:T(8,128)(2,1)S(1)}, u32[]{:S(2)}, u32[]{:S(2)}) collective-permute-start(bf16[256,768]{1,0:T(8,128)(2,1)S(1)} %constant_dynamic-slice_fusion.3), channel_id=1, source_target_pairs={{0,1},{1,0},{2,3},{3,2},{4,5},{5,4},{6,7},{7,6},{8,9},{9,8},{10,11... | collective-permute-start | bytes 1179656 | tf_op jit(solution)/shard_map/ppermute | solution.py:833
  651.2 16.7 %copy-start.2 = (bf16[512,1280]{1,0:T(8,128)(2,1)S(1)}, bf16[512,1280]{1,0:T(8,128)(2,1)}, u32[]{:S(2)}) copy-start(bf16[512,1280]{1,0:T(8,128)(2,1)} %reduce-scatter.9.cloned.1.call-done) | copy-start | bytes 3932164
  652.5 15.4 %collective-permute-start.2 = (bf16[256,1280]{1,0:T(8,128)(2,1)S(1)}, bf16[256,1280]{1,0:T(8,128)(2,1)S(1)}, u32[]{:S(2)}, u32[]{:S(2)}) collective-permute-start(bf16[256,1280]{1,0:T(8,128)(2,1)S(1)} %constant_dynamic-slice_fusion.1), channel_id=1, source_target_pairs={{0,1},{1,0},{2,3},{3,2},{4,5},{5,4},{6,7},{7,6},{8,9},{9,8},{10,11... | collective-permute-start | bytes 1966088 | tf_op jit(solution)/shard_map/ppermute | solution.py:833
  654.1 16.5 %copy-start.3 = (bf16[256,2048]{1,0:T(8,128)(2,1)S(1)}, bf16[256,2048]{1,0:T(8,128)(2,1)}, u32[]{:S(2)}) copy-start(bf16[256,2048]{1,0:T(8,128)(2,1)} %get-tuple-element.51) | copy-start | bytes 3145732
  655.8 15.8 %copy-start.1 = (f32[256,2048]{1,0:T(8,128)S(1)}, f32[256,2048]{1,0:T(8,128)}, u32[]{:S(2)}) copy-start(f32[256,2048]{1,0:T(8,128)} %get-tuple-element.52) | copy-start | bytes 6291460
Sparse Core Ops, SparseCore 0:
  390.2 25.6 reduce-scatter.6
  418.3 51.9 reduce-scatter.10
  472.7 60.2 reduce-scatter.4
  535.3 95.3 reduce-scatter.8

commit v3 on v2

--- a/solution.py
+++ b/solution.py
@@ -151,21 +151,14 @@
         self.send, self.recv = send, recv
         self.half = mine.shape[1] // 2
 
-    def order(self):
+    def place(self, j):
         x, y = self.me.x, self.me.y
-        return ((1 - x, 1 - y), (x, 1 - y), (1 - x, y), (x, y))
-
-    def core_copy(self, i):
-        ox, oy = self.order()[i]
+        return jnp.where(j % 2 == 0, 1 - x, x), jnp.where(j < 2, 1 - y, y)
+
+    def core_copy(self, j):
         return remote(
-            self.peer_out.at[i], self.core_in.at[oy * 2 + ox], self.send.at[i], self.recv.at[i], self.me.core_peer()
+            self.peer_out.at[j % 2], self.core_in.at[j], self.send.at[j], self.recv.at[j], self.me.core_peer()
         )
-
-    def produce(self, i, make):
-        ox, oy = self.order()[i]
-        self.peer_out[i] = make(block_of(ox, 1 - self.me.k, oy))
-        self.core_copy(i).start()
-        self.mine[oy * 2 + ox] = make(block_of(ox, self.me.k, oy))
 
     def rows(self, h):
         return pl.ds(h * self.half, self.half)
@@ -175,84 +168,91 @@
             r = pl.ds(pl.multiple_of(h * self.half + i * 16, 16), 16)
             total = self.mine[slot, r, :].astype(F32) + self.core_in[slot, r, :].astype(F32)
             if extra is not None:
-                total = total + self.extra(extra, i)
+                q = pl.ds(pl.multiple_of(i * 16, 16), 16)
+                total = total + extra[0, q, :].astype(F32)
             self.mine[slot, r, :] = total.astype(BF)
             return carry
 
         lax.fori_loop(0, self.half // 16, body, 0)
 
-    def extra(self, name, i):
-        q = pl.ds(pl.multiple_of(i * 16, 16), 16)
-        return (self.a_y if name == "a" else self.b_x)[0, q, :].astype(F32)
-
-    def copies(self):
-        x, y = self.me.x, self.me.y
+    def copy(self, name):
         xp, yp = self.me.x_peer(), self.me.y_peer()
-        far, yfar, xfar = (1 - y) * 2 + (1 - x), (1 - y) * 2 + x, y * 2 + (1 - x)
-        table = {
-            "ay0": (far, 0, self.a_y.at[0], 4, yp),
-            "ay1": (yfar, 0, self.a_y.at[1], 5, yp),
-            "bx0": (far, 1, self.b_x.at[0], 6, xp),
-            "bx1": (xfar, 1, self.b_x.at[1], 7, xp),
-            "ax": (xfar, 0, self.a_x, 8, xp),
-            "by": (yfar, 1, self.b_y, 9, yp),
-        }
-        return {
-            name: remote(self.mine.at[slot, self.rows(h)], dst, self.send.at[i], self.recv.at[i], dev)
-            for name, (slot, h, dst, i, dev) in table.items()
-        }
-
-    def run(self, make, between=None):
-        x, y = self.me.x, self.me.y
-        far, yfar, xfar = (1 - y) * 2 + (1 - x), (1 - y) * 2 + x, y * 2 + (1 - x)
-        c = self.copies()
-        self.produce(0, make)
-        self.produce(1, make)
-        self.core_copy(0).wait_recv()
-        self.add(far, 0)
-        c["ay0"].start()
-        self.add(far, 1)
-        c["bx0"].start()
-        self.produce(2, make)
-        self.core_copy(1).wait_recv()
-        self.add(yfar, 0)
-        c["ay1"].start()
-        self.produce(3, make)
-        self.core_copy(2).wait_recv()
-        self.add(xfar, 1)
-        c["bx1"].start()
-        c["ay0"].wait_recv()
-        self.add(xfar, 0, "a")
-        c["ax"].start()
-        c["bx0"].wait_recv()
-        self.add(yfar, 1, "b")
-        c["by"].start()
+        slot, h, dst, i, dev = {
+            "ay0": (0, 0, self.a_y.at[0], 4, yp),
+            "ay1": (1, 0, self.a_y.at[1], 5, yp),
+            "bx0": (0, 1, self.b_x.at[0], 6, xp),
+            "bx1": (2, 1, self.b_x.at[1], 7, xp),
+            "ax": (2, 0, self.a_x, 8, xp),
+            "by": (1, 1, self.b_y, 9, yp),
+        }[name]
+        return remote(self.mine.at[slot, self.rows(h)], dst, self.send.at[i], self.recv.at[i], dev)
+
+    def first_sends(self, j):
+        for name in (("ay0", "bx0"), ("ay1",), ("bx1",))[j]:
+            self.copy(name).start()
+
+    def loop(self, make, send=True):
+        def ready(j):
+            self.core_copy(j).wait_recv()
+            if j < 2:
+                self.add(j, 0)
+            if j != 1:
+                self.add(j, 1)
+            if send:
+                self.first_sends(j)
+
+        def body(j, carry):
+            ox, oy = self.place(j)
+
+            @pl.when(j >= 2)
+            def _():
+                self.core_copy(j - 2).wait_send()
+
+            self.peer_out[j % 2] = make(block_of(ox, 1 - self.me.k, oy), 2 * j)
+            self.core_copy(j).start()
+            self.mine[j] = make(block_of(ox, self.me.k, oy), 2 * j + 1)
+            for i in range(3):
+
+                @pl.when(j == i + 1)
+                def _():
+                    ready(i)
+
+            return carry
+
+        lax.fori_loop(0, 4, body, 0)
+
+    def second(self):
+        self.copy("ay0").wait_recv()
+        self.add(2, 0, self.a_y)
+        self.copy("ax").start()
+        self.copy("bx0").wait_recv()
+        self.add(1, 1, self.b_x)
+        self.copy("by").start()
+
+    def arrive(self):
         self.core_copy(3).wait_recv()
-        if between is not None:
-            between()
         for name in ("ay1", "bx1", "ax", "by"):
-            c[name].wait_recv()
+            self.copy(name).wait_recv()
 
     def total(self, h, i):
-        slot = self.me.y * 2 + self.me.x
         r = pl.ds(pl.multiple_of(h * self.half + i * 16, 16), 16)
         q = pl.ds(pl.multiple_of(i * 16, 16), 16)
-        total = self.mine[slot, r, :].astype(F32) + self.core_in[slot, r, :].astype(F32)
+        total = self.mine[3, r, :].astype(F32) + self.core_in[3, r, :].astype(F32)
         if h == 0:
             return total + self.a_y[1, q, :].astype(F32) + self.a_x[q, :].astype(F32)
         return total + self.b_x[1, q, :].astype(F32) + self.b_y[q, :].astype(F32)
 
     def finish(self):
-        for i in range(4):
-            self.core_copy(i).wait_send()
-        for copy in self.copies().values():
-            copy.wait_send()
+        for j in (2, 3):
+            self.core_copy(j).wait_send()
+        for name in ("ay0", "ay1", "bx0", "bx1", "ax", "by"):
+            self.copy(name).wait_send()
 
 
 def reduce_scratch(rows, width):
     half = rows // 2
     return [
-        pltpu.VMEM((4, rows, width), BF),
+        pltpu.VMEM((2, rows, width), BF),
         pltpu.VMEM((4, rows, width), BF),
         pltpu.VMEM((4, rows, width), BF),
         pltpu.VMEM((2, half, width), BF),
@@ -550,12 +550,15 @@
     ffn.pump(1, 1 - y)
     wo_in.wait()
 
-    def attn_term(block):
+    def attn_term(block, i):
         r = pl.ds(pl.multiple_of(block * rows, rows), rows)
         return jnp.dot(o_v[r, :], wo_v[...], preferred_element_type=F32).astype(BF)
 
     red = ActReduce(me, peer_out, core_in, mine, ra_y, rb_x, ra_x, rb_y, red_send, red_recv)
-    red.run(attn_term, lambda: ffn.pump(2, y))
+    red.loop(attn_term)
+    red.second()
+    ffn.pump(2, y)
+    red.arrive()
 
     half = rows // 2
     for h in range(2):
@@ -629,7 +632,7 @@
         pltpu.VMEM((2, TQ, 2 * length), F32),
         pltpu.VMEM((2, TQ, length), BF),
         pltpu.VMEM((rows, width), BF),
-        pltpu.VMEM((4, rows, width), BF),
+        pltpu.VMEM((2, rows, width), BF),
         pltpu.VMEM((4, rows, width), BF),
         pltpu.VMEM((4, rows, width), BF),
         pltpu.VMEM((2, half, width), BF),
@@ -652,186 +655,583 @@
     )(wq, wk, wv, wo, wg, wu, wd, cot, small, seg, xin)
 
 
-def neighbours(me):
-    return [me.x_peer(), me.y_peer(), me.core_peer()]
-
-
-def dz_kernel(part, mid, cot, gain, gmid, dzall, ggain, *scratch):
-    red = scratch[:9]
-    dz, = scratch[9:10]
-    gs = scratch[10:]
+class LineSum:
+    def __init__(self, me, n, views, from_left, from_right, stage, sems, stage_sem):
+        self.me, self.n, self.views = me, n, views
+        self.inbox = {True: from_left, False: from_right}
+        self.stage, self.stage_sem = stage, stage_sem
+        self.sends = {True: sems[0], False: sems[1]}
+        self.recvs = {True: sems[2], False: sems[3]}
+
+    def copies(self, t, yy, right):
+        me = self.me
+        dev = me.device(z=me.z + 1 if right else me.z - 1)
+        return [
+            remote(
+                view, self.inbox[right].at[t, yy, i], self.sends[right].at[t, yy, i],
+                self.recvs[right].at[t, yy, i], dev,
+            )
+            for i, view in enumerate(self.views(t * 2 + yy))
+        ]
+
+    def start(self, t, yy, right):
+        for copy in self.copies(t, yy, right):
+            copy.start()
+
+    def add(self, t, yy, right):
+        for i, (copy, view) in enumerate(zip(self.copies(t, yy, right), self.views(t * 2 + yy))):
+            copy.wait_recv()
+            stage = self.stage[i]
+            load = pltpu.make_async_copy(self.inbox[right].at[t, yy, i], stage, self.stage_sem)
+            load.start()
+            load.wait()
+
+            def body(r, carry):
+                rr = pl.ds(pl.multiple_of(r * 16, 16), 16)
+                view[rr, :] = (view[rr, :].astype(F32) + stage[rr, :].astype(F32)).astype(BF)
+                return carry
+
+            lax.fori_loop(0, view.shape[0] // 16, body, 0)
+
+    def first(self, t, yy):
+        @pl.when((self.me.z == 0) & (t > 0))
+        def _():
+            self.start(t, yy, True)
+
+        @pl.when((self.me.z == self.n - 1) & (t < self.n - 1))
+        def _():
+            self.start(t, yy, False)
+
+    def pump(self, k, yy):
+        z, n = self.me.z, self.n
+
+        @pl.when((z + k <= n - 1) & (z > 0))
+        def _():
+            self.add(z + k, yy, True)
+            self.start(z + k, yy, True)
+
+        @pl.when((z - k >= 0) & (z < n - 1))
+        def _():
+            self.add(z - k, yy, False)
+            self.start(z - k, yy, False)
+
+    def own(self, yy):
+        z, n = self.me.z, self.n
+
+        @pl.when(z > 0)
+        def _():
+            self.add(z, yy, True)
+
+        @pl.when(z < n - 1)
+        def _():
+            self.add(z, yy, False)
+
+    def finish(self):
+        z, n = self.me.z, self.n
+        for yy in range(2):
+            for k in range(1, n):
+
+                @pl.when(z + k <= n - 1)
+                def _():
+                    for copy in self.copies(z + k, yy, True):
+                        copy.wait_send()
+
+                @pl.when(z - k >= 0)
+                def _():
+                    for copy in self.copies(z - k, yy, False):
+                        copy.wait_send()
+
+
+def far_first(n, z, i):
+    slot = 0
+    for a in range(n):
+        order = sorted(range(n), key=lambda d: (-abs(d - a), d))
+        for b in range(n):
+            slot = slot + jnp.where((z == a) & (i == b), order[b], 0)
+    return slot
+
+
+def gelu_parts(gate):
+    th = jnp.tanh(0.7978845608028654 * (gate + 0.044715 * gate * gate * gate))
+    gelu = 0.5 * gate * (1.0 + th)
+    slope = 0.5 * (1.0 + th) + 0.5 * gate * (1.0 - th * th) * 0.7978845608028654 * (
+        1.0 + 3 * 0.044715 * gate * gate
+    )
+    return gelu, slope
+
+
+def norm_back(ga, values, gain):
+    inv = lax.rsqrt(jnp.mean(values * values, axis=-1, keepdims=True) + EPSILON)
+    u = ga * gain
+    corr = jnp.mean(u * values, axis=-1, keepdims=True) * inv * inv * inv
+    return inv * u - values * corr, ga * (values * inv)
+
+
+def backward_kernel(
+    n, length, heads, hid,
+    wgu, wdf, a2all, gall, p, a1, qkv, o, wqkv, wof, hidden, mid, cot, gain1, gain2,
+    out, gx, fo, ao, sums, dzall, f_left, f_right, a_left, a_right,
+    wgu_v, wd_v, row_a, row_g, col_a, col_g, m, dgu, gwf, stage, gmid, dz, wqkv_v,
+    pbuf, acc, dkt, dvt, diag, gg1, gg2, sv, sv_in, sv_z, free,
+    load, p_sem, stage_sem, y_send, y_recv, y_local, sv_send, sv_recv, sz_send, sz_recv,
+    *rest,
+):
+    red_scratch, dz_sems, f_sems, a_sems = rest[:9], rest[9:12], rest[12:16], rest[16:20]
     me = Place()
-    greet(neighbours(me))
-    r = ActReduce(me, *red)
-    r.run(lambda b: part[b])
-    half = mid.shape[0] // 2
-    ggain[...] = jnp.zeros_like(ggain)
+    z, y = me.z, me.y
+    rows, width = cot.shape
+    group = [
+        me.device(x=ox, k=ok, y=oy)
+        for ox in (me.x, 1 - me.x)
+        for ok in (me.k, 1 - me.k)
+        for oy in (me.y, 1 - me.y)
+    ][1:]
+    others = [me.device(z=lax.rem(z + s, n)) for s in range(1, n)]
+    greet(group + others)
+    local_heads = heads // DH
+    half = rows // 2
+
+    def fetch(src, dst, i):
+        return pltpu.make_async_copy(src, dst, load.at[i])
+
+    red = ActReduce(me, *red_scratch)
+    fsum = LineSum(me, n, lambda pc: [gwf.at[pc]], f_left, f_right, [stage], f_sems, stage_sem)
+
+    def piece(pc):
+        return pl.ds(pl.multiple_of(pc * rows, rows), rows)
+
+    asum = LineSum(
+        me, n,
+        lambda pc: [dgu.at[piece(pc), pl.ds(3 * heads, 2 * heads)], m.at[piece(pc), pl.ds(0, 2 * heads)]],
+        a_left, a_right, [stage.at[:, pl.ds(0, 2 * heads)], stage.at[:, pl.ds(2 * heads, 2 * heads)]],
+        a_sems, stage_sem,
+    )
+
+    w_loads = [fetch(wgu, wgu_v, 0), fetch(wdf, wd_v, 1)]
+    for copy in w_loads:
+        copy.start()
+
+    def block_at(i):
+        j = i // 2
+        ox, oy = red.place(j)
+        return block_of(ox, jnp.where(i % 2 == 0, 1 - me.k, me.k), oy)
+
+    fetch(a2all.at[block_at(0)], row_a, 2).start()
+    fetch(gall.at[block_at(0)], row_g, 3).start()
+    for copy in w_loads:
+        copy.wait()
+
+    def make_ffn(block, i):
+        fetch(a2all.at[block], row_a, 2).wait()
+        acc[:, 0 : 2 * hid] = jnp.dot(row_a[...], wgu_v[...], preferred_element_type=F32)
+
+        @pl.when(i < 7)
+        def _():
+            fetch(a2all.at[block_at(i + 1)], row_a, 2).start()
+
+        fetch(gall.at[block], row_g, 3).wait()
+        acc[:, 2 * hid : 3 * hid] = lax.dot_general(
+            row_g[...], wd_v[...], (((1,), (1,)), ((), ())), preferred_element_type=F32
+        )
+
+        @pl.when(i < 7)
+        def _():
+            fetch(gall.at[block_at(i + 1)], row_g, 3).start()
+
+        def body(r, carry):
+            rr = pl.ds(pl.multiple_of(r * 16, 16), 16)
+            tr = pl.ds(pl.multiple_of(block * rows + r * 16, 16), 16)
+            gate, up, gm = acc[rr, 0:hid], acc[rr, hid : 2 * hid], acc[rr, 2 * hid : 3 * hid]
+            gelu, slope = gelu_parts(gate)
+            m[tr, :] = (gelu * up).astype(BF)
+            dgu[tr, 0:hid] = (gm * up * slope).astype(BF)
+            dgu[tr, hid : 2 * hid] = (gm * gelu).astype(BF)
+            return carry
+
+        lax.fori_loop(0, rows // 16, body, 0)
+        return lax.dot_general(
+            dgu[piece(block), :], wgu_v[...], (((1,), (1,)), ((), ())), preferred_element_type=F32
+        ).astype(BF)
+
+    red.loop(make_ffn)
+
+    fetch(wof, row_g, 3).start()
+
+    def piece_at(i):
+        return far_first(n, z, i // 2) * 2 + jnp.where(i % 2 == 0, 1 - y, y)
+
+    def columns(ref, i):
+        return ref.at[:, :, piece(piece_at(i))]
+
+    fetch(columns(a2all, 0), col_a, 4).start()
+    fetch(columns(gall, 0), col_g, 5).start()
+
+    def ffn_grads(i, carry):
+        pc = piece_at(i)
+        fetch(columns(a2all, i), col_a, 4).wait()
+        gwf[pc, :, 0 : 2 * hid] = lax.dot_general(
+            col_a[...].reshape(8 * rows, rows), dgu[...], (((0,), (0,)), ((), ())), preferred_element_type=F32
+        ).astype(BF)
+
+        @pl.when(i < 2 * n - 1)
+        def _():
+            fetch(columns(a2all, i + 1), col_a, 4).start()
+
+        fetch(columns(gall, i), col_g, 5).wait()
+        gwf[pc, :, 2 * hid : 3 * hid] = lax.dot_general(
+            col_g[...].reshape(8 * rows, rows), m[...], (((0,), (0,)), ((), ())), preferred_element_type=F32
+        ).astype(BF)
+
+        @pl.when(i < 2 * n - 1)
+        def _():
+            fetch(columns(gall, i + 1), col_g, 5).start()
+
+        fsum.first(pc // 2, pc % 2)
+        return carry
+
+    lax.fori_loop(0, n, ffn_grads, 0)
+    red.second()
+    fetch(qkv, wgu_v.at[:, pl.ds(0, 3 * heads)], 0).start()
+    fetch(o, wgu_v.at[:, pl.ds(3 * heads, heads)], 6).start()
+    red.arrive()
+
+    gg2[...] = jnp.zeros_like(gg2)
     for h in range(2):
 
         def body(i, carry):
             rr = pl.ds(pl.multiple_of(h * half + i * 16, 16), 16)
-            ga = r.total(h, i)
-            m = mid[rr, :]
-            inv = lax.rsqrt(jnp.mean(m * m, axis=-1, keepdims=True) + EPSILON)
-            prod = ga * (m * inv)
-            ggain[...] += prod[:8] + prod[8:]
-            u = ga * gain[...]
-            corr = jnp.mean(u * m, axis=-1, keepdims=True) * inv * inv * inv
-            gm = cot[rr, :].astype(F32) + inv * u - m * corr
+            back, gains = norm_back(red.total(h, i), mid[rr, :], gain2[...])
+            gm = cot[rr, :].astype(F32) + back
             gmid[rr, :] = gm
             dz[rr, :] = gm.astype(BF)
+            gg2[...] += gains[:8] + gains[8:]
             return carry
 
         lax.fori_loop(0, half // 16, body, 0)
-    g = ActGather(me, dz, dzall, *gs)
-    g.start()
-    g.forward()
-    g.forward_core()
-    g.finish()
-    r.finish()
-
-
-def dz_step(part, mid, cot, gain):
-    rows, width = mid.shape
-    return pl.pallas_call(
-        dz_kernel,
-        out_shape=[
-            jax.ShapeDtypeStruct((rows, width), F32),
-            jax.ShapeDtypeStruct((8, rows, width), BF),
-            jax.ShapeDtypeStruct((8, width), F32),
-        ],
-        in_specs=[VM, VM, VM, VM],
-        out_specs=[VM, ANY, VM],
-        scratch_shapes=reduce_scratch(rows, width) + [pltpu.VMEM((rows, width), BF)] + gather_sems(),
-        compiler_params=pltpu.CompilerParams(collective_id=2, has_side_effects=True, vmem_limit_bytes=60 << 20),
-        name="dz_step",
-    )(part, mid, cot, gain)
-
-
-def last_kernel(ga_part, out_part, xin, gmid, mid, gain, gx, out, ggain, *scratch):
-    me = Place()
-    greet(neighbours(me))
-    r = ActReduce(me, *scratch[:9])
-    q = ActReduce(me, *scratch[9:18])
-    r.run(lambda b: ga_part[b])
-    q.run(lambda b: out_part[b])
-    half = xin.shape[0] // 2
-    ggain[...] = jnp.zeros_like(ggain)
+    act = ActGather(me, dz, dzall, *dz_sems)
+    act.start()
+    red.finish()
+
+    def release():
+        for i, dev in enumerate((me.x_peer(), me.y_peer(), me.core_peer())):
+            pl.semaphore_signal(free.at[i], inc=1, device_id=dev, device_id_type=MESH)
+
+    def claim():
+        for i in range(3):
+            pl.semaphore_wait(free.at[i], 1)
+
+    release()
+    lax.fori_loop(n, 2 * n, ffn_grads, 0)
+    act.forward()
+
+    claim()
+
+    def make_out(block, i):
+        return jnp.dot(m[piece(block), :], wd_v[...], preferred_element_type=F32).astype(BF)
+
+    red.loop(make_out, send=False)
+    order = (1 - y, y)
+    fsum.pump(2, order[0])
+    act.forward_core()
+    for j in range(3):
+        red.first_sends(j)
+    act.finish()
+    fsum.pump(2, order[1])
+
+    fetch(wof, row_g, 3).wait()
+    fetch(dzall.at[0], row_a, 2).start()
+
+    def project_back(b, carry):
+        fetch(dzall.at[b], row_a, 2).wait()
+        wgu_v[piece(b), 4 * heads : 5 * heads] = lax.dot_general(
+            row_a[...], row_g[...], (((1,), (1,)), ((), ())), preferred_element_type=F32
+        ).astype(BF)
+
+        @pl.when(b < 7)
+        def _():
+            fetch(dzall.at[b + 1], row_a, 2).start()
+
+        return carry
+
+    lax.fori_loop(0, 8, project_back, 0)
+    fetch(hidden, row_a, 2).start()
+    fetch(wqkv, wqkv_v, 1).start()
+    fetch(qkv, wgu_v.at[:, pl.ds(0, 3 * heads)], 0).wait()
+    fetch(o, wgu_v.at[:, pl.ds(3 * heads, heads)], 6).wait()
+    diag[...] = jnp.zeros_like(diag)
+    tiles = length // TQ
+
+    def p_load(head, t, slot):
+        return pltpu.make_async_copy(p.at[head, pl.ds(t * TQ, TQ)], pbuf.at[slot], p_sem.at[slot])
+
+    def head_pair(hp):
+        def sequence(s, carry):
+            head0 = s * local_heads + hp * 2
+            base = pl.multiple_of(s * length, length)
+            p_load(head0, 0, 0).start()
+            p_load(head0, 1, 1).start()
+            for h in range(2):
+                lo = hp * 128 + h * DH
+                seq = pl.ds(base, length)
+                kh = wgu_v[seq, heads + lo : heads + lo + DH]
+                vh = wgu_v[seq, 2 * heads + lo : 2 * heads + lo + DH]
+                acc[...] = jnp.zeros_like(acc)
+                for t in range(tiles):
+                    slot = t % 2
+                    r = pl.ds(pl.multiple_of(base + t * TQ, TQ), TQ)
+                    qh = wgu_v[r, lo : lo + DH]
+                    doh = wgu_v[r, 4 * heads + lo : 4 * heads + lo + DH]
+                    p_load(head0 + h, t, slot).wait()
+                    pb = pbuf[slot]
+                    dp = lax.dot_general(doh, vh, (((1,), (1,)), ((), ())), preferred_element_type=F32)
+                    pf = pb.astype(F32)
+                    ds = (pf * (dp - jnp.sum(pf * dp, axis=-1, keepdims=True))).astype(BF)
+                    dgu[r, lo : lo + DH] = jnp.dot(ds, kh, preferred_element_type=F32).astype(BF)
+                    ck = lax.dot_general(qh, ds, (((0,), (0,)), ((), ())), preferred_element_type=F32)
+                    cv = lax.dot_general(doh, pb, (((0,), (0,)), ((), ())), preferred_element_type=F32)
+                    u = h * tiles + t + 2
+                    if u < 2 * tiles:
+                        p_load(head0 + u // tiles, u % tiles, slot).start()
+                    if t == 0:
+                        dkt[...] = ck
+                        dvt[...] = cv
+                    else:
+                        dkt[...] += ck
+                        dvt[...] += cv
+                    acc[:, length - t * TQ : 2 * length - t * TQ] += ds.astype(F32)
+                dgu[seq, heads + lo : heads + lo + DH] = dkt[...].T.astype(BF)
+                dgu[seq, 2 * heads + lo : 2 * heads + lo + DH] = dvt[...].T.astype(BF)
+                c = TQ // 2
+                while c >= 8:
+                    acc[0:c, :] += pltpu.roll(acc[c : 2 * c, :], 2 * length - c, 1)
+                    c //= 2
+                diag[hp * 2 + h] += acc[0:8, :]
+            return carry
+
+        lax.fori_loop(0, 2, sequence, 0)
+
+    head_pair(0)
+    fsum.pump(1, order[0])
+    red.second()
+    head_pair(1)
+    fsum.pump(1, order[1])
+
+    fetch(columns(a1, 0), col_a, 4).start()
+    fetch(columns(dzall, 0), col_g, 5).start()
+
+    def attn_grads(i, carry):
+        pc = piece_at(i)
+        fetch(columns(a1, i), col_a, 4).wait()
+        part = lax.dot_general(
+            col_a[...].reshape(8 * rows, rows), dgu[:, 0 : 3 * heads], (((0,), (0,)), ((), ())),
+            preferred_element_type=F32,
+        ).astype(BF)
+        dgu[piece(pc), 3 * heads : 5 * heads] = part[:, 0 : 2 * heads]
+        m[piece(pc), 0:heads] = part[:, 2 * heads : 3 * heads]
+
+        @pl.when(i < 2 * n - 1)
+        def _():
+            fetch(columns(a1, i + 1), col_a, 4).start()
+
+        fetch(columns(dzall, i), col_g, 5).wait()
+        m[piece(pc), heads : 2 * heads] = lax.dot_general(
+            col_g[...].reshape(8 * rows, rows), wgu_v[:, 3 * heads : 4 * heads], (((0,), (0,)), ((), ())),
+            preferred_element_type=F32,
+        ).astype(BF)
+
+        @pl.when(i < 2 * n - 1)
+        def _():
+            fetch(columns(dzall, i + 1), col_g, 5).start()
+
+        asum.first(pc // 2, pc % 2)
+        return carry
+
+    lax.fori_loop(0, 2 * n, attn_grads, 0)
+
+    red.arrive()
     for h in range(2):
 
         def body(i, carry):
             rr = pl.ds(pl.multiple_of(h * half + i * 16, 16), 16)
-            ga = r.total(h, i)
-            m = xin[rr, :].astype(F32)
-            inv = lax.rsqrt(jnp.mean(m * m, axis=-1, keepdims=True) + EPSILON)
-            prod = ga * (m * inv)
-            ggain[...] += prod[:8] + prod[8:]
-            u = ga * gain[...]
-            corr = jnp.mean(u * m, axis=-1, keepdims=True) * inv * inv * inv
-            gx[rr, :] = gmid[rr, :] + inv * u - m * corr
-            out[rr, :] = (mid[rr, :] + q.total(h, i)).astype(BF)
+            out[rr, :] = (mid[rr, :] + red.total(h, i)).astype(BF)
             return carry
 
         lax.fori_loop(0, half // 16, body, 0)
-    r.finish()
-    q.finish()
-
-
-def last_step(ga_part, out_part, xin, gmid, mid, gain):
-    rows, width = xin.shape
+    red.finish()
+    release()
+    claim()
+    fetch(wqkv, wqkv_v, 1).wait()
+
+    def make_ga1(block, i):
+        return lax.dot_general(
+            dgu[piece(block), 0 : 3 * heads], wqkv_v[...], (((1,), (1,)), ((), ())), preferred_element_type=F32
+        ).astype(BF)
+
+    red.loop(make_ga1)
+
+    offset = lax.broadcasted_iota(jnp.int32, (NB, 2 * length), 1) - length
+    away = jnp.abs(offset)
+    bucket = jnp.where(away < 8, away, 8 + sum((away >= t).astype(jnp.int32) for t in THRESHOLDS))
+    bucket = bucket + 16 * (offset > 0).astype(jnp.int32)
+    own_bucket = bucket == lax.broadcasted_iota(jnp.int32, (NB, 2 * length), 0)
+    lane = lax.broadcasted_iota(jnp.int32, (NB, 128), 1)
+    table = jnp.zeros((NB, 128), F32)
+    for lh in range(local_heads):
+        line = diag[lh, 0:1, :]
+        for r in range(1, 8):
+            line = line + pltpu.roll(diag[lh, r : r + 1, :], 2 * length - r, 1)
+        value = jnp.sum(jnp.where(own_bucket, line, 0.0), axis=1, keepdims=True)
+        table = jnp.where(lane == (me.c * 2 + y) * local_heads + lh, value, table)
+    red.second()
+
+    fsum.own(order[0])
+    red.arrive()
+    gg1[...] = jnp.zeros_like(gg1)
+    fetch(hidden, row_a, 2).wait()
+    for h in range(2):
+
+        def body(i, carry):
+            rr = pl.ds(pl.multiple_of(h * half + i * 16, 16), 16)
+            back, gains = norm_back(red.total(h, i), row_a[rr, :].astype(F32), gain1[...])
+            gx[rr, :] = gmid[rr, :] + back
+            gg1[...] += gains[:8] + gains[8:]
+            return carry
+
+        lax.fori_loop(0, half // 16, body, 0)
+    red.finish()
+
+    first_row = lax.broadcasted_iota(jnp.int32, (8, 128), 0) == 0
+    for d in range(8 * n):
+        g, zz = d % 8, d // 8
+        lanes = slice(d // 2 * 128, d // 2 * 128 + 128)
+        sv[g, zz, :, 0:128] = gg1[:, lanes]
+        sv[g, zz, :, 128:256] = gg2[:, lanes]
+        sv[g, zz, :, 256:384] = jnp.where(first_row, jnp.broadcast_to(table[d : d + 1, :], (8, 128)), 0.0)
+    peers = [
+        (ox * 4 + ok * 2 + oy)
+        for ox in (me.x, 1 - me.x)
+        for ok in (me.k, 1 - me.k)
+        for oy in (me.y, 1 - me.y)
+    ]
+    sv_copies = [
+        remote(sv.at[peers[i + 1]], sv_in.at[i], sv_send.at[i], sv_recv.at[i], dev)
+        for i, dev in enumerate(group)
+    ]
+    for copy in sv_copies:
+        copy.start()
+
+    def swap(line, slot, views, box, i, wait):
+        copies = []
+        for v, (dst, sem) in enumerate(zip(box, range(i, i + len(box)))):
+            copies.append(
+                remote(views(z * 2 + 1 - y)[v], dst.at[y], y_send.at[sem], y_recv.at[sem], me.y_peer())
+            )
+        keeps = [
+            pltpu.make_async_copy(views(z * 2 + y)[v], dst.at[y], y_local.at[sem])
+            for v, (dst, sem) in enumerate(zip(box, range(i, i + len(box))))
+        ]
+        return copies, keeps
+
+    ao_boxes = [ao.at[0], ao.at[1]]
+    f_out, f_keep = swap(fsum, None, fsum.views, [fo], 0, None)
+    a_out, a_keep = swap(asum, None, asum.views, ao_boxes, 1, None)
+    for copy in f_out:
+        copy.start()
+    fsum.own(order[1])
+    for copy in f_keep:
+        copy.start()
+    for yy in order:
+        asum.pump(2, yy)
+    for copy in sv_copies:
+        copy.wait_recv()
+    me_g = me.c * 2 + y
+    total = sv[me_g]
+    for i in range(7):
+        total = total + sv_in[i]
+    sv_z[0] = total
+    z_copies = [
+        remote(sv_z.at[0, lax.rem(z + s, n)], sv_z.at[s, 0], sz_send.at[s - 1], sz_recv.at[s - 1], others[s - 1])
+        for s in range(1, n)
+    ]
+    for copy in z_copies:
+        copy.start()
+    for yy in order:
+        asum.pump(1, yy)
+    asum.own(order[0])
+    for copy in a_out:
+        copy.start()
+    asum.own(order[1])
+    for copy in a_keep:
+        copy.start()
+    for copy in z_copies:
+        copy.wait_recv()
+    total = sv_z[0, z]
+    for s in range(1, n):
+        total = total + sv_z[s, 0]
+    sums[...] = total
+    for copy in f_out + a_out:
+        copy.wait()
+    for copy in f_keep + a_keep:
+        copy.wait()
+    for copy in sv_copies + z_copies:
+        copy.wait_send()
+    fsum.finish()
+    asum.finish()
+
+
+def backward(n, length, heads, hid, wgu, wdf, a2all, gall, p, a1, qkv, o, wqkv, wof, hidden, mid, cot, gain1, gain2):
+    rows, width = cot.shape
+    tokens = 8 * rows
+    shapes = [
+        ((rows, width), BF),
+        ((rows, width), F32),
+        ((2, rows, 3 * hid), BF),
+        ((2, 2, rows, 2 * heads), BF),
+        ((8, 384), F32),
+        ((8, rows, width), BF),
+        ((n, 2, 1, rows, 3 * hid), BF),
+        ((n, 2, 1, rows, 3 * hid), BF),
+        ((n, 2, 2, rows, 2 * heads), BF),
+        ((n, 2, 2, rows, 2 * heads), BF),
+    ]
+    scratch = [
+        pltpu.VMEM((width, 2 * hid), BF),
+        pltpu.VMEM((hid, width), BF),
+        pltpu.VMEM((rows, width), BF),
+        pltpu.VMEM((rows, width), BF),
+        pltpu.VMEM((8, rows, rows), BF),
+        pltpu.VMEM((8, rows, rows), BF),
+        pltpu.VMEM((tokens, hid), BF),
+        pltpu.VMEM((tokens, 2 * hid), BF),
+        pltpu.VMEM((2 * n, rows, 3 * hid), BF),
+        pltpu.VMEM((rows, 3 * hid), BF),
+        pltpu.VMEM((rows, width), F32),
+        pltpu.VMEM((rows, width), BF),
+        pltpu.VMEM((width, 3 * heads), BF),
+        pltpu.VMEM((2, TQ, length), BF),
+        pltpu.VMEM((TQ, 2 * length), F32),
+        pltpu.VMEM((DH, length), F32),
+        pltpu.VMEM((DH, length), F32),
+        pltpu.VMEM((heads // DH, 8, 2 * length), F32),
+        pltpu.VMEM((8, width), F32),
+        pltpu.VMEM((8, width), F32),
+        pltpu.VMEM((8, n, 8, 384), F32),
+        pltpu.VMEM((7, n, 8, 384), F32),
+        pltpu.VMEM((n, n, 8, 384), F32),
+        pltpu.SemaphoreType.REGULAR((3,)),
+        DMA((7,)), DMA((2,)), DMA, DMA((3,)), DMA((3,)), DMA((3,)), DMA((7,)), DMA((7,)), DMA((n - 1,)), DMA((n - 1,)),
+    ] + reduce_scratch(rows, width) + gather_sems() + [DMA((n, 2, 1))] * 4 + [DMA((n, 2, 2))] * 4
     return pl.pallas_call(
-        last_kernel,
-        out_shape=[
-            jax.ShapeDtypeStruct((rows, width), F32),
-            jax.ShapeDtypeStruct((rows, width), BF),
-            jax.ShapeDtypeStruct((8, width), F32),
-        ],
-        in_specs=[VM, VM, VM, VM, VM, VM],
-        out_specs=[VM, VM, VM],
-        scratch_shapes=reduce_scratch(rows, width) * 2,
-        compiler_params=pltpu.CompilerParams(collective_id=3, has_side_effects=True, vmem_limit_bytes=62 << 20),
-        name="last_step",
-    )(ga_part, out_part, xin, gmid, mid, gain)
-
-
-def attention_backward(q, k, v, do, p, dq, dk, dv, diag, acc, dkt, dvt):
-    length = q.shape[0]
-    for h in range(2):
-        cols = slice(h * DH, (h + 1) * DH)
-        kh = k[:, cols]
-        vh = v[:, cols]
-        acc[...] = jnp.zeros_like(acc)
-        for t in range(length // TQ):
-            rows = slice(t * TQ, (t + 1) * TQ)
-            pb = p[h, rows, :]
-            doh = do[rows, cols]
-            qh = q[rows, cols]
-            dp = lax.dot_general(doh, vh, (((1,), (1,)), ((), ())), preferred_element_type=F32)
-            pf = pb.astype(F32)
-            ds = (pf * (dp - jnp.sum(pf * dp, axis=-1, keepdims=True))).astype(BF)
-            dq[rows, cols] = jnp.dot(ds, kh, preferred_element_type=F32).astype(BF)
-            ck = lax.dot_general(qh, ds, (((0,), (0,)), ((), ())), preferred_element_type=F32)
-            cv = lax.dot_general(doh, pb, (((0,), (0,)), ((), ())), preferred_element_type=F32)
-            if t == 0:
-                dkt[...] = ck
-                dvt[...] = cv
-            else:
-                dkt[...] += ck
-                dvt[...] += cv
-            acc[:, length - t * TQ : 2 * length - t * TQ] += ds.astype(F32)
-        dk[:, cols] = dkt[...].T.astype(BF)
-        dv[:, cols] = dvt[...].T.astype(BF)
-        n = TQ // 2
-        while n >= 8:
-            acc[0:n, :] += pltpu.roll(acc[n : 2 * n, :], 2 * length - n, 1)
-            n //= 2
-        diag[h] = acc[0:8, :]
-
-
-def run_attention_backward(qkv, do, p):
-    total, width = qkv.shape
-    heads = width // 3 // DH
-    length = p.shape[1]
-    seqs = total // length
-    pairs = heads // 2
-    qspec = lambda off: pl.BlockSpec((length, 2 * DH), lambda s, h: (s, off * pairs + h))
-    flat = pl.BlockSpec((length, 2 * DH), lambda s, h: (s, h))
-    return pl.pallas_call(
-        attention_backward,
-        grid=(seqs, pairs),
-        out_shape=[jax.ShapeDtypeStruct((total, heads * DH), BF)] * 3
-        + [jax.ShapeDtypeStruct((seqs * heads, 8, 2 * length), F32)],
-        in_specs=[
-            qspec(0),
-            qspec(1),
-            qspec(2),
-            flat,
-            pl.BlockSpec((2, length, length), lambda s, h: (s * pairs + h, 0, 0)),
-        ],
-        out_specs=[flat, flat, flat, pl.BlockSpec((2, 8, 2 * length), lambda s, h: (s * pairs + h, 0, 0))],
-        scratch_shapes=[
-            pltpu.VMEM((TQ, 2 * length), F32),
-            pltpu.VMEM((DH, length), F32),
-            pltpu.VMEM((DH, length), F32),
-        ],
-        compiler_params=pltpu.CompilerParams(vmem_limit_bytes=48 << 20),
-        name="attention_backward",
-    )(qkv, qkv, qkv, do, p)
-
-
-def offset_buckets(length):
-    relative = jnp.arange(2 * length, dtype=jnp.int32) - length
-    distance = jnp.abs(relative)
-    log_bucket = 8 + sum((distance >= t).astype(jnp.int32) for t in THRESHOLDS)
-    bucket = jnp.where(distance < 8, distance, log_bucket) + 16 * (relative > 0).astype(jnp.int32)
-    return (bucket[:, None] == jnp.arange(NB, dtype=jnp.int32)[None, :]).astype(F32)
-
-
-def swap_rows(part, y, swap):
-    rows = part.shape[0] // 2
-    mine = lax.dynamic_slice_in_dim(part, y * rows, rows, 0)
-    theirs = lax.ppermute(lax.dynamic_slice_in_dim(part, (1 - y) * rows, rows, 0), "fsdp", swap)
-    return jnp.where(y == 0, mine, theirs), jnp.where(y == 0, theirs, mine)
+        functools.partial(backward_kernel, n, length, heads, hid),
+        out_shape=[jax.ShapeDtypeStruct(s, d) for s, d in shapes],
+        in_specs=[ANY] * 11 + [VM] * 4,
+        out_specs=[VM, VM, ANY, ANY, VM] + [ANY] * 5,
+        scratch_shapes=scratch,
+        compiler_params=pltpu.CompilerParams(
+            collective_id=1, has_side_effects=True, vmem_limit_bytes=64 << 20
+        ),
+        name="backward",
+    )(wgu, wdf, a2all, gall, p, a1, qkv, o, wqkv, wof, hidden, mid, cot, gain1, gain2)
 
 
 def on_device(
@@ -840,88 +1240,31 @@
 ):
     xin = hidden[0]
     cot = cotangent[0]
-    rows, width = xin.shape
     length = segment_ids.shape[1]
     heads = w_query.shape[1] // 2
     hid = w_gate.shape[1] // 2
+    share = attn_gain.shape[0]
     y = lax.axis_index("fsdp")
-    c = lax.axis_index("ctx")
-    swap = [(0, 1), (1, 0)]
-    lanes = lambda v: jnp.where(y == 0, jnp.pad(v, (0, 64)), jnp.pad(v, (64, 0))).astype(F32)
-    packed = jnp.concatenate([lanes(attn_gain), lanes(ffn_gain), jnp.pad(rel_table.astype(F32), (0, 96))])
+    lanes = lambda v: jnp.where(y == 0, jnp.pad(v, (0, 128 - share)), jnp.pad(v, (128 - share, 0))).astype(F32)
+    packed = jnp.concatenate([lanes(attn_gain), lanes(ffn_gain), jnp.pad(rel_table.astype(F32), (0, 128 - H))])
     small = jnp.broadcast_to(packed[None, :], (8, packed.shape[0]))
     seg = jnp.broadcast_to(segment_ids, (8, length))
     wqkv, wo, wgu, wd, a1, qkv, o, p, mid, a2all, gall, gain1, gain2 = forward(
         n, w_query, w_key, w_value, w_attn_out, w_gate, w_up, w_down, cot, small, seg, xin
     )
-    local_heads = heads // DH
-    one_hot = offset_buckets(length)
-    a1 = a1.reshape(8 * rows, width)
-    a2 = a2all.reshape(8 * rows, width)
-    gall = gall.reshape(8 * rows, width)
-    gate_up = jnp.dot(a2, wgu, preferred_element_type=F32)
-    gate, up = gate_up[:, :hid], gate_up[:, hid:]
-    inner = 0.7978845608028654 * (gate + 0.044715 * gate * gate * gate)
-    th = jnp.tanh(inner)
-    gelu = 0.5 * gate * (1.0 + th)
-    slope = 0.5 * (1.0 + th) + 0.5 * gate * (1.0 - th * th) * 0.7978845608028654 * (
-        1.0 + 3 * 0.044715 * gate * gate
-    )
-    m = (gelu * up).astype(BF)
-    gm = lax.dot_general(gall, wd, (((1,), (1,)), ((), ())), preferred_element_type=F32)
-    dgu = jnp.concatenate([(gm * up * slope).astype(BF), (gm * gelu).astype(BF)], axis=1)
-    gw_gu = lax.dot_general(a2, dgu, (((0,), (0,)), ((), ())), preferred_element_type=F32).astype(BF)
-    gw_d = lax.dot_general(m, gall, (((0,), (0,)), ((), ())), preferred_element_type=F32).astype(BF)
-    ga2 = lax.dot_general(dgu, wgu, (((1,), (1,)), ((), ())), preferred_element_type=F32).astype(BF)
-    out_part = jnp.dot(m, wd, preferred_element_type=F32).astype(BF)
-    rs_gu = lax.psum_scatter(gw_gu, "dp", scatter_dimension=0, tiled=True)
-    rs_d = lax.psum_scatter(gw_d, "dp", scatter_dimension=1, tiled=True)
-    gmid, dzall, ggain2 = dz_step(ga2.reshape(8, rows, width), mid, cot, gain2)
-    dz = dzall.reshape(8 * rows, width)
-    do = lax.dot_general(dz, wo, (((1,), (1,)), ((), ())), preferred_element_type=F32).astype(BF)
-    gw_o = lax.dot_general(o, dz, (((0,), (0,)), ((), ())), preferred_element_type=F32).astype(BF)
-    rs_o = lax.psum_scatter(gw_o, "dp", scatter_dimension=1, tiled=True)
-    dq, dk, dv, diag = run_attention_backward(qkv, do, p)
-    dqkv = jnp.concatenate([dq, dk, dv], axis=1)
-    gw_qkv = lax.dot_general(a1, dqkv, (((0,), (0,)), ((), ())), preferred_element_type=F32).astype(BF)
-    rs_qkv = lax.psum_scatter(gw_qkv, "dp", scatter_dimension=0, tiled=True)
-    ga1 = lax.dot_general(dqkv, wqkv, (((1,), (1,)), ((), ())), preferred_element_type=F32).astype(BF)
-    gx, out, ggain1 = last_step(
-        ga1.reshape(8, rows, width), out_part.reshape(8, rows, width), xin, gmid, mid, gain1
-    )
-
-    d8 = jnp.sum(diag.reshape(-1, local_heads, 8, 2 * length), axis=0)
-    shifted = sum(jnp.roll(d8[:, r, :], -r, axis=-1) for r in range(8))
-    bias = lax.dot_general(
-        one_hot, shifted, (((0,), (1,)), ((), ())), precision=lax.Precision.HIGHEST
-    )
-    table_term = lax.dynamic_update_slice(
-        jnp.zeros((NB, H), F32), bias, (jnp.int32(0), (c * 2 + y) * local_heads)
-    )
-    axes = ("dp", "ctx", "fsdp")
-    g_attn_gain = lax.psum_scatter(jnp.sum(ggain1, axis=0), axes, scatter_dimension=0, tiled=True)
-    g_ffn_gain = lax.psum_scatter(jnp.sum(ggain2, axis=0), axes, scatter_dimension=0, tiled=True)
-    g_table = lax.psum_scatter(table_term.reshape(NB * H), axes, scatter_dimension=0, tiled=True)
-
-    lo, hi = swap_rows(rs_gu, y, swap)
-    g_gate = jnp.concatenate([lo[:, :hid], hi[:, :hid]], axis=1).astype(F32)
-    g_up = jnp.concatenate([lo[:, hid:], hi[:, hid:]], axis=1).astype(F32)
-    lo, hi = swap_rows(rs_qkv, y, swap)
-    g_q, g_k, g_v = (
-        jnp.concatenate([lo[:, i * heads : (i + 1) * heads], hi[:, i * heads : (i + 1) * heads]], axis=1).astype(F32)
-        for i in range(3)
-    )
-
-    def swap_cols(part):
-        mine = lax.dynamic_slice_in_dim(part, y * rows, rows, 1)
-        theirs = lax.ppermute(lax.dynamic_slice_in_dim(part, (1 - y) * rows, rows, 1), "fsdp", swap)
-        return jnp.concatenate(
-            [jnp.where(y == 0, mine, theirs), jnp.where(y == 0, theirs, mine)], axis=0
-        ).astype(F32)
-
+    out, gx, fo, ao, sums = backward(
+        n, length, heads, hid, wgu, wd, a2all, gall, p, a1, qkv, o, wqkv, wo, xin, mid, cot, gain1, gain2
+    )[:5]
+    sides = lambda part: jnp.concatenate([part[0], part[1]], axis=1).astype(F32)
+    g_gate, g_up = sides(fo[:, :, :hid]), sides(fo[:, :, hid : 2 * hid])
+    g_down = sides(fo[:, :, 2 * hid :]).T
+    g_q, g_k = sides(ao[0, :, :, :heads]), sides(ao[0, :, :, heads:])
+    g_v, g_o = sides(ao[1, :, :, :heads]), sides(ao[1, :, :, heads:]).T
+    line = jnp.sum(sums, axis=0)
+    half_of = lambda v: jnp.where(y == 0, v[:share], v[128 - share :])
     return (
-        out[None], gx[None], g_attn_gain, g_q, g_k, g_v, swap_cols(rs_o), g_table, g_ffn_gain,
-        g_gate, g_up, swap_cols(rs_d),
+        out[None], gx[None], half_of(line[:128]), g_q, g_k, g_v, g_o, line[256 : 256 + H],
+        half_of(line[128:256]), g_gate, g_up, g_down,
     )
 
 

time: 687 us -> 563 us (0.82)
  matrix products: 120 us -> 0 us
  Pallas kernels: 444 us -> 534 us
  blocking collectives: 47.4 us -> 0 us
  waiting for transfers between devices: 23.5 us -> 0 us
  between operations: 14.6 us -> 1.14 us
    dot_general x11 -> x0, matrix products: 120 us -> none  [the longest x1 17.8 us: on_device(): gate_up = jnp.dot(a2, wgu, preferred_element_type=F32)]
    pallas_call x3 -> x1, Pallas kernels: 207 us -> 296 us  [backward(): pl.pallas_call(functools.partial(backward_kernel, n, length, heads, hid),...]
    unnamed x1 -> x0, blocking collectives: 47.4 us -> none
    ppermute x4 -> x0, waiting for transfers between devices: 23.4 us -> none  [the longest x2 16.9 us: swap_rows(): lax.ppermute(lax.dynamic_slice_in_dim(part, (1 - y) * rows, rows, 0), 'fs...]
  transfers between devices with their start and end apart: 8 -> 0, of which waited for: 3 -> 0; matrix products, arithmetic and copies ran while one was open for 12% -> 0% of each run, Pallas kernels for 18% -> 0%
where the time goes in v3:
time: 563 us; the launch traced here: 552 us
  Pallas kernels  534 us (95%)
  local copies, waits for them, and re-layouts  9.45 us (2%)
  other arithmetic  7.77 us (1%)
    pallas_call x1, Pallas kernels, backward(): pl.pallas_call(functools.partial(backward_kernel, n, length, heads, hid),...  296 us
    pallas_call x1, Pallas kernels, forward(): pl.pallas_call(functools.partial(forward_kernel, n, length), out_shape=[j...  238 us

profile of v3, /device:TPU:8, one launch (start us, length us, event | category | flops | bytes accessed | tf_op | source)
XLA Modules:
  0.0 552.4 jit_solution(12954194326110073233)
XLA Ops:
  0.6 0.8 broadcast_select_fusion.2
  1.5 0.7 fusion.2
  2.1 0.6 broadcast_in_dim.19.small
  2.7 1.3 broadcast_in_dim.21.seg
  4.0 237.5 %forward.1 = (bf16[2048,768]{1,0:T(8,128)(2,1)}, bf16[256,2048]{1,0:T(8,128)(2,1)}, bf16[2048,1280]{1,0:T(8,128)(2,1)}, bf16[640,2048]{1,0:T(8,128)(2,1)}, bf16[...) custom-call(bf16[256,512]{1,0:T(8,128)(2,1)} %wq.1, ...), custom_call_target="tpu_custom_call" | custom-call | tf_op jit(solution)/shard_map/forward/pallas_call | solution.py:645
  241.6 296.5 %backward.1 = (bf16[256,2048]{1,0:T(8,128)(2,1)}, f32[256,2048]{1,0:T(8,128)}, bf16[2,256,1920]{2,1,0:T(8,128)(2,1)}, bf16[2,2,256,512]{3,2,1,0:T(8,128)(2,1)}, ...) custom-call(bf16[2048,1280]{1,0:T(8,128)(2,1)} %get-tuple-element.30, ...), custom_call_target="tpu_custom_call" | custom-call | tf_op jit(solution)/shard_map/backward/pallas_call | solution.py:1224
  538.1 0.7 reduce_sum.9
  538.8 0.5 slice.102
  539.3 0.6 broadcast_select_fusion
  539.9 1.4 slice_bitcast_fusion.7
  541.2 0.0 copy-start.1
  541.3 0.1 convert_bitcast_fusion.1
  541.3 1.0 copy.25
  542.3 0.9 maximum_convert_fusion.4
  543.2 0.9 maximum_convert_fusion.3
  544.0 0.9 maximum_convert_fusion.2
  544.9 0.0 copy-done.1
  544.9 0.9 slice_bitcast_fusion.1
  545.8 0.0 copy-start.2
  545.8 0.1 convert_bitcast_fusion
  545.9 1.5 copy.26
  547.3 0.0 copy-done.2
  547.3 0.0 copy-start.3
  547.3 1.1 maximum_convert_fusion.1
  548.5 0.0 copy-start
  548.5 1.1 maximum_convert_fusion
  549.6 0.0 copy-done.3
  549.6 1.0 copy.29
  550.6 0.0 copy-done
  550.6 1.3 copy.30
Async XLA Ops:
  541.2 3.6 copy-start.1
  545.8 1.6 copy-start.2
  547.3 2.3 copy-start.3
  548.5 2.1 copy-start

commit v4 on v3

--- a/solution.py
+++ b/solution.py
@@ -118,26 +118,32 @@
         self.start_x()
         self.start_y()
 
+    def onward(self, *steps):
+        for i, after in steps:
+            self.copy(i).wait_recv()
+            if after:
+                self.copy(after).start()
+            self.copy(i + 7).start()
+
     def forward(self):
-        self.copy(0).wait_recv()
-        self.copy(3).start()
-        self.copy(7).start()
-        self.copy(1).wait_recv()
-        self.copy(5).start()
-        self.copy(8).start()
+        self.onward((0, 3), (1, 5))
 
     def forward_core(self):
-        for i in (2, 4, 3, 5):
+        self.onward((2, 0), (4, 0), (3, 0), (5, 0))
+
+    def land(self, *pieces):
+        for i in pieces:
             self.copy(i).wait_recv()
-            self.copy(i + 7).start()
-
-    def finish(self):
-        for i in range(6, 13):
-            self.copy(i).wait_recv()
+
+    def sent(self):
         for i in range(13):
             self.copy(i).wait_send()
         own = block_of(self.me.x, self.me.k, self.me.y)
         pltpu.make_async_copy(self.own, self.out.at[own], self.local).wait()
+
+    def finish(self):
+        self.land(*range(6, 13))
+        self.sent()
 
 
 def gather_sems():
@@ -191,7 +197,7 @@
         for name in (("ay0", "bx0"), ("ay1",), ("bx1",))[j]:
             self.copy(name).start()
 
-    def loop(self, make, send=True):
+    def loop(self, make, send=True, first=0, last=4, hooks=()):
         def ready(j):
             self.core_copy(j).wait_recv()
             if j < 2:
@@ -217,9 +223,15 @@
                 def _():
                     ready(i)
 
+            for i, hook in hooks:
+
+                @pl.when(j == i)
+                def _():
+                    hook()
+
             return carry
 
-        lax.fori_loop(0, 4, body, 0)
+        lax.fori_loop(first, last, body, 0)
 
     def second(self):
         self.copy("ay0").wait_recv()
@@ -306,34 +318,37 @@
     def own(self, yy):
         self.send(self.me.z, yy, {True: None, False: None}, True)
 
+    def came(self, s):
+        z, n = self.me.z, self.n
+        return (
+            (True, z - s, z - s >= 0, z + 1 <= n - 1),
+            (False, z + s, z + s <= n - 1, z >= 1),
+        )
+
     def pump(self, s, yy):
-        z, n = self.me.z, self.n
-        for right in (True, False):
-            t = z - s if right else z + s
-            here = (z - s >= 0) if right else (z + s <= n - 1)
-            on = (z + 1 <= n - 1) if right else (z >= 1)
-
-            @pl.when(here)
+        for right, t, here, on in self.came(s):
+
+            @pl.when(here & on)
             def _():
                 for copy in self.copies(t, yy, right):
                     copy.wait_recv()
-
-            if s < n - 1:
-
-                @pl.when(here & on)
-                def _():
-                    for copy in self.copies(t, yy, right):
-                        copy.start()
+                    copy.start()
+
+    def land(self, yys):
+        for s in range(1, self.n):
+            for yy in yys:
+                for right, t, here, on in self.came(s):
+
+                    @pl.when(here & jnp.logical_not(on))
+                    def _():
+                        for copy in self.copies(t, yy, right):
+                            copy.wait_recv()
 
     def finish(self):
-        z, n = self.me.z, self.n
         for yy in range(2):
-            self.send(z, yy, {True: None, False: None}, False)
-            for s in range(1, n - 1):
-                for right in (True, False):
-                    t = z - s if right else z + s
-                    here = (z - s >= 0) if right else (z + s <= n - 1)
-                    on = (z + 1 <= n - 1) if right else (z >= 1)
+            self.send(self.me.z, yy, {True: None, False: None}, False)
+            for s in range(1, self.n):
+                for right, t, here, on in self.came(s):
 
                     @pl.when(here & on)
                     def _():
@@ -346,20 +361,22 @@
 
 
 def forward_kernel(
-    n, length, wq, wk, wv, wo, wg, wu, wd, cot, small, seg, xin,
-    wqkv, wof, wgu, wdf, a1, qkv, o, p, mid, a2all, gall, gain1, gain2,
-    smalls, segs, segt, xv, wqkv_v, wo_v, qkv_v, o_v, toep, pbuf, a2,
-    peer_out, mine, core_in, ra_y, rb_x, ra_x, rb_y,
-    y_send, y_recv, y_local, s_send, s_recv, s2_send, s2_recv, s_local, c_local, p_sem, red_send, red_recv,
+    n, length, wq, wk, wv, wo, wg, wu, wd, cot, xin, seg_row, gain_a, gain_f, table_row,
+    wqkv, wof, wg1, wd1, wg2, wd2, a1, qkv, o, p, mid, a2all, gall, m1, dgu1, gwf1, gain1, gain2,
+    small, seg, smalls, segs, segt, xv, wqkv_v, wo_v, qkv_v, o_v, toep, pbuf, a2, wg1_v, wd1_v, gw_v, acc,
+    y_send, y_recv, y_local, s_send, s_recv, s2_send, s2_recv, s_local, c_local, p_sem, f_sem,
     *rest,
 ):
-    attn_sems, ffn_sems, x_sems, g_sems = rest[0:3], rest[3:6], rest[6:9], rest[9:12]
+    red_scratch, f1_sems, f2_sems, in_sems, wo_sems = rest[0:9], rest[9:12], rest[12:15], rest[15:18], rest[18:21]
+    x_sems, g_sems, a_sems = rest[21:24], rest[24:27], rest[27:30]
     me = Place()
     z, y = me.z, me.y
     rows, width = xin.shape
     piece_rows = wq.shape[0]
     heads = wq.shape[1] // 2
     hid = wg.shape[1] // 2
+    h1 = wd1.shape[0]
+    h2 = hid - h1
     group = [
         me.device(x=ox, k=ok, y=oy)
         for ox in (me.x, 1 - me.x)
@@ -368,6 +385,18 @@
     ][1:]
     others = [me.device(z=lax.rem(z + s, n)) for s in range(1, n)]
     greet(group + others)
+    small[...] = jnp.zeros_like(small)
+    share = gain_a.shape[1]
+    for yy in range(2):
+
+        @pl.when(y == yy)
+        def _():
+            for i, ref in enumerate((gain_a, gain_f)):
+                at = i * 128 + yy * share
+                small[:, at : at + share] = jnp.broadcast_to(ref[...].astype(F32), (8, share))
+
+    small[:, 256 : 256 + table_row.shape[1]] = jnp.broadcast_to(table_row[...].astype(F32), (8, table_row.shape[1]))
+    seg[...] = jnp.broadcast_to(seg_row[...], seg.shape)
 
     def piece(t, yy):
         return pl.ds(pl.multiple_of((t * 2 + yy) * piece_rows, piece_rows), piece_rows)
@@ -376,15 +405,19 @@
 
     def y_copies(yh):
         col = pl.ds(pl.multiple_of(yh * heads, heads), heads)
-        fcol = pl.ds(pl.multiple_of(yh * hid, hid), hid)
+        at1 = pl.ds(pl.multiple_of(yh * hid, 128), h1)
+        at2 = pl.ds(pl.multiple_of(yh * hid + h1, 128), h2)
         return [
             (wq.at[:, col], wqkv.at[row, pl.ds(0, heads)]),
             (wk.at[:, col], wqkv.at[row, pl.ds(heads, heads)]),
             (wv.at[:, col], wqkv.at[row, pl.ds(2 * heads, heads)]),
             (wo.at[col, :], wof.at[:, row]),
-            (wg.at[:, fcol], wgu.at[row, pl.ds(0, hid)]),
-            (wu.at[:, fcol], wgu.at[row, pl.ds(hid, hid)]),
-            (wd.at[fcol, :], wdf.at[:, row]),
+            (wg.at[:, at1], wg1.at[row, pl.ds(0, h1)]),
+            (wu.at[:, at1], wg1.at[row, pl.ds(h1, h1)]),
+            (wd.at[at1, :], wd1.at[:, row]),
+            (wg.at[:, at2], wg2.at[row, pl.ds(0, h2)]),
+            (wu.at[:, at2], wg2.at[row, pl.ds(h2, h2)]),
+            (wd.at[at2, :], wd2.at[:, row]),
         ]
 
     sends = [
@@ -399,8 +432,10 @@
         remote(small, smalls.at[me_small], s_send.at[i], s_recv.at[i], dev) for i, dev in enumerate(group)
     ]
     seg_send = remote(seg, segs.at[y], s_send.at[7], s_recv.at[7], me.y_peer())
-    attn = Line(me, n, lambda t, yy: (wqkv.at[piece(t, yy), :], wof.at[:, piece(t, yy)]), *attn_sems)
-    ffn = Line(me, n, lambda t, yy: (wgu.at[piece(t, yy), :], wdf.at[:, piece(t, yy)]), *ffn_sems)
+    attn = Line(me, n, lambda t, yy: (wqkv.at[piece(t, yy), :],), *in_sems)
+    attn_o = Line(me, n, lambda t, yy: (wof.at[:, piece(t, yy)],), *wo_sems)
+    f1 = Line(me, n, lambda t, yy: (wg1.at[piece(t, yy), :], wd1.at[:, piece(t, yy)]), *f1_sems)
+    f2 = Line(me, n, lambda t, yy: (wg2.at[piece(t, yy), :], wd2.at[:, piece(t, yy)]), *f2_sems)
     xact = ActGather(me, xin, xv, *x_sems)
     gact = ActGather(me, cot, gall, *g_sems)
 
@@ -413,6 +448,8 @@
         copy.start()
     seg_send.start()
     xact.start_x()
+    for i in range(4, 10):
+        keeps[i].start()
     for i in range(4):
         keeps[i].wait()
     attn.own(y)
@@ -420,9 +457,6 @@
         sends[i].wait_recv()
     attn.own(1 - y)
     xact.start_y()
-    for i in range(4, 7):
-        keeps[i].start()
-        sends[i].start()
     small_local.wait()
     for copy in small_sends:
         copy.wait_recv()
@@ -430,10 +464,13 @@
     small_z = [remote(block8, block8, s2_send.at[i], s2_recv.at[i], dev) for i, dev in enumerate(others)]
     for copy in small_z:
         copy.start()
-    xact.forward()
+    xact.onward((0, 3))
     attn.pump(1, y)
     attn.pump(1, 1 - y)
-    xact.forward_core()
+    xact.onward((1, 5))
+    for i in range(4, 10):
+        sends[i].start()
+    gact.start()
 
     for copy in small_z:
         copy.wait_recv()
@@ -446,48 +483,13 @@
         wide = jnp.concatenate([segs[s]] * 16, axis=0).astype(F32)
         segt[s] = wide.T
     attn.pump(2, y)
-    xact.finish()
-    gact.start_x()
-    gact.start_y()
-
-    def norm_rows(i, carry):
-        r = pl.ds(pl.multiple_of(lax.rem(i, rows // 16) * 16, 16), 16)
-        b = i // (rows // 16)
-        xf = xv[b, r, :].astype(F32)
-        inv = lax.rsqrt(jnp.mean(xf * xf, axis=-1, keepdims=True) + EPSILON)
-        xv[b, r, :] = (xf * inv * gain1[...]).astype(BF)
-        return carry
-
-    lax.fori_loop(0, 8 * rows // 16, norm_rows, 0)
-    a1_out = pltpu.make_async_copy(xv, a1, c_local.at[0])
-    a1_out.start()
+    xact.onward((2, 0), (4, 0))
     attn.pump(2, 1 - y)
+    attn_o.own(y)
+    attn_o.own(1 - y)
     for i in range(4, 7):
         keeps[i].wait()
-    ffn.own(y)
-    for i in range(4, 7):
-        sends[i].wait_recv()
-    ffn.own(1 - y)
-    gact.forward()
-    for yy in (y, 1 - y):
-        for s in range(3, n):
-            attn.pump(s, yy)
-    w_in = pltpu.make_async_copy(wqkv, wqkv_v, c_local.at[1])
-    wo_in = pltpu.make_async_copy(wof, wo_v, c_local.at[2])
-    w_in.start()
-    wo_in.start()
-    w_in.wait()
-
-    def project(b, carry):
-        r = pl.ds(pl.multiple_of(b * rows, rows), rows)
-        qkv_v[r, :] = jnp.dot(xv[b], wqkv_v[...], preferred_element_type=F32).astype(BF)
-        return carry
-
-    lax.fori_loop(0, 8, project, 0)
-    qkv_out = pltpu.make_async_copy(qkv_v, qkv, c_local.at[3])
-    qkv_out.start()
-    gact.forward_core()
-
+    f1.own(y)
     offset = lax.broadcasted_iota(jnp.int32, (NB, 2 * length), 1) - length
     far = jnp.abs(offset)
     bucket = jnp.where(far < 8, far, 8 + sum((far >= t).astype(jnp.int32) for t in THRESHOLDS))
@@ -496,6 +498,47 @@
     table = smalls[:, 0, 256:384]
     lane = lax.broadcasted_iota(jnp.int32, (NB, 128), 1)
     local_heads = heads // DH
+    for lh in range(local_heads):
+        head = (me.c * 2 + y) * local_heads + lh
+        value = jnp.sum(jnp.where(lane == head, table, 0.0), axis=1, keepdims=True)
+        fvec = jnp.sum(jnp.where(own_bucket, value, 0.0), axis=0, keepdims=True)
+        toep[lh] = pltpu.roll(jnp.broadcast_to(fvec, (TQ, 2 * length)), 0, 1, stride=1, stride_axis=0)
+    xact.onward((3, 0), (5, 0))
+    xact.finish()
+
+    def norm_rows(i, carry):
+        r = pl.ds(pl.multiple_of(lax.rem(i, rows // 16) * 16, 16), 16)
+        b = i // (rows // 16)
+        xf = xv[b, r, :].astype(F32)
+        inv = lax.rsqrt(jnp.mean(xf * xf, axis=-1, keepdims=True) + EPSILON)
+        xv[b, r, :] = (xf * inv * gain1[...]).astype(BF)
+        return carry
+
+    lax.fori_loop(0, 4 * rows // 16, norm_rows, 0)
+    for i in range(4, 7):
+        sends[i].wait_recv()
+    f1.own(1 - y)
+    attn_o.pump(1, y)
+    attn_o.pump(1, 1 - y)
+    lax.fori_loop(4 * rows // 16, 8 * rows // 16, norm_rows, 0)
+    a1_out = pltpu.make_async_copy(xv, a1, c_local.at[0])
+    a1_out.start()
+    attn_o.pump(2, y)
+    attn_o.pump(2, 1 - y)
+    attn.land((y, 1 - y))
+    w_in = pltpu.make_async_copy(wqkv, wqkv_v, c_local.at[1])
+    w_in.start()
+    w_in.wait()
+
+    def project(b, carry):
+        r = pl.ds(pl.multiple_of(b * rows, rows), rows)
+        qkv_v[r, :] = jnp.dot(xv[b], wqkv_v[...], preferred_element_type=F32).astype(BF)
+        return carry
+
+    lax.fori_loop(0, 8, project, 0)
+    qkv_out = pltpu.make_async_copy(qkv_v, qkv, c_local.at[3])
+    qkv_out.start()
+    f1.pump(1, y)
     tiles = length // TQ
 
     def p_copy(slot, head, t):
@@ -503,61 +546,81 @@
             pbuf.at[slot], p.at[head, pl.ds(t * TQ, TQ)], p_sem.at[slot]
         )
 
-    def head_pair(hp):
-        for h in range(2):
-            head = (me.c * 2 + y) * local_heads + hp * 2 + h
-            value = jnp.sum(jnp.where(lane == head, table, 0.0), axis=1, keepdims=True)
-            fvec = jnp.sum(jnp.where(own_bucket, value, 0.0), axis=0, keepdims=True)
-            toep[h] = pltpu.roll(jnp.broadcast_to(fvec, (TQ, 2 * length)), 0, 1, stride=1, stride_axis=0)
-
-        def sequence(s, carry):
-            for h in range(2):
-                first = hp * 128
-                base = pl.multiple_of(s * length, length)
-                kh = qkv_v[pl.ds(base, length), heads + first + h * DH : heads + first + (h + 1) * DH]
-                vh = qkv_v[pl.ds(base, length), 2 * heads + first + h * DH : 2 * heads + first + (h + 1) * DH]
-                head = s * local_heads + hp * 2 + h
-                for t in range(tiles):
-                    r = pl.ds(pl.multiple_of(base + t * TQ, TQ), TQ)
-                    qt = qkv_v[r, first + h * DH : first + (h + 1) * DH]
-                    same = segt[s, t * TQ : (t + 1) * TQ, 0:1] == segs[s, 0:1, :].astype(F32)
+    def sequence(s, fresh, between):
+        base = pl.multiple_of(s * length, length)
+        seq = pl.ds(base, length)
+
+        def head_pair(hp, carry):
+            def lanes(part):
+                return pl.ds(pl.multiple_of(part * heads + hp * 2 * DH, 128), 2 * DH)
+
+            k2 = qkv_v[seq, lanes(1)]
+            v2 = qkv_v[seq, lanes(2)]
+            for t in range(tiles):
+                r = pl.ds(pl.multiple_of(base + t * TQ, TQ), TQ)
+                q2 = qkv_v[r, lanes(0)]
+                same = segt[s, t * TQ : (t + 1) * TQ, 0:1] == segs[s, 0:1, :].astype(F32)
+                outs = []
+                for h in range(2):
+                    cut = slice(h * DH, (h + 1) * DH)
                     pb, ot = softmax_tile(
-                        qt, kh, vh, toep[h, :, length - t * TQ : 2 * length - t * TQ], same
+                        q2[:, cut], k2[:, cut], v2[:, cut],
+                        toep[hp * 2 + h, :, length - t * TQ : 2 * length - t * TQ], same,
                     )
-                    slot = t % 2
-                    if hp or h or t >= 2:
-                        p_copy(slot, head, t).wait()
+                    head = s * local_heads + hp * 2 + h
+                    if fresh and t == 0:
+
+                        @pl.when(hp > 0)
+                        def _():
+                            p_copy(h, head, t).wait()
                     else:
-
-                        @pl.when(s > 0)
-                        def _():
-                            p_copy(slot, head, t).wait()
-
-                    pbuf[slot] = pb
-                    p_copy(slot, head, t).start()
-                    o_v[r, first + h * DH : first + (h + 1) * DH] = ot
+                        p_copy(h, head, t).wait()
+                    pbuf[h] = pb
+                    p_copy(h, head, t).start()
+                    outs.append(ot)
+                o_v[r, pl.ds(pl.multiple_of(hp * 2 * DH, 128), 2 * DH)] = jnp.concatenate(outs, axis=1)
+
+            @pl.when(hp == 0)
+            def _():
+                between()
+
             return carry
 
-        lax.fori_loop(0, 2, sequence, 0)
-
-    head_pair(0)
-    ffn.pump(1, y)
-    head_pair(1)
-    for slot in range(2):
-        p_copy(slot, 0, slot).wait()
-    o_out = pltpu.make_async_copy(o_v, o, c_local.at[4])
-    o_out.start()
-    ffn.pump(1, 1 - y)
-    wo_in.wait()
+        lax.fori_loop(0, local_heads // 2, head_pair, 0)
 
     def attn_term(block, i):
         r = pl.ds(pl.multiple_of(block * rows, rows), rows)
         return jnp.dot(o_v[r, :], wo_v[...], preferred_element_type=F32).astype(BF)
 
-    red = ActReduce(me, peer_out, core_in, mine, ra_y, rb_x, ra_x, rb_y, red_send, red_recv)
-    red.loop(attn_term)
+    red = ActReduce(me, *red_scratch)
+    def beside_first():
+        f1.pump(1, 1 - y)
+        gact.forward()
+
+    def beside_second():
+        for i in range(7, 10):
+            keeps[i].wait()
+            sends[i].wait_recv()
+        f2.own(y)
+        f2.own(1 - y)
+        gact.forward_core()
+
+    sequence(1 - y, True, beside_first)
+    attn_o.land((y, 1 - y))
+    wo_in = pltpu.make_async_copy(wof, wo_v, c_local.at[2])
+    wo_in.start()
+    f1.pump(2, y)
+    f1.pump(2, 1 - y)
+    wo_in.wait()
+    red.loop(attn_term, first=0, last=2)
+    sequence(y, False, beside_second)
+    for slot in range(2):
+        p_copy(slot, 0, 0).wait()
+    o_out = pltpu.make_async_copy(o_v, o, c_local.at[4])
+    o_out.start()
+    red.loop(attn_term, first=2, last=4)
     red.second()
-    ffn.pump(2, y)
+    f2.pump(1, y)
     red.arrive()
 
     half = rows // 2
@@ -572,20 +635,123 @@
             return carry
 
         lax.fori_loop(0, half // 16, body, 0)
+    aact = ActGather(me, a2, a2all, *a_sems)
+    aact.start()
+    f2.pump(1, 1 - y)
+    f1.land((y, 1 - y))
+
+    def fetch(src, dst, i):
+        return pltpu.make_async_copy(src, dst, f_sem.at[i])
+
+    a1_out.wait()
+    fetch(wg1, wg1_v, 0).start()
+    fetch(wd1, wd1_v, 1).start()
     gact.finish()
-    aact = ActGather(me, a2, a2all, *rest[12:15])
-    aact.start_x()
-    aact.start_y()
+
+    def block_at(i):
+        ox, oy = red.place(3 - i // 2)
+        return block_of(ox, jnp.where(i % 2 == 0, me.k, 1 - me.k), oy)
+
+    def load_rows(i):
+        slot = lax.rem(i, 2)
+        b = block_at(i)
+        return fetch(a2all.at[b], xv.at[slot], 2 + slot), fetch(gall.at[b], xv.at[2 + slot], 4 + slot)
+
+    def first_units(j, last, carry):
+        b = block_at(j)
+
+        @pl.when(j < last)
+        def _():
+            for copy in load_rows(j + 1):
+                copy.start()
+
+        for copy in load_rows(j):
+            copy.wait()
+        slot = lax.rem(j, 2)
+        acc[:, 0 : 2 * h1] = jnp.dot(xv[slot], wg1_v[...], preferred_element_type=F32)
+        acc[:, 2 * h1 : 3 * h1] = lax.dot_general(
+            xv[2 + slot], wd1_v[...], (((1,), (1,)), ((), ())), preferred_element_type=F32
+        )
+
+        def body(i, inner):
+            rr = pl.ds(pl.multiple_of(i * 16, 16), 16)
+            tr = pl.ds(pl.multiple_of(b * rows + i * 16, 16), 16)
+            gate, up, gm = acc[rr, 0:h1], acc[rr, h1 : 2 * h1], acc[rr, 2 * h1 : 3 * h1]
+            gelu, slope = gelu_parts(gate)
+            wqkv_v[tr, 0:h1] = (gm * up * slope).astype(BF)
+            wqkv_v[tr, h1 : 2 * h1] = (gm * gelu).astype(BF)
+            wqkv_v[tr, 2 * h1 : 3 * h1] = (gelu * up).astype(BF)
+            return inner
+
+        lax.fori_loop(0, rows // 16, body, 0)
+        return carry
+
+    def units(first, last):
+        for copy in load_rows(first):
+            copy.start()
+        lax.fori_loop(first, last, lambda j, carry: first_units(j, last - 1, carry), 0)
+
+    pltpu.make_async_copy(a2, a2all.at[block_at(0)], a_sems[2]).wait()
+    fetch(wg1, wg1_v, 0).wait()
+    fetch(wd1, wd1_v, 1).wait()
+    aact.land(6)
+    units(0, 2)
     aact.forward()
-    ffn.pump(2, 1 - y)
-    aact.forward_core()
-    aact.finish()
+    f2.pump(2, y)
+    aact.onward((2, 0), (4, 0))
+    aact.land(7, 8, 9, 11)
+    units(2, 6)
+    aact.onward((3, 0), (5, 0))
+    aact.land(10, 12)
+    f2.pump(2, 1 - y)
+    units(6, 8)
     red.finish()
-    for yy in (y, 1 - y):
-        for s in range(3, n):
-            ffn.pump(s, yy)
-    attn.finish()
-    ffn.finish()
+    kept = [fetch(wqkv_v.at[:, pl.ds(0, 2 * h1)], dgu1, 0), fetch(wqkv_v.at[:, pl.ds(2 * h1, h1)], m1, 1)]
+    for copy in kept:
+        copy.start()
+
+    def load_columns(i):
+        slot = lax.rem(i, 2)
+        at = pl.ds(pl.multiple_of(i * rows, rows), rows)
+        here = pl.ds(pl.multiple_of(slot * rows, rows), rows)
+        there = pl.ds(pl.multiple_of((2 + slot) * rows, rows), rows)
+        return (
+            fetch(a2all.at[:, :, at], xv.at[:, :, here], 2 + slot),
+            fetch(gall.at[:, :, at], xv.at[:, :, there], 4 + slot),
+        )
+
+    for copy in load_columns(0):
+        copy.start()
+
+    def first_grads(i, carry):
+        @pl.when(i < 2 * n - 1)
+        def _():
+            for copy in load_columns(i + 1):
+                copy.start()
+
+        for copy in load_columns(i):
+            copy.wait()
+        slot = lax.rem(i, 2)
+        here = pl.ds(pl.multiple_of(slot * rows, rows), rows)
+        there = pl.ds(pl.multiple_of((2 + slot) * rows, rows), rows)
+        gw_v[i, :, 0 : 2 * h1] = lax.dot_general(
+            xv[:, :, here].reshape(8 * rows, rows), wqkv_v[:, 0 : 2 * h1], (((0,), (0,)), ((), ())),
+            preferred_element_type=F32,
+        ).astype(BF)
+        gw_v[i, :, 2 * h1 : 3 * h1] = lax.dot_general(
+            xv[:, :, there].reshape(8 * rows, rows), wqkv_v[:, 2 * h1 : 3 * h1], (((0,), (0,)), ((), ())),
+            preferred_element_type=F32,
+        ).astype(BF)
+        return carry
+
+    lax.fori_loop(0, 2 * n, first_grads, 0)
+    kept.append(fetch(gw_v, gwf1, 2))
+    kept[2].start()
+    for i in range(13):
+        aact.copy(i).wait_send()
+    f2.land((y, 1 - y))
+    for line in (attn, attn_o, f1, f2):
+        line.finish()
     for copy in small_sends:
         copy.wait_send()
     for copy in small_z:
@@ -593,66 +759,72 @@
     seg_send.wait_send()
     for copy in sends:
         copy.wait_send()
-    a1_out.wait()
     qkv_out.wait()
     o_out.wait()
-
-
-def forward(n, wq, wk, wv, wo, wg, wu, wd, cot, small, seg, xin):
+    for copy in kept:
+        copy.wait()
+
+
+def forward(n, h1, wq, wk, wv, wo, wg, wu, wd, cot, xin, seg_row, gain_a, gain_f, table_row):
     rows, width = xin.shape
     heads = wq.shape[1] // 2
     hid = wg.shape[1] // 2
-    length = seg.shape[1]
+    length = seg_row.shape[1]
+    small, seg = (8, 384), (8, length)
     local_heads = heads // DH
+    tokens = 8 * rows
     shapes = [
         ((width, 3 * heads), BF),
         ((heads, width), BF),
-        ((width, 2 * hid), BF),
-        ((hid, width), BF),
+        ((width, 2 * h1), BF),
+        ((h1, width), BF),
+        ((width, 2 * (hid - h1)), BF),
+        ((hid - h1, width), BF),
         ((8, rows, width), BF),
-        ((8 * rows, 3 * heads), BF),
-        ((8 * rows, heads), BF),
+        ((tokens, 3 * heads), BF),
+        ((tokens, heads), BF),
         ((2 * local_heads, length, length), BF),
         ((rows, width), F32),
         ((8, rows, width), BF),
         ((8, rows, width), BF),
+        ((tokens, h1), BF),
+        ((tokens, 2 * h1), BF),
+        ((2 * n, rows, 3 * h1), BF),
         ((1, width), F32),
         ((1, width), F32),
     ]
-    half = rows // 2
     scratch = [
-        pltpu.VMEM((8 * n,) + small.shape, F32),
-        pltpu.VMEM((2,) + seg.shape, jnp.int32),
+        pltpu.VMEM(small, F32),
+        pltpu.VMEM(seg, jnp.int32),
+        pltpu.VMEM((8 * n,) + small, F32),
+        pltpu.VMEM((2,) + seg, jnp.int32),
         pltpu.VMEM((2, length, 128), F32),
         pltpu.VMEM((8, rows, width), BF),
         pltpu.VMEM((width, 3 * heads), BF),
         pltpu.VMEM((heads, width), BF),
-        pltpu.VMEM((8 * rows, 3 * heads), BF),
-        pltpu.VMEM((8 * rows, heads), BF),
-        pltpu.VMEM((2, TQ, 2 * length), F32),
+        pltpu.VMEM((tokens, 3 * heads), BF),
+        pltpu.VMEM((tokens, heads), BF),
+        pltpu.VMEM((local_heads, TQ, 2 * length), F32),
         pltpu.VMEM((2, TQ, length), BF),
         pltpu.VMEM((rows, width), BF),
-        pltpu.VMEM((2, rows, width), BF),
-        pltpu.VMEM((4, rows, width), BF),
-        pltpu.VMEM((4, rows, width), BF),
-        pltpu.VMEM((2, half, width), BF),
-        pltpu.VMEM((2, half, width), BF),
-        pltpu.VMEM((half, width), BF),
-        pltpu.VMEM((half, width), BF),
-        DMA((7,)), DMA((7,)), DMA((7,)), DMA((8,)), DMA((8,)), DMA((n - 1,)), DMA((n - 1,)), DMA((2,)),
-        DMA((5,)), DMA((2,)), DMA((10,)), DMA((10,)),
-    ] + line_sems(n, 2) * 2 + gather_sems() * 3
+        pltpu.VMEM((width, 2 * h1), BF),
+        pltpu.VMEM((h1, width), BF),
+        pltpu.VMEM((2 * n, rows, 3 * h1), BF),
+        pltpu.VMEM((rows, 3 * h1), F32),
+        DMA((10,)), DMA((10,)), DMA((10,)), DMA((8,)), DMA((8,)), DMA((n - 1,)), DMA((n - 1,)), DMA((2,)),
+        DMA((5,)), DMA((2,)), DMA((6,)),
+    ] + reduce_scratch(rows, width) + line_sems(n, 2) * 2 + line_sems(n, 1) * 2 + gather_sems() * 3
     return pl.pallas_call(
         functools.partial(forward_kernel, n, length),
         out_shape=[jax.ShapeDtypeStruct(s, d) for s, d in shapes],
-        in_specs=[ANY] * 10 + [VM],
-        out_specs=[ANY] * 8 + [VM] + [ANY] * 2 + [VM] * 2,
+        in_specs=[ANY] * 8 + [VM] * 5,
+        out_specs=[ANY] * 10 + [VM] + [ANY] * 5 + [VM] * 2,
         scratch_shapes=scratch,
         compiler_params=pltpu.CompilerParams(
-            collective_id=0, has_side_effects=True, vmem_limit_bytes=60 << 20
+            collective_id=0, has_side_effects=True, vmem_limit_bytes=64 << 20
         ),
         name="forward",
-    )(wq, wk, wv, wo, wg, wu, wd, cot, small, seg, xin)
+    )(wq, wk, wv, wo, wg, wu, wd, cot, xin, seg_row, gain_a, gain_f, table_row)
 
 
 class LineSum:
@@ -768,15 +940,18 @@
 
 
 def backward_kernel(
-    n, length, heads, hid,
-    wgu, wdf, a2all, gall, p, a1, qkv, o, wqkv, wof, hidden, mid, cot, gain1, gain2,
-    out, gx, fo, ao, sums, dzall, f_left, f_right, a_left, a_right,
-    wgu_v, wd_v, row_a, row_g, col_a, col_g, m, dgu, gwf, stage, gmid, dz, wqkv_v,
+    n, length, heads, hid, h1,
+    wg1, wd1, wg2, wd2, m1, dgu1, gwf1, a2all, gall, p, a1, qkv, o, wqkv, wof, hidden, mid, cot, gain1, gain2,
+    out, gx, fo1, fo2, ao, bo, co, sums, dzall, e_left, e_right, f_left, f_right, a_left, a_right,
+    b_left, b_right, c_left, c_right,
+    wgu_v, wd_v, row_a, row_b, row_g, col_a, col_g, m, dgu, gw1, gw2, stage, gmid, dz, wqkv_v,
     pbuf, acc, dkt, dvt, diag, gg1, gg2, sv, sv_in, sv_z, free,
     load, p_sem, stage_sem, y_send, y_recv, y_local, sv_send, sv_recv, sz_send, sz_recv,
     *rest,
 ):
-    red_scratch, dz_sems, f_sems, a_sems = rest[:9], rest[9:12], rest[12:16], rest[16:20]
+    red_scratch, dz_sems = rest[:9], rest[9:12]
+    e_sems, f_sems, a_sems, b_sems, c_sems = (rest[i : i + 4] for i in range(12, 32, 4))
+    h2 = hid - h1
     me = Place()
     z, y = me.z, me.y
     rows, width = cot.shape
@@ -795,19 +970,34 @@
         return pltpu.make_async_copy(src, dst, load.at[i])
 
     red = ActReduce(me, *red_scratch)
-    fsum = LineSum(me, n, lambda pc: [gwf.at[pc]], f_left, f_right, [stage], f_sems, stage_sem)
+    stage1 = stage.at[:, pl.ds(0, 3 * h1)]
+    esum = LineSum(me, n, lambda pc: [gw1.at[pc]], e_left, e_right, [stage1], e_sems, stage_sem)
+    fsum = LineSum(me, n, lambda pc: [gw2.at[pc]], f_left, f_right, [stage], f_sems, stage_sem)
+    order = (1 - y, y)
 
     def piece(pc):
         return pl.ds(pl.multiple_of(pc * rows, rows), rows)
 
-    asum = LineSum(
-        me, n,
-        lambda pc: [dgu.at[piece(pc), pl.ds(3 * heads, 2 * heads)], m.at[piece(pc), pl.ds(0, 2 * heads)]],
-        a_left, a_right, [stage.at[:, pl.ds(0, 2 * heads)], stage.at[:, pl.ds(2 * heads, 2 * heads)]],
-        a_sems, stage_sem,
-    )
-
-    w_loads = [fetch(wgu, wgu_v, 0), fetch(wdf, wd_v, 1)]
+    def line_sum(view, left, right, width, sems):
+        return LineSum(me, n, lambda pc: [view(pc)], left, right, [stage.at[:, pl.ds(0, width)]], sems, stage_sem)
+
+    pair = 3 * 2 * DH
+    osum = line_sum(lambda pc: m.at[piece(pc), pl.ds(0, heads)], a_left, a_right, heads, a_sems)
+    bsum = line_sum(lambda pc: dgu.at[piece(pc), pl.ds(3 * heads, pair)], b_left, b_right, pair, b_sems)
+    csum = line_sum(lambda pc: m.at[piece(pc), pl.ds(heads, pair)], c_left, c_right, pair, c_sems)
+
+    def piece_at(i):
+        return far_first(n, z, i // 2) * 2 + jnp.where(i % 2 == 0, 1 - y, y)
+
+    w_loads = [
+        fetch(gwf1, gw1, 0),
+        fetch(wg2, wgu_v.at[:, pl.ds(2 * h1, 2 * h2)], 1),
+        fetch(wd2, wd_v.at[pl.ds(h1, h2), :], 6),
+        fetch(wg1, wgu_v.at[:, pl.ds(0, 2 * h1)], 7),
+        fetch(dgu1, dgu.at[:, pl.ds(0, 2 * h1)], 8),
+        fetch(wd1, wd_v.at[pl.ds(0, h1), :], 9),
+        fetch(m1, m.at[:, pl.ds(0, h1)], 10),
+    ]
     for copy in w_loads:
         copy.start()
 
@@ -818,20 +1008,29 @@
 
     fetch(a2all.at[block_at(0)], row_a, 2).start()
     fetch(gall.at[block_at(0)], row_g, 3).start()
-    for copy in w_loads:
+    w_loads[0].wait()
+
+    def first_slots(i, carry):
+        pc = piece_at(i)
+        esum.first(pc // 2, pc % 2)
+        return carry
+
+    lax.fori_loop(0, 2 * n, first_slots, 0)
+    for copy in w_loads[1:]:
         copy.wait()
+
 
     def make_ffn(block, i):
         fetch(a2all.at[block], row_a, 2).wait()
-        acc[:, 0 : 2 * hid] = jnp.dot(row_a[...], wgu_v[...], preferred_element_type=F32)
+        acc[:, 0 : 2 * h2] = jnp.dot(row_a[...], wgu_v[:, 2 * h1 : 2 * hid], preferred_element_type=F32)
 
         @pl.when(i < 7)
         def _():
             fetch(a2all.at[block_at(i + 1)], row_a, 2).start()
 
         fetch(gall.at[block], row_g, 3).wait()
-        acc[:, 2 * hid : 3 * hid] = lax.dot_general(
-            row_g[...], wd_v[...], (((1,), (1,)), ((), ())), preferred_element_type=F32
+        acc[:, 2 * h2 : 3 * h2] = lax.dot_general(
+            row_g[...], wd_v[h1:hid, :], (((1,), (1,)), ((), ())), preferred_element_type=F32
         )
 
         @pl.when(i < 7)
@@ -841,11 +1040,11 @@
         def body(r, carry):
             rr = pl.ds(pl.multiple_of(r * 16, 16), 16)
             tr = pl.ds(pl.multiple_of(block * rows + r * 16, 16), 16)
-            gate, up, gm = acc[rr, 0:hid], acc[rr, hid : 2 * hid], acc[rr, 2 * hid : 3 * hid]
+            gate, up, gm = acc[rr, 0:h2], acc[rr, h2 : 2 * h2], acc[rr, 2 * h2 : 3 * h2]
             gelu, slope = gelu_parts(gate)
-            m[tr, :] = (gelu * up).astype(BF)
-            dgu[tr, 0:hid] = (gm * up * slope).astype(BF)
-            dgu[tr, hid : 2 * hid] = (gm * gelu).astype(BF)
+            m[tr, h1:hid] = (gelu * up).astype(BF)
+            dgu[tr, 2 * h1 : 2 * h1 + h2] = (gm * up * slope).astype(BF)
+            dgu[tr, 2 * h1 + h2 : 2 * hid] = (gm * gelu).astype(BF)
             return carry
 
         lax.fori_loop(0, rows // 16, body, 0)
@@ -853,44 +1052,48 @@
             dgu[piece(block), :], wgu_v[...], (((1,), (1,)), ((), ())), preferred_element_type=F32
         ).astype(BF)
 
-    red.loop(make_ffn)
+    red.loop(make_ffn, hooks=((1, lambda: esum.pump(2, order[0])), (2, lambda: esum.pump(2, order[1]))))
+    esum.pump(1, order[0])
 
     fetch(wof, row_g, 3).start()
-
-    def piece_at(i):
-        return far_first(n, z, i // 2) * 2 + jnp.where(i % 2 == 0, 1 - y, y)
 
     def columns(ref, i):
         return ref.at[:, :, piece(piece_at(i))]
 
-    fetch(columns(a2all, 0), col_a, 4).start()
-    fetch(columns(gall, 0), col_g, 5).start()
+    def load_columns(left, right, i):
+        slot = lax.rem(i, 2)
+        return fetch(columns(left, i), col_a.at[slot], 11 + slot), fetch(columns(right, i), col_g.at[slot], 13 + slot)
+
+    def next_columns(left, right, i):
+        @pl.when(i < 2 * n - 1)
+        def _():
+            for copy in load_columns(left, right, i + 1):
+                copy.start()
+
+        for copy in load_columns(left, right, i):
+            copy.wait()
+
+    for copy in load_columns(a2all, gall, 0):
+        copy.start()
 
     def ffn_grads(i, carry):
         pc = piece_at(i)
-        fetch(columns(a2all, i), col_a, 4).wait()
-        gwf[pc, :, 0 : 2 * hid] = lax.dot_general(
-            col_a[...].reshape(8 * rows, rows), dgu[...], (((0,), (0,)), ((), ())), preferred_element_type=F32
+        slot = lax.rem(i, 2)
+        next_columns(a2all, gall, i)
+        gw2[pc, :, 0 : 2 * h2] = lax.dot_general(
+            col_a[slot].reshape(8 * rows, rows), dgu[:, 2 * h1 : 2 * hid], (((0,), (0,)), ((), ())),
+            preferred_element_type=F32,
         ).astype(BF)
-
-        @pl.when(i < 2 * n - 1)
-        def _():
-            fetch(columns(a2all, i + 1), col_a, 4).start()
-
-        fetch(columns(gall, i), col_g, 5).wait()
-        gwf[pc, :, 2 * hid : 3 * hid] = lax.dot_general(
-            col_g[...].reshape(8 * rows, rows), m[...], (((0,), (0,)), ((), ())), preferred_element_type=F32
+        gw2[pc, :, 2 * h2 : 3 * h2] = lax.dot_general(
+            col_g[slot].reshape(8 * rows, rows), m[:, h1:hid], (((0,), (0,)), ((), ())),
+            preferred_element_type=F32,
         ).astype(BF)
-
-        @pl.when(i < 2 * n - 1)
-        def _():
-            fetch(columns(gall, i + 1), col_g, 5).start()
-
         fsum.first(pc // 2, pc % 2)
         return carry
 
     lax.fori_loop(0, n, ffn_grads, 0)
     red.second()
+    esum.pump(1, order[1])
     fetch(qkv, wgu_v.at[:, pl.ds(0, 3 * heads)], 0).start()
     fetch(o, wgu_v.at[:, pl.ds(3 * heads, heads)], 6).start()
     red.arrive()
@@ -930,32 +1133,60 @@
         return jnp.dot(m[piece(block), :], wd_v[...], preferred_element_type=F32).astype(BF)
 
     red.loop(make_out, send=False)
-    order = (1 - y, y)
+    def swap(views, box, i):
+        out = remote(views(z * 2 + 1 - y)[0], box.at[y], y_send.at[i], y_recv.at[i], me.y_peer())
+        keep = pltpu.make_async_copy(views(z * 2 + y)[0], box.at[y], y_local.at[i])
+        return out, keep
+
+    lines = (esum, fsum, osum, bsum, csum)
+    swaps = [swap(line.views, box, i) for i, (line, box) in enumerate(zip(lines, (fo1, fo2, ao, bo, co)))]
+
+    def settle(i):
+        lines[i].own(order[0])
+        swaps[i][0].start()
+        lines[i].own(order[1])
+        swaps[i][1].start()
+
     fsum.pump(2, order[0])
     act.forward_core()
     for j in range(3):
         red.first_sends(j)
+    settle(0)
     act.finish()
+
+    fetch(wof, row_g, 3).wait()
+    slots = ((row_a, 2), (row_b, 4))
+    for b in range(2):
+        fetch(dzall.at[b], *slots[b]).start()
+
+    def project_back(i, carry):
+        for b, (buffer, sem) in enumerate(slots):
+            block = i * 2 + b
+            fetch(dzall.at[block], buffer, sem).wait()
+            wgu_v[piece(block), 4 * heads : 5 * heads] = lax.dot_general(
+                buffer[...], row_g[...], (((1,), (1,)), ((), ())), preferred_element_type=F32
+            ).astype(BF)
+
+            @pl.when(i < 3)
+            def _():
+                fetch(dzall.at[block + 2], buffer, sem).start()
+
+        return carry
+
+    lax.fori_loop(0, 4, project_back, 0)
     fsum.pump(2, order[1])
-
-    fetch(wof, row_g, 3).wait()
-    fetch(dzall.at[0], row_a, 2).start()
-
-    def project_back(b, carry):
-        fetch(dzall.at[b], row_a, 2).wait()
-        wgu_v[piece(b), 4 * heads : 5 * heads] = lax.dot_general(
-            row_a[...], row_g[...], (((1,), (1,)), ((), ())), preferred_element_type=F32
-        ).astype(BF)
-
-        @pl.when(b < 7)
-        def _():
-            fetch(dzall.at[b + 1], row_a, 2).start()
-
-        return carry
-
-    lax.fori_loop(0, 8, project_back, 0)
     fetch(hidden, row_a, 2).start()
-    fetch(wqkv, wqkv_v, 1).start()
+    w_parts = [
+        fetch(
+            wqkv.at[:, pl.ds(part * heads + hp * 2 * DH, 2 * DH)],
+            wqkv_v.at[:, pl.ds(hp * pair + part * 2 * DH, 2 * DH)],
+            15 + hp * 3 + part,
+        )
+        for hp in range(2)
+        for part in range(3)
+    ]
+    for copy in w_parts:
+        copy.start()
     fetch(qkv, wgu_v.at[:, pl.ds(0, 3 * heads)], 0).wait()
     fetch(o, wgu_v.at[:, pl.ds(3 * heads, heads)], 6).wait()
     diag[...] = jnp.zeros_like(diag)
@@ -972,6 +1203,7 @@
             p_load(head0, 1, 1).start()
             for h in range(2):
                 lo = hp * 128 + h * DH
+                to = hp * pair + h * DH
                 seq = pl.ds(base, length)
                 kh = wgu_v[seq, heads + lo : heads + lo + DH]
                 vh = wgu_v[seq, 2 * heads + lo : 2 * heads + lo + DH]
@@ -986,7 +1218,7 @@
                     dp = lax.dot_general(doh, vh, (((1,), (1,)), ((), ())), preferred_element_type=F32)
                     pf = pb.astype(F32)
                     ds = (pf * (dp - jnp.sum(pf * dp, axis=-1, keepdims=True))).astype(BF)
-                    dgu[r, lo : lo + DH] = jnp.dot(ds, kh, preferred_element_type=F32).astype(BF)
+                    dgu[r, to : to + DH] = jnp.dot(ds, kh, preferred_element_type=F32).astype(BF)
                     ck = lax.dot_general(qh, ds, (((0,), (0,)), ((), ())), preferred_element_type=F32)
                     cv = lax.dot_general(doh, pb, (((0,), (0,)), ((), ())), preferred_element_type=F32)
                     u = h * tiles + t + 2
@@ -999,8 +1231,8 @@
                         dkt[...] += ck
                         dvt[...] += cv
                     acc[:, length - t * TQ : 2 * length - t * TQ] += ds.astype(F32)
-                dgu[seq, heads + lo : heads + lo + DH] = dkt[...].T.astype(BF)
-                dgu[seq, 2 * heads + lo : 2 * heads + lo + DH] = dvt[...].T.astype(BF)
+                dgu[seq, to + 2 * DH : to + 3 * DH] = dkt[...].T.astype(BF)
+                dgu[seq, to + 4 * DH : to + 5 * DH] = dvt[...].T.astype(BF)
                 c = TQ // 2
                 while c >= 8:
                     acc[0:c, :] += pltpu.roll(acc[c : 2 * c, :], 2 * length - c, 1)
@@ -1010,43 +1242,39 @@
 
         lax.fori_loop(0, 2, sequence, 0)
 
+    def pair_grads(hp, line, with_o):
+        for copy in load_columns(a1, dzall, 0):
+            copy.start()
+
+        def body(i, carry):
+            pc = piece_at(i)
+            slot = lax.rem(i, 2)
+            next_columns(a1, dzall, i)
+            if with_o:
+                m[piece(pc), 0:heads] = lax.dot_general(
+                    col_g[slot].reshape(8 * rows, rows), wgu_v[:, 3 * heads : 4 * heads], (((0,), (0,)), ((), ())),
+                    preferred_element_type=F32,
+                ).astype(BF)
+                osum.first(pc // 2, pc % 2)
+            part = lax.dot_general(
+                col_a[slot].reshape(8 * rows, rows), dgu[:, hp * pair : (hp + 1) * pair], (((0,), (0,)), ((), ())),
+                preferred_element_type=F32,
+            ).astype(BF)
+            line.views(pc)[0][...] = part
+            line.first(pc // 2, pc % 2)
+            return carry
+
+        lax.fori_loop(0, 2 * n, body, 0)
+
     head_pair(0)
     fsum.pump(1, order[0])
     red.second()
+    pair_grads(0, bsum, True)
+    fsum.pump(1, order[1])
     head_pair(1)
-    fsum.pump(1, order[1])
-
-    fetch(columns(a1, 0), col_a, 4).start()
-    fetch(columns(dzall, 0), col_g, 5).start()
-
-    def attn_grads(i, carry):
-        pc = piece_at(i)
-        fetch(columns(a1, i), col_a, 4).wait()
-        part = lax.dot_general(
-            col_a[...].reshape(8 * rows, rows), dgu[:, 0 : 3 * heads], (((0,), (0,)), ((), ())),
-            preferred_element_type=F32,
-        ).astype(BF)
-        dgu[piece(pc), 3 * heads : 5 * heads] = part[:, 0 : 2 * heads]
-        m[piece(pc), 0:heads] = part[:, 2 * heads : 3 * heads]
-
-        @pl.when(i < 2 * n - 1)
-        def _():
-            fetch(columns(a1, i + 1), col_a, 4).start()
-
-        fetch(columns(dzall, i), col_g, 5).wait()
-        m[piece(pc), heads : 2 * heads] = lax.dot_general(
-            col_g[...].reshape(8 * rows, rows), wgu_v[:, 3 * heads : 4 * heads], (((0,), (0,)), ((), ())),
-            preferred_element_type=F32,
-        ).astype(BF)
-
-        @pl.when(i < 2 * n - 1)
-        def _():
-            fetch(columns(dzall, i + 1), col_g, 5).start()
-
-        asum.first(pc // 2, pc % 2)
-        return carry
-
-    lax.fori_loop(0, 2 * n, attn_grads, 0)
+    for yy in order:
+        osum.pump(2, yy)
+        bsum.pump(2, yy)
 
     red.arrive()
     for h in range(2):
@@ -1060,7 +1288,8 @@
     red.finish()
     release()
     claim()
-    fetch(wqkv, wqkv_v, 1).wait()
+    for copy in w_parts:
+        copy.wait()
 
     def make_ga1(block, i):
         return lax.dot_general(
@@ -1068,6 +1297,13 @@
         ).astype(BF)
 
     red.loop(make_ga1)
+    pair_grads(1, csum, False)
+    red.second()
+    settle(1)
+    for yy in order:
+        osum.pump(1, yy)
+        bsum.pump(1, yy)
+        csum.pump(2, yy)
 
     offset = lax.broadcasted_iota(jnp.int32, (NB, 2 * length), 1) - length
     away = jnp.abs(offset)
@@ -1082,9 +1318,8 @@
             line = line + pltpu.roll(diag[lh, r : r + 1, :], 2 * length - r, 1)
         value = jnp.sum(jnp.where(own_bucket, line, 0.0), axis=1, keepdims=True)
         table = jnp.where(lane == (me.c * 2 + y) * local_heads + lh, value, table)
-    red.second()
-
-    fsum.own(order[0])
+    for yy in order:
+        csum.pump(1, yy)
     red.arrive()
     gg1[...] = jnp.zeros_like(gg1)
     fetch(hidden, row_a, 2).wait()
@@ -1120,28 +1355,8 @@
     for copy in sv_copies:
         copy.start()
 
-    def swap(line, slot, views, box, i, wait):
-        copies = []
-        for v, (dst, sem) in enumerate(zip(box, range(i, i + len(box)))):
-            copies.append(
-                remote(views(z * 2 + 1 - y)[v], dst.at[y], y_send.at[sem], y_recv.at[sem], me.y_peer())
-            )
-        keeps = [
-            pltpu.make_async_copy(views(z * 2 + y)[v], dst.at[y], y_local.at[sem])
-            for v, (dst, sem) in enumerate(zip(box, range(i, i + len(box))))
-        ]
-        return copies, keeps
-
-    ao_boxes = [ao.at[0], ao.at[1]]
-    f_out, f_keep = swap(fsum, None, fsum.views, [fo], 0, None)
-    a_out, a_keep = swap(asum, None, asum.views, ao_boxes, 1, None)
-    for copy in f_out:
-        copy.start()
-    fsum.own(order[1])
-    for copy in f_keep:
-        copy.start()
-    for yy in order:
-        asum.pump(2, yy)
+    settle(2)
+    settle(3)
     for copy in sv_copies:
         copy.wait_recv()
     me_g = me.c * 2 + y
@@ -1155,56 +1370,58 @@
     ]
     for copy in z_copies:
         copy.start()
-    for yy in order:
-        asum.pump(1, yy)
-    asum.own(order[0])
-    for copy in a_out:
-        copy.start()
-    asum.own(order[1])
-    for copy in a_keep:
-        copy.start()
+    settle(4)
     for copy in z_copies:
         copy.wait_recv()
     total = sv_z[0, z]
     for s in range(1, n):
         total = total + sv_z[s, 0]
     sums[...] = total
-    for copy in f_out + a_out:
-        copy.wait()
-    for copy in f_keep + a_keep:
-        copy.wait()
+    for pair_of in swaps:
+        for copy in pair_of:
+            copy.wait()
     for copy in sv_copies + z_copies:
         copy.wait_send()
-    fsum.finish()
-    asum.finish()
-
-
-def backward(n, length, heads, hid, wgu, wdf, a2all, gall, p, a1, qkv, o, wqkv, wof, hidden, mid, cot, gain1, gain2):
+    for line in lines:
+        line.finish()
+
+
+def backward(n, length, heads, hid, h1, *arrays):
+    cot = arrays[-3]
     rows, width = cot.shape
     tokens = 8 * rows
+    h2 = hid - h1
+    pair = 3 * 2 * DH
     shapes = [
         ((rows, width), BF),
         ((rows, width), F32),
-        ((2, rows, 3 * hid), BF),
-        ((2, 2, rows, 2 * heads), BF),
+        ((2, rows, 3 * h1), BF),
+        ((2, rows, 3 * h2), BF),
+        ((2, rows, heads), BF),
+        ((2, rows, pair), BF),
+        ((2, rows, pair), BF),
         ((8, 384), F32),
         ((8, rows, width), BF),
-        ((n, 2, 1, rows, 3 * hid), BF),
-        ((n, 2, 1, rows, 3 * hid), BF),
-        ((n, 2, 2, rows, 2 * heads), BF),
-        ((n, 2, 2, rows, 2 * heads), BF),
-    ]
+        ((n, 2, 1, rows, 3 * h1), BF),
+        ((n, 2, 1, rows, 3 * h1), BF),
+        ((n, 2, 1, rows, 3 * h2), BF),
+        ((n, 2, 1, rows, 3 * h2), BF),
+        ((n, 2, 1, rows, heads), BF),
+        ((n, 2, 1, rows, heads), BF),
+    ] + [((n, 2, 1, rows, pair), BF)] * 4
     scratch = [
         pltpu.VMEM((width, 2 * hid), BF),
         pltpu.VMEM((hid, width), BF),
         pltpu.VMEM((rows, width), BF),
         pltpu.VMEM((rows, width), BF),
-        pltpu.VMEM((8, rows, rows), BF),
-        pltpu.VMEM((8, rows, rows), BF),
+        pltpu.VMEM((rows, width), BF),
+        pltpu.VMEM((2, 8, rows, rows), BF),
+        pltpu.VMEM((2, 8, rows, rows), BF),
         pltpu.VMEM((tokens, hid), BF),
         pltpu.VMEM((tokens, 2 * hid), BF),
-        pltpu.VMEM((2 * n, rows, 3 * hid), BF),
-        pltpu.VMEM((rows, 3 * hid), BF),
+        pltpu.VMEM((2 * n, rows, 3 * h1), BF),
+        pltpu.VMEM((2 * n, rows, 3 * h2), BF),
+        pltpu.VMEM((rows, 3 * h2), BF),
         pltpu.VMEM((rows, width), F32),
         pltpu.VMEM((rows, width), BF),
         pltpu.VMEM((width, 3 * heads), BF),
@@ -1219,19 +1436,19 @@
         pltpu.VMEM((7, n, 8, 384), F32),
         pltpu.VMEM((n, n, 8, 384), F32),
         pltpu.SemaphoreType.REGULAR((3,)),
-        DMA((7,)), DMA((2,)), DMA, DMA((3,)), DMA((3,)), DMA((3,)), DMA((7,)), DMA((7,)), DMA((n - 1,)), DMA((n - 1,)),
-    ] + reduce_scratch(rows, width) + gather_sems() + [DMA((n, 2, 1))] * 4 + [DMA((n, 2, 2))] * 4
+        DMA((21,)), DMA((2,)), DMA, DMA((5,)), DMA((5,)), DMA((5,)), DMA((7,)), DMA((7,)), DMA((n - 1,)), DMA((n - 1,)),
+    ] + reduce_scratch(rows, width) + gather_sems() + [DMA((n, 2, 1))] * 20
     return pl.pallas_call(
-        functools.partial(backward_kernel, n, length, heads, hid),
+        functools.partial(backward_kernel, n, length, heads, hid, h1),
         out_shape=[jax.ShapeDtypeStruct(s, d) for s, d in shapes],
-        in_specs=[ANY] * 11 + [VM] * 4,
-        out_specs=[VM, VM, ANY, ANY, VM] + [ANY] * 5,
+        in_specs=[ANY] * 16 + [VM] * 4,
+        out_specs=[VM, VM] + [ANY] * 5 + [VM] + [ANY] * 11,
         scratch_shapes=scratch,
         compiler_params=pltpu.CompilerParams(
             collective_id=1, has_side_effects=True, vmem_limit_bytes=64 << 20
         ),
         name="backward",
-    )(wgu, wdf, a2all, gall, p, a1, qkv, o, wqkv, wof, hidden, mid, cot, gain1, gain2)
+    )(*arrays)
 
 
 def on_device(
@@ -1245,27 +1462,69 @@
     hid = w_gate.shape[1] // 2
     share = attn_gain.shape[0]
     y = lax.axis_index("fsdp")
-    lanes = lambda v: jnp.where(y == 0, jnp.pad(v, (0, 128 - share)), jnp.pad(v, (128 - share, 0))).astype(F32)
-    packed = jnp.concatenate([lanes(attn_gain), lanes(ffn_gain), jnp.pad(rel_table.astype(F32), (0, 128 - H))])
-    small = jnp.broadcast_to(packed[None, :], (8, packed.shape[0]))
-    seg = jnp.broadcast_to(segment_ids, (8, length))
-    wqkv, wo, wgu, wd, a1, qkv, o, p, mid, a2all, gall, gain1, gain2 = forward(
-        n, w_query, w_key, w_value, w_attn_out, w_gate, w_up, w_down, cot, small, seg, xin
-    )
-    out, gx, fo, ao, sums = backward(
-        n, length, heads, hid, wgu, wd, a2all, gall, p, a1, qkv, o, wqkv, wo, xin, mid, cot, gain1, gain2
-    )[:5]
-    sides = lambda part: jnp.concatenate([part[0], part[1]], axis=1).astype(F32)
-    g_gate, g_up = sides(fo[:, :, :hid]), sides(fo[:, :, hid : 2 * hid])
-    g_down = sides(fo[:, :, 2 * hid :]).T
-    g_q, g_k = sides(ao[0, :, :, :heads]), sides(ao[0, :, :, heads:])
-    g_v, g_o = sides(ao[1, :, :, :heads]), sides(ao[1, :, :, heads:]).T
+    h1 = 256
+    h2 = hid - h1
+    wqkv, wo, wg1, wd1, wg2, wd2, a1, qkv, o, p, mid, a2all, gall, m1, dgu1, gwf1, gain1, gain2 = forward(
+        n, h1, w_query, w_key, w_value, w_attn_out, w_gate, w_up, w_down, cot, xin, segment_ids,
+        attn_gain[None], ffn_gain[None], rel_table[None],
+    )
+    out, gx, fo1, fo2, ao, bo, co, sums = backward(
+        n, length, heads, hid, h1, wg1, wd1, wg2, wd2, m1, dgu1, gwf1, a2all, gall, p, a1, qkv, o, wqkv, wo,
+        xin, mid, cot, gain1, gain2,
+    )[:8]
+    out, gx, g_q, g_k, g_v, g_o, g_gate, g_up, g_down = finish(h1, out, gx, fo1, fo2, ao, bo, co)
     line = jnp.sum(sums, axis=0)
     half_of = lambda v: jnp.where(y == 0, v[:share], v[128 - share :])
     return (
         out[None], gx[None], half_of(line[:128]), g_q, g_k, g_v, g_o, line[256 : 256 + H],
         half_of(line[128:256]), g_gate, g_up, g_down,
     )
+
+
+def finish_kernel(h1, out_in, gx_in, *refs):
+    sources, (out, gx, g_q, g_k, g_v, g_o, g_gate, g_up, g_down) = refs[:5], refs[5:14]
+    fo1, fo2, ao, bo, co = held = refs[14:19]
+    sem = refs[19]
+    loads = [pltpu.make_async_copy(src, dst, sem.at[i + 2]) for i, (src, dst) in enumerate(zip(sources, held))]
+    moves = [
+        pltpu.make_async_copy(src, dst, sem.at[i]) for i, (src, dst) in enumerate(((out_in, out), (gx_in, gx)))
+    ]
+    for copy in loads + moves:
+        copy.start()
+    for copy in loads:
+        copy.wait()
+    heads = ao.shape[2]
+    h2 = fo2.shape[2] // 3
+    hid = h1 + h2
+    for yy in range(2):
+        for part, ref in enumerate((g_q, g_k, g_v)):
+            ref[:, yy * heads : yy * heads + 128] = bo[yy, :, part * 128 : part * 128 + 128].astype(F32)
+            ref[:, yy * heads + 128 : yy * heads + 256] = co[yy, :, part * 128 : part * 128 + 128].astype(F32)
+        g_o[yy * heads : (yy + 1) * heads, :] = ao[yy].astype(F32).T
+        for part, ref in enumerate((g_gate, g_up)):
+            ref[:, yy * hid : yy * hid + h1] = fo1[yy, :, part * h1 : (part + 1) * h1].astype(F32)
+            ref[:, yy * hid + h1 : (yy + 1) * hid] = fo2[yy, :, part * h2 : (part + 1) * h2].astype(F32)
+        g_down[yy * hid : yy * hid + h1, :] = fo1[yy, :, 2 * h1 : 3 * h1].astype(F32).T
+        g_down[yy * hid + h1 : (yy + 1) * hid, :] = fo2[yy, :, 2 * h2 : 3 * h2].astype(F32).T
+    for copy in moves:
+        copy.wait()
+
+
+def finish(h1, out, gx, fo1, fo2, ao, bo, co):
+    rows = out.shape[0]
+    heads = ao.shape[2]
+    hid = h1 + fo2.shape[2] // 3
+    shapes = [(rows, 2 * heads)] * 3 + [(2 * heads, rows)] + [(rows, 2 * hid)] * 2 + [(2 * hid, rows)]
+    return pl.pallas_call(
+        functools.partial(finish_kernel, h1),
+        out_shape=[jax.ShapeDtypeStruct(out.shape, BF), jax.ShapeDtypeStruct(gx.shape, F32)]
+        + [jax.ShapeDtypeStruct(s, F32) for s in shapes],
+        in_specs=[ANY] * 7,
+        out_specs=[ANY] * 2 + [VM] * 7,
+        scratch_shapes=[pltpu.VMEM(part.shape, BF) for part in (fo1, fo2, ao, bo, co)] + [DMA((7,))],
+        compiler_params=pltpu.CompilerParams(vmem_limit_bytes=32 << 20),
+        name="finish",
+    )(out, gx, fo1, fo2, ao, bo, co)
 
 
 QB = 512

time: 563 us -> 523 us (0.929)
  Pallas kernels: 534 us -> 503 us
  other arithmetic: 7.77 us -> 0.61 us
    pallas_call x1 -> x2, Pallas kernels: 296 us -> 270 us  [the longest x1 265 us: backward(): pl.pallas_call(functools.partial(backward_kernel, n, length, heads, hid,...]
where the time goes in v4:
time: 523 us; the launch traced here: 513 us
  Pallas kernels  503 us (96%)
  local copies, waits for them, and re-layouts  8.67 us (2%)
    pallas_call x1, Pallas kernels, backward(): pl.pallas_call(functools.partial(backward_kernel, n, length, heads, hid,...  265 us
    pallas_call x1, Pallas kernels, forward(): pl.pallas_call(functools.partial(forward_kernel, n, length), out_shape=[j...  232 us

profile of v4, /device:TPU:8, one launch (start us, length us, event | category | flops | bytes accessed | tf_op | source)
XLA Modules:
  0.0 513.0 jit_solution(4116023748889875264)
XLA Ops:
  0.6 232.3 %forward.1 = (bf16[2048,768]{1,0:T(8,128)(2,1)}, bf16[256,2048]{1,0:T(8,128)(2,1)}, bf16[2048,512]{1,0:T(8,128)(2,1)}, bf16[256,2048]{1,0:T(8,128)(2,1)}, bf16[2...) custom-call(bf16[256,512]{1,0:T(8,128)(2,1)} %wq.1, ...), custom_call_target="tpu_custom_call" | custom-call | tf_op jit(solution)/shard_map/forward/pallas_call | solution.py:817
  233.0 265.2 %backward.1 = (bf16[256,2048]{1,0:T(8,128)(2,1)}, f32[256,2048]{1,0:T(8,128)}, bf16[2,256,768]{2,1,0:T(8,128)(2,1)}, bf16[2,256,1152]{2,1,0:T(8,128)(2,1)}, bf16...) custom-call(bf16[2048,512]{1,0:T(8,128)(2,1)} %get-tuple-element.47., ...), custom_call_target="tpu_custom_call" | custom-call | tf_op jit(solution)/shard_map/backward/pallas_call | solution.py:1441
  498.2 0.0 copy-start
  498.2 1.6 copy-done
  499.8 0.0 copy-start.1
  499.8 1.3 copy-done.1
  501.1 0.0 copy-start.2
  501.1 1.2 copy-done.2
  502.3 0.0 copy-start.3
  502.3 1.1 copy-done.3
  503.4 0.0 copy-start.4
  503.4 1.0 copy-done.4
  504.4 0.0 copy-start.5
  504.4 1.0 copy-done.5
  505.4 0.0 copy-start.6
  505.4 0.9 copy-done.6
  506.4 0.0 copy-start.7
  506.4 5.0 finish.1
  511.4 0.0 copy-done.7
  511.4 0.6 broadcast_select_fusion
  512.0 0.5 slice.23
  (1 shorter events, 0.0 us)
Async XLA Ops:
  498.2 1.6 copy-start
  499.8 1.3 copy-start.1
  501.1 1.2 copy-start.2
  502.3 1.1 copy-start.3
  503.4 1.0 copy-start.4
  504.4 1.0 copy-start.5
  505.4 0.9 copy-start.6
  506.4 5.0 copy-start.7

commit v5 on v4

--- a/solution.py
+++ b/solution.py
@@ -216,12 +216,13 @@
 
             self.peer_out[j % 2] = make(block_of(ox, 1 - self.me.k, oy), 2 * j)
             self.core_copy(j).start()
-            self.mine[j] = make(block_of(ox, self.me.k, oy), 2 * j + 1)
             for i in range(3):
 
                 @pl.when(j == i + 1)
                 def _():
                     ready(i)
+
+            self.mine[j] = make(block_of(ox, self.me.k, oy), 2 * j + 1)
 
             for i, hook in hooks:
 
@@ -363,7 +364,7 @@
 def forward_kernel(
     n, length, wq, wk, wv, wo, wg, wu, wd, cot, xin, seg_row, gain_a, gain_f, table_row,
     wqkv, wof, wg1, wd1, wg2, wd2, a1, qkv, o, p, mid, a2all, gall, m1, dgu1, gwf1, gain1, gain2,
-    small, seg, smalls, segs, segt, xv, wqkv_v, wo_v, qkv_v, o_v, toep, pbuf, a2, wg1_v, wd1_v, gw_v, acc,
+    st_in, st_o, st_1, st_d1, st_2, st_d2, small, seg, smalls, segs, segt, xv, wqkv_v, wo_v, qkv_v, o_v, toep, pbuf, a2, wg1_v, wd1_v, gw_v, acc,
     y_send, y_recv, y_local, s_send, s_recv, s2_send, s2_recv, s_local, c_local, p_sem, f_sem,
     *rest,
 ):
@@ -424,7 +425,26 @@
         remote(src, dst, y_send.at[i], y_recv.at[i], me.y_peer())
         for i, (src, dst) in enumerate(y_copies(1 - y))
     ]
-    keeps = [pltpu.make_async_copy(src, dst, y_local.at[i]) for i, (src, dst) in enumerate(y_copies(y))]
+    staged = [
+        st_in.at[:, pl.ds(0, heads)],
+        st_in.at[:, pl.ds(heads, heads)],
+        st_in.at[:, pl.ds(2 * heads, heads)],
+        st_o,
+        st_1.at[:, pl.ds(0, h1)],
+        st_1.at[:, pl.ds(h1, h1)],
+        st_d1,
+        st_2.at[:, pl.ds(0, h2)],
+        st_2.at[:, pl.ds(h2, h2)],
+        st_d2,
+    ]
+    takes = [
+        pltpu.make_async_copy(src, mid_ref, y_local.at[i])
+        for i, ((src, dst), mid_ref) in enumerate(zip(y_copies(y), staged))
+    ]
+    keeps = [
+        pltpu.make_async_copy(mid_ref, dst, y_local.at[i])
+        for i, ((src, dst), mid_ref) in enumerate(zip(y_copies(y), staged))
+    ]
     me_small = z * 8 + me.c * 2 + y
     small_local = pltpu.make_async_copy(small, smalls.at[me_small], s_local.at[0])
     seg_local = pltpu.make_async_copy(seg, segs.at[y], s_local.at[1])
@@ -440,7 +460,7 @@
     gact = ActGather(me, cot, gall, *g_sems)
 
     for i in range(4):
-        keeps[i].start()
+        takes[i].start()
         sends[i].start()
     small_local.start()
     seg_local.start()
@@ -449,6 +469,9 @@
     seg_send.start()
     xact.start_x()
     for i in range(4, 10):
+        takes[i].start()
+    for i in range(10):
+        takes[i].wait()
         keeps[i].start()
     for i in range(4):
         keeps[i].wait()
@@ -680,7 +703,7 @@
             gelu, slope = gelu_parts(gate)
             wqkv_v[tr, 0:h1] = (gm * up * slope).astype(BF)
             wqkv_v[tr, h1 : 2 * h1] = (gm * gelu).astype(BF)
-            wqkv_v[tr, 2 * h1 : 3 * h1] = (gelu * up).astype(BF)
+            qkv_v[tr, 0:h1] = (gelu * up).astype(BF)
             return inner
 
         lax.fori_loop(0, rows // 16, body, 0)
@@ -692,6 +715,7 @@
         lax.fori_loop(first, last, lambda j, carry: first_units(j, last - 1, carry), 0)
 
     pltpu.make_async_copy(a2, a2all.at[block_at(0)], a_sems[2]).wait()
+    qkv_out.wait()
     fetch(wg1, wg1_v, 0).wait()
     fetch(wd1, wd1_v, 1).wait()
     aact.land(6)
@@ -706,7 +730,7 @@
     f2.pump(2, 1 - y)
     units(6, 8)
     red.finish()
-    kept = [fetch(wqkv_v.at[:, pl.ds(0, 2 * h1)], dgu1, 0), fetch(wqkv_v.at[:, pl.ds(2 * h1, h1)], m1, 1)]
+    kept = [fetch(wqkv_v.at[:, pl.ds(0, 2 * h1)], dgu1, 0), fetch(qkv_v.at[:, pl.ds(0, h1)], m1, 1)]
     for copy in kept:
         copy.start()
 
@@ -739,7 +763,7 @@
             preferred_element_type=F32,
         ).astype(BF)
         gw_v[i, :, 2 * h1 : 3 * h1] = lax.dot_general(
-            xv[:, :, there].reshape(8 * rows, rows), wqkv_v[:, 2 * h1 : 3 * h1], (((0,), (0,)), ((), ())),
+            xv[:, :, there].reshape(8 * rows, rows), qkv_v[:, 0:h1], (((0,), (0,)), ((), ())),
             preferred_element_type=F32,
         ).astype(BF)
         return carry
@@ -759,7 +783,6 @@
     seg_send.wait_send()
     for copy in sends:
         copy.wait_send()
-    qkv_out.wait()
     o_out.wait()
     for copy in kept:
         copy.wait()
@@ -794,6 +817,12 @@
         ((1, width), F32),
     ]
     scratch = [
+        pltpu.VMEM((wq.shape[0], 3 * heads), BF),
+        pltpu.VMEM((heads, wo.shape[1]), BF),
+        pltpu.VMEM((wq.shape[0], 2 * h1), BF),
+        pltpu.VMEM((h1, wd.shape[1]), BF),
+        pltpu.VMEM((wq.shape[0], 2 * (hid - h1)), BF),
+        pltpu.VMEM((hid - h1, wd.shape[1]), BF),
         pltpu.VMEM(small, F32),
         pltpu.VMEM(seg, jnp.int32),
         pltpu.VMEM((8 * n,) + small, F32),
@@ -817,7 +846,7 @@
     return pl.pallas_call(
         functools.partial(forward_kernel, n, length),
         out_shape=[jax.ShapeDtypeStruct(s, d) for s, d in shapes],
-        in_specs=[ANY] * 8 + [VM] * 5,
+        in_specs=[ANY] * 7 + [VM] * 6,
         out_specs=[ANY] * 10 + [VM] + [ANY] * 5 + [VM] * 2,
         scratch_shapes=scratch,
         compiler_params=pltpu.CompilerParams(
@@ -850,20 +879,24 @@
         for copy in self.copies(t, yy, right):
             copy.start()
 
+    def take(self, t, yy, right):
+        slot = 0 if right else 1
+        return pltpu.make_async_copy(self.inbox[right].at[t, yy, 0], self.stage[slot], self.stage_sem.at[slot])
+
+    def open(self, t, yy, right):
+        self.copies(t, yy, right)[0].wait_recv()
+        self.take(t, yy, right).start()
+
     def add(self, t, yy, right):
-        for i, (copy, view) in enumerate(zip(self.copies(t, yy, right), self.views(t * 2 + yy))):
-            copy.wait_recv()
-            stage = self.stage[i]
-            load = pltpu.make_async_copy(self.inbox[right].at[t, yy, i], stage, self.stage_sem)
-            load.start()
-            load.wait()
-
-            def body(r, carry):
-                rr = pl.ds(pl.multiple_of(r * 16, 16), 16)
-                view[rr, :] = (view[rr, :].astype(F32) + stage[rr, :].astype(F32)).astype(BF)
-                return carry
-
-            lax.fori_loop(0, view.shape[0] // 16, body, 0)
+        self.take(t, yy, right).wait()
+        view, stage = self.views(t * 2 + yy)[0], self.stage[0 if right else 1]
+
+        def body(r, carry):
+            rr = pl.ds(pl.multiple_of(r * 16, 16), 16)
+            view[rr, :] = (view[rr, :].astype(F32) + stage[rr, :].astype(F32)).astype(BF)
+            return carry
+
+        lax.fori_loop(0, view.shape[0] // 16, body, 0)
 
     def first(self, t, yy):
         @pl.when((self.me.z == 0) & (t > 0))
@@ -876,27 +909,37 @@
 
     def pump(self, k, yy):
         z, n = self.me.z, self.n
-
-        @pl.when((z + k <= n - 1) & (z > 0))
-        def _():
-            self.add(z + k, yy, True)
-            self.start(z + k, yy, True)
-
-        @pl.when((z - k >= 0) & (z < n - 1))
-        def _():
-            self.add(z - k, yy, False)
-            self.start(z - k, yy, False)
+        sides = (
+            (True, z + k, (z + k <= n - 1) & (z > 0)),
+            (False, z - k, (z - k >= 0) & (z < n - 1)),
+        )
+        for right, t, go in sides:
+
+            @pl.when(go)
+            def _():
+                self.open(t, yy, right)
+
+        for right, t, go in sides:
+
+            @pl.when(go)
+            def _():
+                self.add(t, yy, right)
+                self.start(t, yy, right)
 
     def own(self, yy):
-        z, n = self.me.z, self.n
-
-        @pl.when(z > 0)
-        def _():
-            self.add(z, yy, True)
-
-        @pl.when(z < n - 1)
-        def _():
-            self.add(z, yy, False)
+        z = self.me.z
+        sides = ((True, z > 0), (False, z < self.n - 1))
+        for right, go in sides:
+
+            @pl.when(go)
+            def _():
+                self.open(z, yy, right)
+
+        for right, go in sides:
+
+            @pl.when(go)
+            def _():
+                self.add(z, yy, right)
 
     def finish(self):
         z, n = self.me.z, self.n
@@ -942,15 +985,14 @@
 def backward_kernel(
     n, length, heads, hid, h1,
     wg1, wd1, wg2, wd2, m1, dgu1, gwf1, a2all, gall, p, a1, qkv, o, wqkv, wof, hidden, mid, cot, gain1, gain2,
-    out, gx, fo1, fo2, ao, bo, co, sums, dzall, e_left, e_right, f_left, f_right, a_left, a_right,
-    b_left, b_right, c_left, c_right,
+    out, gx, fo1, fo2, bo, co, sums, dzall, e_left, e_right, f_left, f_right, b_left, b_right, c_left, c_right,
     wgu_v, wd_v, row_a, row_b, row_g, col_a, col_g, m, dgu, gw1, gw2, stage, gmid, dz, wqkv_v,
     pbuf, acc, dkt, dvt, diag, gg1, gg2, sv, sv_in, sv_z, free,
     load, p_sem, stage_sem, y_send, y_recv, y_local, sv_send, sv_recv, sz_send, sz_recv,
     *rest,
 ):
     red_scratch, dz_sems = rest[:9], rest[9:12]
-    e_sems, f_sems, a_sems, b_sems, c_sems = (rest[i : i + 4] for i in range(12, 32, 4))
+    e_sems, f_sems, b_sems, c_sems = (rest[i : i + 4] for i in range(12, 28, 4))
     h2 = hid - h1
     me = Place()
     z, y = me.z, me.y
@@ -970,21 +1012,21 @@
         return pltpu.make_async_copy(src, dst, load.at[i])
 
     red = ActReduce(me, *red_scratch)
-    stage1 = stage.at[:, pl.ds(0, 3 * h1)]
-    esum = LineSum(me, n, lambda pc: [gw1.at[pc]], e_left, e_right, [stage1], e_sems, stage_sem)
-    fsum = LineSum(me, n, lambda pc: [gw2.at[pc]], f_left, f_right, [stage], f_sems, stage_sem)
     order = (1 - y, y)
+
+    def line_sum(view, left, right, width, sems):
+        stages = [stage.at[i, :, pl.ds(0, width)] for i in range(2)]
+        return LineSum(me, n, lambda pc: [view(pc)], left, right, stages, sems, stage_sem)
+
+    esum = line_sum(lambda pc: gw1.at[pc], e_left, e_right, 3 * h1, e_sems)
+    fsum = line_sum(lambda pc: gw2.at[pc], f_left, f_right, 3 * h2, f_sems)
 
     def piece(pc):
         return pl.ds(pl.multiple_of(pc * rows, rows), rows)
 
-    def line_sum(view, left, right, width, sems):
-        return LineSum(me, n, lambda pc: [view(pc)], left, right, [stage.at[:, pl.ds(0, width)]], sems, stage_sem)
-
     pair = 3 * 2 * DH
-    osum = line_sum(lambda pc: m.at[piece(pc), pl.ds(0, heads)], a_left, a_right, heads, a_sems)
-    bsum = line_sum(lambda pc: dgu.at[piece(pc), pl.ds(3 * heads, pair)], b_left, b_right, pair, b_sems)
-    csum = line_sum(lambda pc: m.at[piece(pc), pl.ds(heads, pair)], c_left, c_right, pair, c_sems)
+    bsum = line_sum(lambda pc: m.at[piece(pc), :], b_left, b_right, heads + pair, b_sems)
+    csum = line_sum(lambda pc: dgu.at[piece(pc), pl.ds(3 * heads, pair)], c_left, c_right, pair, c_sems)
 
     def piece_at(i):
         return far_first(n, z, i // 2) * 2 + jnp.where(i % 2 == 0, 1 - y, y)
@@ -1138,8 +1180,8 @@
         keep = pltpu.make_async_copy(views(z * 2 + y)[0], box.at[y], y_local.at[i])
         return out, keep
 
-    lines = (esum, fsum, osum, bsum, csum)
-    swaps = [swap(line.views, box, i) for i, (line, box) in enumerate(zip(lines, (fo1, fo2, ao, bo, co)))]
+    lines = (esum, fsum, bsum, csum)
+    swaps = [swap(line.views, box, i) for i, (line, box) in enumerate(zip(lines, (fo1, fo2, bo, co)))]
 
     def settle(i):
         lines[i].own(order[0])
@@ -1243,24 +1285,38 @@
         lax.fori_loop(0, 2, sequence, 0)
 
     def pair_grads(hp, line, with_o):
-        for copy in load_columns(a1, dzall, 0):
+        def loads(i):
+            slot = lax.rem(i, 2)
+            both = fetch(columns(a1, i), col_a.at[slot], 11 + slot), fetch(columns(dzall, i), col_g.at[slot], 13 + slot)
+            return both if with_o else both[:1]
+
+        for copy in loads(0):
             copy.start()
 
         def body(i, carry):
             pc = piece_at(i)
             slot = lax.rem(i, 2)
-            next_columns(a1, dzall, i)
+
+            @pl.when(i < 2 * n - 1)
+            def _():
+                for copy in loads(i + 1):
+                    copy.start()
+
+            for copy in loads(i):
+                copy.wait()
             if with_o:
                 m[piece(pc), 0:heads] = lax.dot_general(
                     col_g[slot].reshape(8 * rows, rows), wgu_v[:, 3 * heads : 4 * heads], (((0,), (0,)), ((), ())),
                     preferred_element_type=F32,
                 ).astype(BF)
-                osum.first(pc // 2, pc % 2)
             part = lax.dot_general(
                 col_a[slot].reshape(8 * rows, rows), dgu[:, hp * pair : (hp + 1) * pair], (((0,), (0,)), ((), ())),
                 preferred_element_type=F32,
             ).astype(BF)
-            line.views(pc)[0][...] = part
+            if with_o:
+                m[piece(pc), heads : heads + pair] = part
+            else:
+                dgu[piece(pc), 3 * heads : 3 * heads + pair] = part
             line.first(pc // 2, pc % 2)
             return carry
 
@@ -1273,7 +1329,6 @@
     fsum.pump(1, order[1])
     head_pair(1)
     for yy in order:
-        osum.pump(2, yy)
         bsum.pump(2, yy)
 
     red.arrive()
@@ -1301,7 +1356,6 @@
     red.second()
     settle(1)
     for yy in order:
-        osum.pump(1, yy)
         bsum.pump(1, yy)
         csum.pump(2, yy)
 
@@ -1356,7 +1410,6 @@
         copy.start()
 
     settle(2)
-    settle(3)
     for copy in sv_copies:
         copy.wait_recv()
     me_g = me.c * 2 + y
@@ -1370,7 +1423,7 @@
     ]
     for copy in z_copies:
         copy.start()
-    settle(4)
+    settle(3)
     for copy in z_copies:
         copy.wait_recv()
     total = sv_z[0, z]
@@ -1397,8 +1450,7 @@
         ((rows, width), F32),
         ((2, rows, 3 * h1), BF),
         ((2, rows, 3 * h2), BF),
-        ((2, rows, heads), BF),
-        ((2, rows, pair), BF),
+        ((2, rows, heads + pair), BF),
         ((2, rows, pair), BF),
         ((8, 384), F32),
         ((8, rows, width), BF),
@@ -1406,9 +1458,11 @@
         ((n, 2, 1, rows, 3 * h1), BF),
         ((n, 2, 1, rows, 3 * h2), BF),
         ((n, 2, 1, rows, 3 * h2), BF),
-        ((n, 2, 1, rows, heads), BF),
-        ((n, 2, 1, rows, heads), BF),
-    ] + [((n, 2, 1, rows, pair), BF)] * 4
+        ((n, 2, 1, rows, heads + pair), BF),
+        ((n, 2, 1, rows, heads + pair), BF),
+        ((n, 2, 1, rows, pair), BF),
+        ((n, 2, 1, rows, pair), BF),
+    ]
     scratch = [
         pltpu.VMEM((width, 2 * hid), BF),
         pltpu.VMEM((hid, width), BF),
@@ -1421,7 +1475,7 @@
         pltpu.VMEM((tokens, 2 * hid), BF),
         pltpu.VMEM((2 * n, rows, 3 * h1), BF),
         pltpu.VMEM((2 * n, rows, 3 * h2), BF),
-        pltpu.VMEM((rows, 3 * h2), BF),
+        pltpu.VMEM((2, rows, 3 * max(h1, h2)), BF),
         pltpu.VMEM((rows, width), F32),
         pltpu.VMEM((rows, width), BF),
         pltpu.VMEM((width, 3 * heads), BF),
@@ -1436,13 +1490,13 @@
         pltpu.VMEM((7, n, 8, 384), F32),
         pltpu.VMEM((n, n, 8, 384), F32),
         pltpu.SemaphoreType.REGULAR((3,)),
-        DMA((21,)), DMA((2,)), DMA, DMA((5,)), DMA((5,)), DMA((5,)), DMA((7,)), DMA((7,)), DMA((n - 1,)), DMA((n - 1,)),
-    ] + reduce_scratch(rows, width) + gather_sems() + [DMA((n, 2, 1))] * 20
+        DMA((21,)), DMA((2,)), DMA((2,)), DMA((4,)), DMA((4,)), DMA((4,)), DMA((7,)), DMA((7,)), DMA((n - 1,)), DMA((n - 1,)),
+    ] + reduce_scratch(rows, width) + gather_sems() + [DMA((n, 2, 1))] * 16
     return pl.pallas_call(
         functools.partial(backward_kernel, n, length, heads, hid, h1),
         out_shape=[jax.ShapeDtypeStruct(s, d) for s, d in shapes],
         in_specs=[ANY] * 16 + [VM] * 4,
-        out_specs=[VM, VM] + [ANY] * 5 + [VM] + [ANY] * 11,
+        out_specs=[VM, VM] + [ANY] * 4 + [VM] + [ANY] * 9,
         scratch_shapes=scratch,
         compiler_params=pltpu.CompilerParams(
             collective_id=1, has_side_effects=True, vmem_limit_bytes=64 << 20
@@ -1468,11 +1522,11 @@
         n, h1, w_query, w_key, w_value, w_attn_out, w_gate, w_up, w_down, cot, xin, segment_ids,
         attn_gain[None], ffn_gain[None], rel_table[None],
     )
-    out, gx, fo1, fo2, ao, bo, co, sums = backward(
+    out, gx, fo1, fo2, bo, co, sums = backward(
         n, length, heads, hid, h1, wg1, wd1, wg2, wd2, m1, dgu1, gwf1, a2all, gall, p, a1, qkv, o, wqkv, wo,
         xin, mid, cot, gain1, gain2,
-    )[:8]
-    out, gx, g_q, g_k, g_v, g_o, g_gate, g_up, g_down = finish(h1, out, gx, fo1, fo2, ao, bo, co)
+    )[:7]
+    out, gx, g_q, g_k, g_v, g_o, g_gate, g_up, g_down = finish(h1, heads, out, gx, fo1, fo2, bo, co)
     line = jnp.sum(sums, axis=0)
     half_of = lambda v: jnp.where(y == 0, v[:share], v[128 - share :])
     return (
@@ -1481,26 +1535,27 @@
     )
 
 
-def finish_kernel(h1, out_in, gx_in, *refs):
-    sources, (out, gx, g_q, g_k, g_v, g_o, g_gate, g_up, g_down) = refs[:5], refs[5:14]
-    fo1, fo2, ao, bo, co = held = refs[14:19]
+def finish_kernel(h1, heads, out_in, gx_in, *refs):
+    sources, (out, gx, g_q, g_k, g_v, g_o, g_gate, g_up, g_down) = refs[:4], refs[4:13]
+    held = refs[13:19]
+    fo1, fo2, bo, co = held[:4]
     sem = refs[19]
-    loads = [pltpu.make_async_copy(src, dst, sem.at[i + 2]) for i, (src, dst) in enumerate(zip(sources, held))]
-    moves = [
-        pltpu.make_async_copy(src, dst, sem.at[i]) for i, (src, dst) in enumerate(((out_in, out), (gx_in, gx)))
-    ]
-    for copy in loads + moves:
+    sources = sources + (out_in, gx_in)
+    loads = [pltpu.make_async_copy(src, dst, sem.at[i]) for i, (src, dst) in enumerate(zip(sources, held))]
+    moves = [pltpu.make_async_copy(held[4 + i], dst, sem.at[4 + i]) for i, dst in enumerate((out, gx))]
+    for copy in loads:
         copy.start()
     for copy in loads:
         copy.wait()
-    heads = ao.shape[2]
+    for copy in moves:
+        copy.start()
     h2 = fo2.shape[2] // 3
     hid = h1 + h2
     for yy in range(2):
         for part, ref in enumerate((g_q, g_k, g_v)):
-            ref[:, yy * heads : yy * heads + 128] = bo[yy, :, part * 128 : part * 128 + 128].astype(F32)
+            ref[:, yy * heads : yy * heads + 128] = bo[yy, :, heads + part * 128 : heads + part * 128 + 128].astype(F32)
             ref[:, yy * heads + 128 : yy * heads + 256] = co[yy, :, part * 128 : part * 128 + 128].astype(F32)
-        g_o[yy * heads : (yy + 1) * heads, :] = ao[yy].astype(F32).T
+        g_o[yy * heads : (yy + 1) * heads, :] = bo[yy, :, 0:heads].astype(F32).T
         for part, ref in enumerate((g_gate, g_up)):
             ref[:, yy * hid : yy * hid + h1] = fo1[yy, :, part * h1 : (part + 1) * h1].astype(F32)
             ref[:, yy * hid + h1 : (yy + 1) * hid] = fo2[yy, :, part * h2 : (part + 1) * h2].astype(F32)
@@ -1510,21 +1565,20 @@
         copy.wait()
 
 
-def finish(h1, out, gx, fo1, fo2, ao, bo, co):
+def finish(h1, heads, out, gx, fo1, fo2, bo, co):
     rows = out.shape[0]
-    heads = ao.shape[2]
     hid = h1 + fo2.shape[2] // 3
     shapes = [(rows, 2 * heads)] * 3 + [(2 * heads, rows)] + [(rows, 2 * hid)] * 2 + [(2 * hid, rows)]
     return pl.pallas_call(
-        functools.partial(finish_kernel, h1),
+        functools.partial(finish_kernel, h1, heads),
         out_shape=[jax.ShapeDtypeStruct(out.shape, BF), jax.ShapeDtypeStruct(gx.shape, F32)]
         + [jax.ShapeDtypeStruct(s, F32) for s in shapes],
-        in_specs=[ANY] * 7,
+        in_specs=[ANY] * 6,
         out_specs=[ANY] * 2 + [VM] * 7,
-        scratch_shapes=[pltpu.VMEM(part.shape, BF) for part in (fo1, fo2, ao, bo, co)] + [DMA((7,))],
-        compiler_params=pltpu.CompilerParams(vmem_limit_bytes=32 << 20),
+        scratch_shapes=[pltpu.VMEM(part.shape, part.dtype) for part in (fo1, fo2, bo, co, out, gx)] + [DMA((6,))],
+        compiler_params=pltpu.CompilerParams(vmem_limit_bytes=64 << 20),
         name="finish",
-    )(out, gx, fo1, fo2, ao, bo, co)
+    )(out, gx, fo1, fo2, bo, co)
 
 
 QB = 512

time: 523 us -> 489 us (0.935)
  Pallas kernels: 503 us -> 477 us
  local copies, waits for them, and re-layouts: 8.67 us -> 0.51 us
    pallas_call x1, Pallas kernels: 265 us -> 249 us  [backward(): pl.pallas_call(functools.partial(backward_kernel, n, length, heads, hid,...]
    pallas_call x1, Pallas kernels: 232 us -> 221 us  [forward(): pl.pallas_call(functools.partial(forward_kernel, n, length), out_shape=[j...]
    unnamed x16 -> x0, local copies, waits for them, and re-layouts: 8.15 us -> none
where the time goes in v5:
time: 489 us; the launch traced here: 480 us
  Pallas kernels  477 us (98%)
    pallas_call x1, Pallas kernels, backward(): pl.pallas_call(functools.partial(backward_kernel, n, length, heads, hid,...  249 us
    pallas_call x1, Pallas kernels, forward(): pl.pallas_call(functools.partial(forward_kernel, n, length), out_shape=[j...  221 us

profile of v5, /device:TPU:8, one launch (start us, length us, event | category | flops | bytes accessed | tf_op | source)
XLA Modules:
  0.0 480.0 jit_solution(16875716624870167099)
XLA Ops:
  0.6 221.1 %forward.1 = (bf16[2048,768]{1,0:T(8,128)(2,1)}, bf16[256,2048]{1,0:T(8,128)(2,1)}, bf16[2048,512]{1,0:T(8,128)(2,1)}, bf16[256,2048]{1,0:T(8,128)(2,1)}, bf16[2...) custom-call(bf16[256,512]{1,0:T(8,128)(2,1)} %wq.1, ...), custom_call_target="tpu_custom_call" | custom-call | tf_op jit(solution)/shard_map/forward/pallas_call | solution.py:846
  221.8 248.8 %backward.1 = (bf16[256,2048]{1,0:T(8,128)(2,1)}, f32[256,2048]{1,0:T(8,128)}, bf16[2,256,768]{2,1,0:T(8,128)(2,1)}, bf16[2,256,1152]{2,1,0:T(8,128)(2,1)}, bf16...) custom-call(bf16[2048,512]{1,0:T(8,128)(2,1)} %get-tuple-element.46., ...), custom_call_target="tpu_custom_call" | custom-call | tf_op jit(solution)/shard_map/backward/pallas_call | solution.py:1495
  470.5 7.2 %finish.1 = (bf16[256,2048]{1,0:T(8,128)(2,1)}, f32[256,2048]{1,0:T(8,128)}, f32[256,512]{1,0:T(8,128)}, f32[256,512]{1,0:T(8,128)}, f32[256,512]{1,0:T(8,128)},...) custom-call(bf16[256,2048]{1,0:T(8,128)(2,1)} %get-tuple-element.64.out_in, ...), custom_call_target="tpu_custom_call" | custom-call | tf_op jit(solution)/shard_map/finish/pallas_call | solution.py:1572
  477.7 0.7 reduce_sum.9
  478.4 0.6 broadcast_select_fusion
  479.0 0.5 slice.23

commit v6 on v5

--- a/solution.py
+++ b/solution.py
@@ -69,30 +69,31 @@
 
 
 class ActGather:
-    def __init__(self, me, own, out, send, recv, local):
+    def __init__(self, me, own, out, send, recv, local, cut=None):
         self.me, self.own, self.out = me, own, out
         self.send, self.recv, self.local = send, recv, local
-        self.rows = own.shape[0]
-        self.half = self.rows // 2
+        rows = own.shape[0]
+        cut = cut or rows // 2
+        self.halves = (pl.ds(0, cut), pl.ds(cut, rows - cut))
 
     def part(self, ref, block, h):
-        return ref.at[block, pl.ds(h * self.half, self.half)]
+        return ref.at[block, self.halves[h]]
 
     def copy(self, i):
         me = self.me
         x, k, y = me.x, me.k, me.y
         own = block_of(x, k, y)
         if i == 0:
-            src, dst, dev = self.own.at[pl.ds(0, self.half)], self.part(self.out, own, 0), me.x_peer()
+            src, dst, dev = self.own.at[self.halves[0]], self.part(self.out, own, 0), me.x_peer()
         elif i == 1:
-            src, dst, dev = self.own.at[pl.ds(self.half, self.half)], self.part(self.out, own, 1), me.y_peer()
+            src, dst, dev = self.own.at[self.halves[1]], self.part(self.out, own, 1), me.y_peer()
         elif i == 2:
-            src, dst, dev = self.own.at[pl.ds(0, self.half)], self.part(self.out, own, 0), me.y_peer()
+            src, dst, dev = self.own.at[self.halves[0]], self.part(self.out, own, 0), me.y_peer()
         elif i == 3:
             b = block_of(1 - x, k, y)
             src, dst, dev = self.part(self.out, b, 0), self.part(self.out, b, 0), me.y_peer()
         elif i == 4:
-            src, dst, dev = self.own.at[pl.ds(self.half, self.half)], self.part(self.out, own, 1), me.x_peer()
+            src, dst, dev = self.own.at[self.halves[1]], self.part(self.out, own, 1), me.x_peer()
         elif i == 5:
             b = block_of(x, k, 1 - y)
             src, dst, dev = self.part(self.out, b, 1), self.part(self.out, b, 1), me.x_peer()
@@ -135,14 +136,17 @@
         for i in pieces:
             self.copy(i).wait_recv()
 
+    def placed(self):
+        own = block_of(self.me.x, self.me.k, self.me.y)
+        pltpu.make_async_copy(self.own, self.out.at[own], self.local).wait()
+
     def sent(self):
         for i in range(13):
             self.copy(i).wait_send()
-        own = block_of(self.me.x, self.me.k, self.me.y)
-        pltpu.make_async_copy(self.own, self.out.at[own], self.local).wait()
 
     def finish(self):
         self.land(*range(6, 13))
+        self.placed()
         self.sent()
 
 
@@ -456,8 +460,8 @@
     attn_o = Line(me, n, lambda t, yy: (wof.at[:, piece(t, yy)],), *wo_sems)
     f1 = Line(me, n, lambda t, yy: (wg1.at[piece(t, yy), :], wd1.at[:, piece(t, yy)]), *f1_sems)
     f2 = Line(me, n, lambda t, yy: (wg2.at[piece(t, yy), :], wd2.at[:, piece(t, yy)]), *f2_sems)
-    xact = ActGather(me, xin, xv, *x_sems)
-    gact = ActGather(me, cot, gall, *g_sems)
+    xact = ActGather(me, xin, xv, *x_sems, cut=5 * rows // 16)
+    gact = ActGather(me, cot, gall, *g_sems, cut=rows // 4)
 
     for i in range(4):
         takes[i].start()
@@ -530,20 +534,20 @@
     xact.finish()
 
     def norm_rows(i, carry):
-        r = pl.ds(pl.multiple_of(lax.rem(i, rows // 16) * 16, 16), 16)
-        b = i // (rows // 16)
+        r = pl.ds(pl.multiple_of(lax.rem(i, rows // 32) * 32, 32), 32)
+        b = i // (rows // 32)
         xf = xv[b, r, :].astype(F32)
         inv = lax.rsqrt(jnp.mean(xf * xf, axis=-1, keepdims=True) + EPSILON)
         xv[b, r, :] = (xf * inv * gain1[...]).astype(BF)
         return carry
 
-    lax.fori_loop(0, 4 * rows // 16, norm_rows, 0)
+    lax.fori_loop(0, 4 * rows // 32, norm_rows, 0)
     for i in range(4, 7):
         sends[i].wait_recv()
     f1.own(1 - y)
     attn_o.pump(1, y)
     attn_o.pump(1, 1 - y)
-    lax.fori_loop(4 * rows // 16, 8 * rows // 16, norm_rows, 0)
+    lax.fori_loop(4 * rows // 32, 8 * rows // 32, norm_rows, 0)
     a1_out = pltpu.make_async_copy(xv, a1, c_local.at[0])
     a1_out.start()
     attn_o.pump(2, y)
@@ -714,7 +718,7 @@
             copy.start()
         lax.fori_loop(first, last, lambda j, carry: first_units(j, last - 1, carry), 0)
 
-    pltpu.make_async_copy(a2, a2all.at[block_at(0)], a_sems[2]).wait()
+    aact.placed()
     qkv_out.wait()
     fetch(wg1, wg1_v, 0).wait()
     fetch(wd1, wd1_v, 1).wait()
@@ -771,8 +775,7 @@
     lax.fori_loop(0, 2 * n, first_grads, 0)
     kept.append(fetch(gw_v, gwf1, 2))
     kept[2].start()
-    for i in range(13):
-        aact.copy(i).wait_send()
+    aact.sent()
     f2.land((y, 1 - y))
     for line in (attn, attn_o, f1, f2):
         line.finish()
@@ -1050,6 +1053,7 @@
 
     fetch(a2all.at[block_at(0)], row_a, 2).start()
     fetch(gall.at[block_at(0)], row_g, 3).start()
+    fetch(cot, row_b, 4).start()
     w_loads[0].wait()
 
     def first_slots(i, carry):
@@ -1058,7 +1062,7 @@
         return carry
 
     lax.fori_loop(0, 2 * n, first_slots, 0)
-    for copy in w_loads[1:]:
+    for copy in w_loads[1:3]:
         copy.wait()
 
 
@@ -1090,6 +1094,12 @@
             return carry
 
         lax.fori_loop(0, rows // 16, body, 0)
+
+        @pl.when(i == 0)
+        def _():
+            for copy in w_loads[3:]:
+                copy.wait()
+
         return lax.dot_general(
             dgu[piece(block), :], wgu_v[...], (((1,), (1,)), ((), ())), preferred_element_type=F32
         ).astype(BF)
@@ -1141,12 +1151,13 @@
     red.arrive()
 
     gg2[...] = jnp.zeros_like(gg2)
+    fetch(cot, row_b, 4).wait()
     for h in range(2):
 
         def body(i, carry):
             rr = pl.ds(pl.multiple_of(h * half + i * 16, 16), 16)
             back, gains = norm_back(red.total(h, i), mid[rr, :], gain2[...])
-            gm = cot[rr, :].astype(F32) + back
+            gm = row_b[rr, :].astype(F32) + back
             gmid[rr, :] = gm
             dz[rr, :] = gm.astype(BF)
             gg2[...] += gains[:8] + gains[8:]
@@ -1190,45 +1201,31 @@
         swaps[i][1].start()
 
     fsum.pump(2, order[0])
-    act.forward_core()
-    for j in range(3):
-        red.first_sends(j)
-    settle(0)
-    act.finish()
+    act.onward((4, 0))
+    act.placed()
+    act.land(6, 7, 11)
 
     fetch(wof, row_g, 3).wait()
     slots = ((row_a, 2), (row_b, 4))
-    for b in range(2):
-        fetch(dzall.at[b], *slots[b]).start()
-
-    def project_back(i, carry):
+
+    def come(i):
+        ox, oy = red.place(3 - i // 2)
+        return block_of(ox, jnp.where(i % 2 == 0, me.k, 1 - me.k), oy)
+
+    def project_back(first):
         for b, (buffer, sem) in enumerate(slots):
-            block = i * 2 + b
-            fetch(dzall.at[block], buffer, sem).wait()
-            wgu_v[piece(block), 4 * heads : 5 * heads] = lax.dot_general(
-                buffer[...], row_g[...], (((1,), (1,)), ((), ())), preferred_element_type=F32
-            ).astype(BF)
-
-            @pl.when(i < 3)
-            def _():
-                fetch(dzall.at[block + 2], buffer, sem).start()
-
-        return carry
-
-    lax.fori_loop(0, 4, project_back, 0)
-    fsum.pump(2, order[1])
-    fetch(hidden, row_a, 2).start()
-    w_parts = [
-        fetch(
-            wqkv.at[:, pl.ds(part * heads + hp * 2 * DH, 2 * DH)],
-            wqkv_v.at[:, pl.ds(hp * pair + part * 2 * DH, 2 * DH)],
-            15 + hp * 3 + part,
-        )
-        for hp in range(2)
-        for part in range(3)
-    ]
-    for copy in w_parts:
-        copy.start()
+            fetch(dzall.at[come(first + b)], buffer, sem).start()
+        for i in range(2):
+            for b, (buffer, sem) in enumerate(slots):
+                block = come(first + 2 * i + b)
+                fetch(dzall.at[block], buffer, sem).wait()
+                wgu_v[piece(block), 4 * heads : 5 * heads] = lax.dot_general(
+                    buffer[...], row_g[...], (((1,), (1,)), ((), ())), preferred_element_type=F32
+                ).astype(BF)
+                if i == 0:
+                    fetch(dzall.at[come(first + 2 + b)], buffer, sem).start()
+
+    project_back(0)
     fetch(qkv, wgu_v.at[:, pl.ds(0, 3 * heads)], 0).wait()
     fetch(o, wgu_v.at[:, pl.ds(3 * heads, heads)], 6).wait()
     diag[...] = jnp.zeros_like(diag)
@@ -1237,52 +1234,48 @@
     def p_load(head, t, slot):
         return pltpu.make_async_copy(p.at[head, pl.ds(t * TQ, TQ)], pbuf.at[slot], p_sem.at[slot])
 
-    def head_pair(hp):
-        def sequence(s, carry):
-            head0 = s * local_heads + hp * 2
-            base = pl.multiple_of(s * length, length)
-            p_load(head0, 0, 0).start()
-            p_load(head0, 1, 1).start()
-            for h in range(2):
-                lo = hp * 128 + h * DH
-                to = hp * pair + h * DH
-                seq = pl.ds(base, length)
-                kh = wgu_v[seq, heads + lo : heads + lo + DH]
-                vh = wgu_v[seq, 2 * heads + lo : 2 * heads + lo + DH]
-                acc[...] = jnp.zeros_like(acc)
-                for t in range(tiles):
-                    slot = t % 2
-                    r = pl.ds(pl.multiple_of(base + t * TQ, TQ), TQ)
-                    qh = wgu_v[r, lo : lo + DH]
-                    doh = wgu_v[r, 4 * heads + lo : 4 * heads + lo + DH]
-                    p_load(head0 + h, t, slot).wait()
-                    pb = pbuf[slot]
-                    dp = lax.dot_general(doh, vh, (((1,), (1,)), ((), ())), preferred_element_type=F32)
-                    pf = pb.astype(F32)
-                    ds = (pf * (dp - jnp.sum(pf * dp, axis=-1, keepdims=True))).astype(BF)
-                    dgu[r, to : to + DH] = jnp.dot(ds, kh, preferred_element_type=F32).astype(BF)
-                    ck = lax.dot_general(qh, ds, (((0,), (0,)), ((), ())), preferred_element_type=F32)
-                    cv = lax.dot_general(doh, pb, (((0,), (0,)), ((), ())), preferred_element_type=F32)
-                    u = h * tiles + t + 2
-                    if u < 2 * tiles:
-                        p_load(head0 + u // tiles, u % tiles, slot).start()
-                    if t == 0:
-                        dkt[...] = ck
-                        dvt[...] = cv
-                    else:
-                        dkt[...] += ck
-                        dvt[...] += cv
-                    acc[:, length - t * TQ : 2 * length - t * TQ] += ds.astype(F32)
-                dgu[seq, to + 2 * DH : to + 3 * DH] = dkt[...].T.astype(BF)
-                dgu[seq, to + 4 * DH : to + 5 * DH] = dvt[...].T.astype(BF)
-                c = TQ // 2
-                while c >= 8:
-                    acc[0:c, :] += pltpu.roll(acc[c : 2 * c, :], 2 * length - c, 1)
-                    c //= 2
-                diag[hp * 2 + h] += acc[0:8, :]
-            return carry
-
-        lax.fori_loop(0, 2, sequence, 0)
+    def head_pair(hp, s):
+        head0 = s * local_heads + hp * 2
+        base = pl.multiple_of(s * length, length)
+        p_load(head0, 0, 0).start()
+        p_load(head0, 1, 1).start()
+        for h in range(2):
+            lo = hp * 128 + h * DH
+            to = hp * pair + h * DH
+            seq = pl.ds(base, length)
+            kh = wgu_v[seq, heads + lo : heads + lo + DH]
+            vh = wgu_v[seq, 2 * heads + lo : 2 * heads + lo + DH]
+            acc[...] = jnp.zeros_like(acc)
+            for t in range(tiles):
+                slot = t % 2
+                r = pl.ds(pl.multiple_of(base + t * TQ, TQ), TQ)
+                qh = wgu_v[r, lo : lo + DH]
+                doh = wgu_v[r, 4 * heads + lo : 4 * heads + lo + DH]
+                p_load(head0 + h, t, slot).wait()
+                pb = pbuf[slot]
+                dp = lax.dot_general(doh, vh, (((1,), (1,)), ((), ())), preferred_element_type=F32)
+                pf = pb.astype(F32)
+                ds = (pf * (dp - jnp.sum(pf * dp, axis=-1, keepdims=True))).astype(BF)
+                dgu[r, to : to + DH] = jnp.dot(ds, kh, preferred_element_type=F32).astype(BF)
+                ck = lax.dot_general(qh, ds, (((0,), (0,)), ((), ())), preferred_element_type=F32)
+                cv = lax.dot_general(doh, pb, (((0,), (0,)), ((), ())), preferred_element_type=F32)
+                u = h * tiles + t + 2
+                if u < 2 * tiles:
+                    p_load(head0 + u // tiles, u % tiles, slot).start()
+                if t == 0:
+                    dkt[...] = ck
+                    dvt[...] = cv
+                else:
+                    dkt[...] += ck
+                    dvt[...] += cv
+                acc[:, length - t * TQ : 2 * length - t * TQ] += ds.astype(F32)
+            dgu[seq, to + 2 * DH : to + 3 * DH] = dkt[...].T.astype(BF)
+            dgu[seq, to + 4 * DH : to + 5 * DH] = dvt[...].T.astype(BF)
+            c = TQ // 2
+            while c >= 8:
+                acc[0:c, :] += pltpu.roll(acc[c : 2 * c, :], 2 * length - c, 1)
+                c //= 2
+            diag[hp * 2 + h] += acc[0:8, :]
 
     def pair_grads(hp, line, with_o):
         def loads(i):
@@ -1322,12 +1315,34 @@
 
         lax.fori_loop(0, 2 * n, body, 0)
 
-    head_pair(0)
+    head_pair(0, y)
+    act.onward((2, 0), (3, 0), (5, 0))
+    for j in range(3):
+        red.first_sends(j)
+    fsum.pump(2, order[1])
+    settle(0)
+    head_pair(1, y)
+    act.land(8, 9, 10, 12)
+    project_back(4)
+    act.sent()
+    fetch(hidden, row_a, 2).start()
+    w_parts = [
+        fetch(
+            wqkv.at[:, pl.ds(part * heads + hp * 2 * DH, 2 * DH)],
+            wqkv_v.at[:, pl.ds(hp * pair + part * 2 * DH, 2 * DH)],
+            15 + hp * 3 + part,
+        )
+        for hp in range(2)
+        for part in range(3)
+    ]
+    for copy in w_parts:
+        copy.start()
     fsum.pump(1, order[0])
     red.second()
+    head_pair(0, 1 - y)
     pair_grads(0, bsum, True)
     fsum.pump(1, order[1])
-    head_pair(1)
+    head_pair(1, 1 - y)
     for yy in order:
         bsum.pump(2, yy)
 
@@ -1495,7 +1510,7 @@
     return pl.pallas_call(
         functools.partial(backward_kernel, n, length, heads, hid, h1),
         out_shape=[jax.ShapeDtypeStruct(s, d) for s, d in shapes],
-        in_specs=[ANY] * 16 + [VM] * 4,
+        in_specs=[ANY] * 16 + [VM, ANY, VM, VM],
         out_specs=[VM, VM] + [ANY] * 4 + [VM] + [ANY] * 9,
         scratch_shapes=scratch,
         compiler_params=pltpu.CompilerParams(
@@ -1551,17 +1566,33 @@
         copy.start()
     h2 = fo2.shape[2] // 3
     hid = h1 + h2
-    for yy in range(2):
-        for part, ref in enumerate((g_q, g_k, g_v)):
-            ref[:, yy * heads : yy * heads + 128] = bo[yy, :, heads + part * 128 : heads + part * 128 + 128].astype(F32)
-            ref[:, yy * heads + 128 : yy * heads + 256] = co[yy, :, part * 128 : part * 128 + 128].astype(F32)
-        g_o[yy * heads : (yy + 1) * heads, :] = bo[yy, :, 0:heads].astype(F32).T
-        for part, ref in enumerate((g_gate, g_up)):
+    s_q, s_k, s_v, s_o, s_gate, s_up, s_down = refs[20:27]
+    sem_out = refs[27]
+    leave = [
+        pltpu.make_async_copy(src, dst, sem_out.at[i])
+        for i, (src, dst) in enumerate(
+            zip((s_q, s_k, s_v, s_o, s_gate, s_up, s_down), (g_q, g_k, g_v, g_o, g_gate, g_up, g_down))
+        )
+    ]
+    for part, ref in enumerate((s_gate, s_up)):
+        for yy in range(2):
             ref[:, yy * hid : yy * hid + h1] = fo1[yy, :, part * h1 : (part + 1) * h1].astype(F32)
             ref[:, yy * hid + h1 : (yy + 1) * hid] = fo2[yy, :, part * h2 : (part + 1) * h2].astype(F32)
-        g_down[yy * hid : yy * hid + h1, :] = fo1[yy, :, 2 * h1 : 3 * h1].astype(F32).T
-        g_down[yy * hid + h1 : (yy + 1) * hid, :] = fo2[yy, :, 2 * h2 : 3 * h2].astype(F32).T
-    for copy in moves:
+        leave[4 + part].start()
+    for part, ref in enumerate((s_q, s_k, s_v)):
+        for yy in range(2):
+            at = heads + part * 128
+            ref[:, yy * heads : yy * heads + 128] = bo[yy, :, at : at + 128].astype(F32)
+            ref[:, yy * heads + 128 : yy * heads + 256] = co[yy, :, part * 128 : part * 128 + 128].astype(F32)
+        leave[part].start()
+    for yy in range(2):
+        s_down[yy * hid : yy * hid + h1, :] = fo1[yy, :, 2 * h1 : 3 * h1].astype(F32).T
+        s_down[yy * hid + h1 : (yy + 1) * hid, :] = fo2[yy, :, 2 * h2 : 3 * h2].astype(F32).T
+    leave[6].start()
+    for yy in range(2):
+        s_o[yy * heads : (yy + 1) * heads, :] = bo[yy, :, 0:heads].astype(F32).T
+    leave[3].start()
+    for copy in moves + leave:
         copy.wait()
 
 
@@ -1574,8 +1605,11 @@
         out_shape=[jax.ShapeDtypeStruct(out.shape, BF), jax.ShapeDtypeStruct(gx.shape, F32)]
         + [jax.ShapeDtypeStruct(s, F32) for s in shapes],
         in_specs=[ANY] * 6,
-        out_specs=[ANY] * 2 + [VM] * 7,
-        scratch_shapes=[pltpu.VMEM(part.shape, part.dtype) for part in (fo1, fo2, bo, co, out, gx)] + [DMA((6,))],
+        out_specs=[ANY] * 9,
+        scratch_shapes=[pltpu.VMEM(part.shape, part.dtype) for part in (fo1, fo2, bo, co, out, gx)]
+        + [DMA((6,))]
+        + [pltpu.VMEM(s, F32) for s in shapes]
+        + [DMA((7,))],
         compiler_params=pltpu.CompilerParams(vmem_limit_bytes=64 << 20),
         name="finish",
     )(out, gx, fo1, fo2, bo, co)

time: 489 us -> 480 us (0.982)
  Pallas kernels: 477 us -> 468 us
    pallas_call x1, Pallas kernels: 249 us -> 243 us  [backward(): pl.pallas_call(functools.partial(backward_kernel, n, length, heads, hid,...]
where the time goes in v6:
time: 480 us; the launch traced here: 471 us
  Pallas kernels  468 us (98%)
    pallas_call x1, Pallas kernels, backward(): pl.pallas_call(functools.partial(backward_kernel, n, length, heads, hid,...  243 us
    pallas_call x1, Pallas kernels, forward(): pl.pallas_call(functools.partial(forward_kernel, n, length), out_shape=[j...  218 us

profile of v6, /device:TPU:8, one launch (start us, length us, event | category | flops | bytes accessed | tf_op | source)
XLA Modules:
  0.0 470.6 jit_solution(3750757784446125474)
XLA Ops:
  0.6 218.0 %forward.1 = (bf16[2048,768]{1,0:T(8,128)(2,1)}, bf16[256,2048]{1,0:T(8,128)(2,1)}, bf16[2048,512]{1,0:T(8,128)(2,1)}, bf16[256,2048]{1,0:T(8,128)(2,1)}, bf16[2...) custom-call(bf16[256,512]{1,0:T(8,128)(2,1)} %wq.1, ...), custom_call_target="tpu_custom_call" | custom-call | tf_op jit(solution)/shard_map/forward/pallas_call | solution.py:849
  218.6 243.2 %backward.1 = (bf16[256,2048]{1,0:T(8,128)(2,1)}, f32[256,2048]{1,0:T(8,128)}, bf16[2,256,768]{2,1,0:T(8,128)(2,1)}, bf16[2,256,1152]{2,1,0:T(8,128)(2,1)}, bf16...) custom-call(bf16[2048,512]{1,0:T(8,128)(2,1)} %get-tuple-element.46., ...), custom_call_target="tpu_custom_call" | custom-call | tf_op jit(solution)/shard_map/backward/pallas_call | solution.py:1510
  461.8 6.5 %finish.1 = (bf16[256,2048]{1,0:T(8,128)(2,1)}, f32[256,2048]{1,0:T(8,128)}, f32[256,512]{1,0:T(8,128)}, f32[256,512]{1,0:T(8,128)}, f32[256,512]{1,0:T(8,128)},...) custom-call(bf16[256,2048]{1,0:T(8,128)(2,1)} %get-tuple-element.64.out_in, ...), custom_call_target="tpu_custom_call" | custom-call | tf_op jit(solution)/shard_map/finish/pallas_call | solution.py:1603
  468.3 0.7 reduce_sum.9
  469.0 0.6 broadcast_select_fusion
  469.6 0.5 slice.23

commit v7 on v6

--- a/solution.py
+++ b/solution.py
@@ -1245,7 +1245,8 @@
             seq = pl.ds(base, length)
             kh = wgu_v[seq, heads + lo : heads + lo + DH]
             vh = wgu_v[seq, 2 * heads + lo : 2 * heads + lo + DH]
-            acc[...] = jnp.zeros_like(acc)
+            near = acc.at[:, 0:length]
+            near[...] = jnp.zeros(near.shape, F32)
             for t in range(tiles):
                 slot = t % 2
                 r = pl.ds(pl.multiple_of(base + t * TQ, TQ), TQ)
@@ -1268,14 +1269,21 @@
                 else:
                     dkt[...] += ck
                     dvt[...] += cv
-                acc[:, length - t * TQ : 2 * length - t * TQ] += ds.astype(F32)
+                df = ds.astype(F32)
+                lo_t, hi_t = max(t - 1, 0), min(t + 2, tiles)
+                near[:, (lo_t - t + 2) * TQ : (hi_t - t + 2) * TQ] += df[:, lo_t * TQ : hi_t * TQ]
+                for at, part in ((128, df[:, : lo_t * TQ]), (length + 2 * TQ, df[:, hi_t * TQ :])):
+                    if part.shape[1]:
+                        diag[hp * 2 + h, :, at : at + part.shape[1]] += jnp.sum(
+                            part.reshape(TQ // 8, 8, part.shape[1]), axis=0
+                        )
             dgu[seq, to + 2 * DH : to + 3 * DH] = dkt[...].T.astype(BF)
             dgu[seq, to + 4 * DH : to + 5 * DH] = dvt[...].T.astype(BF)
             c = TQ // 2
             while c >= 8:
-                acc[0:c, :] += pltpu.roll(acc[c : 2 * c, :], 2 * length - c, 1)
+                near[0:c, :] += pltpu.roll(near[c : 2 * c, :], length - c, 1)
                 c //= 2
-            diag[hp * 2 + h] += acc[0:8, :]
+            diag[hp * 2 + h, :, length - 2 * TQ : 2 * length - 2 * TQ] += near[0:8, :]
 
     def pair_grads(hp, line, with_o):
         def loads(i):

time: 480 us -> 478 us (level)
  no operation moved by 1% of the time
where the time goes in v7:
time: 478 us; the launch traced here: 469 us
  Pallas kernels  466 us (97%)
    pallas_call x1, Pallas kernels, backward(): pl.pallas_call(functools.partial(backward_kernel, n, length, heads, hid,...  242 us
    pallas_call x1, Pallas kernels, forward(): pl.pallas_call(functools.partial(forward_kernel, n, length), out_shape=[j...  218 us

profile of v7, /device:TPU:8, one launch (start us, length us, event | category | flops | bytes accessed | tf_op | source)
XLA Modules:
  0.0 469.2 jit_solution(17023124195445176713)
XLA Ops:
  0.6 218.0 %forward.1 = (bf16[2048,768]{1,0:T(8,128)(2,1)}, bf16[256,2048]{1,0:T(8,128)(2,1)}, bf16[2048,512]{1,0:T(8,128)(2,1)}, bf16[256,2048]{1,0:T(8,128)(2,1)}, bf16[2...) custom-call(bf16[256,512]{1,0:T(8,128)(2,1)} %wq.1, ...), custom_call_target="tpu_custom_call" | custom-call | tf_op jit(solution)/shard_map/forward/pallas_call | solution.py:849
  218.6 241.8 %backward.1 = (bf16[256,2048]{1,0:T(8,128)(2,1)}, f32[256,2048]{1,0:T(8,128)}, bf16[2,256,768]{2,1,0:T(8,128)(2,1)}, bf16[2,256,1152]{2,1,0:T(8,128)(2,1)}, bf16...) custom-call(bf16[2048,512]{1,0:T(8,128)(2,1)} %get-tuple-element.46., ...), custom_call_target="tpu_custom_call" | custom-call | tf_op jit(solution)/shard_map/backward/pallas_call | solution.py:1518
  460.4 6.5 %finish.1 = (bf16[256,2048]{1,0:T(8,128)(2,1)}, f32[256,2048]{1,0:T(8,128)}, f32[256,512]{1,0:T(8,128)}, f32[256,512]{1,0:T(8,128)}, f32[256,512]{1,0:T(8,128)},...) custom-call(bf16[256,2048]{1,0:T(8,128)(2,1)} %get-tuple-element.64.out_in, ...), custom_call_target="tpu_custom_call" | custom-call | tf_op jit(solution)/shard_map/finish/pallas_call | solution.py:1611
  466.9 0.7 reduce_sum.9
  467.6 0.6 broadcast_select_fusion
  468.2 0.5 slice.23
